TPU v7x, 32 devices: a whole 2x2x4 slice. The times are simulated.
32 devices in a mesh: rows: 8 (over z, y), pairs: 4 (over x, core).
Axes of the slice: x: 2, y: 2, z: 4, core: 2. Of those that a mesh axis runs over, the one named last changes fastest.
Arguments:
- latent: float32 [16384, 128], P('rows'), may hold values from -2.5 to 2.5
- left_block: int32 [8, 4, 8, 2], P('rows', 'pairs'), may hold values from 0 to 15, as said below
- right_block: int32 [8, 4, 8, 2], P('rows', 'pairs'), may hold values from 0 to 15
- slot_kind: int32 [8, 4, 8, 2], P('rows', 'pairs'), may hold values from 0 to 2, as said below
- edge_cols: int32 [8, 4, 8, 2, 8, 128], P('rows', 'pairs'), may hold values from 0 to 127
Outputs:
- latent_grad: float32 [16384, 128], P(('rows', 'pairs'))
Inputs may be any that keep to these rules, and one draw needn't show every extreme that they name: `slot_kind`: exactly the slots whose third index s is lower than the first index r hold 0; every other slot holds 1 or 2. On slots whose third index equals the first, left_block <= right_block, so that every listed pair has its left block at or before its right block.
All inputs are finite; a program needn't handle non-finite values.
Results may differ from a plain program's by a relative error of at most 0.0003.
Values sent between devices are 32-bit elements; how exact they have to be, the bound alone decides.
No kernel may reach another device: no remote copies, remote signals or barrier semaphores. Data moves between devices by JAX's collectives and lax.ppermute only.
A program may use at most 128 MiB of HBM per device.

v0:
```python
import jax
import jax.numpy as jnp
from jax import lax
from jax.sharding import PartitionSpec as P

HIGHEST_PRECISION = lax.Precision.HIGHEST


def residual(left_rows, right_rows, slot_kinds, edge_ids):
    scores = jnp.einsum("...id,...jd->...ij", left_rows, right_rows, precision=HIGHEST_PRECISION)
    columns = lax.broadcasted_iota(jnp.int32, scores.shape, scores.ndim - 1)
    target_hit = jnp.zeros(scores.shape, jnp.bool_)
    for which in range(edge_ids.shape[-2]):
        target_hit = target_hit | (edge_ids[..., which, :, None] == columns)
    positive = (slot_kinds == 2)[..., None, None]
    target = jnp.where(target_hit & positive, jnp.ones_like(scores), jnp.zeros_like(scores))
    live = (slot_kinds > 0)[..., None, None]
    return jnp.where(live, jax.nn.sigmoid(scores) - target, jnp.zeros_like(scores))


def add_blocks(tiles, block_ids, block_count):
    flat_ids = block_ids.reshape(-1)
    rows_of = lax.broadcasted_iota(jnp.int32, (block_count, flat_ids.shape[0]), 0)
    onehot = (rows_of == flat_ids[None, :]).astype(jnp.float32)
    flat_tiles = tiles.reshape(flat_ids.shape[0], -1)
    return jnp.dot(
        onehot, flat_tiles, precision=HIGHEST_PRECISION, preferred_element_type=jnp.float32
    )


def left_product(residue, right_rows):
    return jnp.einsum("psij,psjd->psid", residue, right_rows, precision=HIGHEST_PRECISION)


def right_product(residue, left_rows):
    return jnp.einsum("psij,psid->psjd", residue, left_rows, precision=HIGHEST_PRECISION)


def body(latent, left_block, right_block, slot_kind, edge_cols):
    tile_size = edge_cols.shape[-1]
    latent_width = latent.shape[1]
    block_count = latent.shape[0] // tile_size
    blocks = latent.reshape(block_count, tile_size, latent_width)
    peer_count = left_block.shape[2]
    slot_count = left_block.shape[3]
    list_count = edge_cols.shape[4]
    left_ids = left_block.reshape(peer_count, slot_count)
    right_ids = right_block.reshape(peer_count, slot_count)
    slot_kinds = slot_kind.reshape(peer_count, slot_count)
    edge_ids = edge_cols.reshape(peer_count, slot_count, list_count, tile_size)
    outgoing = blocks[left_ids]
    left_rows = lax.all_to_all(outgoing, "rows", split_axis=0, concat_axis=0, tiled=True)
    right_float = lax.all_to_all(
        right_ids.astype(jnp.float32), "rows", split_axis=0, concat_axis=0, tiled=True
    )
    kind_float = lax.all_to_all(
        slot_kinds.astype(jnp.float32), "rows", split_axis=0, concat_axis=0, tiled=True
    )
    edge_float = lax.all_to_all(
        edge_ids.astype(jnp.float32), "rows", split_axis=0, concat_axis=0, tiled=True
    )
    local_right = blocks[right_float.astype(jnp.int32)]
    residue = residual(
        left_rows, local_right, kind_float.astype(jnp.int32), edge_float.astype(jnp.int32)
    )
    left_grad = left_product(residue, local_right)
    right_grad = right_product(residue, left_rows)
    sent_back = lax.all_to_all(left_grad, "rows", split_axis=0, concat_axis=0, tiled=True)
    sent_back, right_grad, right_float = (sent_back, right_grad, right_float)
    gradient = add_blocks(sent_back, left_ids, block_count) + add_blocks(
        right_grad, right_float.astype(jnp.int32), block_count
    )
    summed = lax.psum_scatter(
        gradient.reshape(block_count * tile_size, latent_width),
        "pairs",
        scatter_dimension=0,
        tiled=True,
    )
    return summed


def solution(mesh):
    return jax.shard_map(
        body,
        mesh=mesh,
        in_specs=(
            P("rows", None),
            P("rows", "pairs", None, None),
            P("rows", "pairs", None, None),
            P("rows", "pairs", None, None),
            P("rows", "pairs", None, None, None, None),
        ),
        out_specs=P(("rows", "pairs"), None),
        check_vma=False,
    )
```

profile of v0, /device:TPU:0, one launch (start us, length us, event | category | flops | bytes accessed | tf_op | source)
XLA Modules:
  0.0 139.8 jit_solution(8283643832050964205)
XLA Ops:
  6.5 0.0 copy-start
  6.5 0.8 convert_bitcast_fusion.1
  7.3 0.7 copy.36
  8.0 0.0 copy-start.4
  8.0 7.4 %all-to-all-start.2 = ((f32[8,1,2]{2,1,0:T(1,128)}), f32[8,1,2]{2,1,0:T(1,128)S(1)}, u32[]{:S(2)}, u32[]{:S(2)}) async-start(f32[8,1,2]{2,1,0:T(1,128)} %copy.36), calls=%async_computation.2 | async-start | bytes 8192 | tf_op jit(solution)/shard_map/all_to_all | solution.py:53
  15.4 0.0 copy-done.4
  15.4 0.7 copy.32
  16.1 5.7 %all-to-all-done.2 = f32[8,1,2]{2,1,0:T(1,128)S(1)} async-done(((f32[8,1,2]{2,1,0:T(1,128)}), f32[8,1,2]{2,1,0:T(1,128)S(1)}, u32[]{:S(2)}, u32[]{:S(2)}) %all-to-all-start.2) | async-done | bytes 96 | tf_op jit(solution)/shard_map/all_to_all | solution.py:53
  21.8 3.3 %all-to-all-start = ((f32[8,1,2]{2,1,0:T(1,128)}), f32[8,1,2]{2,1,0:T(1,128)S(1)}, u32[]{:S(2)}, u32[]{:S(2)}) async-start(f32[8,1,2]{2,1,0:T(1,128)} %copy.32), calls=%async_computation | async-start | bytes 8192 | tf_op jit(solution)/shard_map/all_to_all | solution.py:56
  25.1 1.5 %convert_bitcast_fusion = f32[8,2,8,128]{3,2,1,0:T(8,128)} fusion(s32[1,1,8,2,8,128]{5,4,3,2,1,0:T(8,128)} %param.9), kind=kLoop, calls=%fused_computation.30 | loop fusion | flops 16384 | bytes 131072 | tf_op jit(solution)/shard_map/convert_element_type | solution.py:60
  26.6 0.0 copy-start.3
  26.6 4.9 %all-to-all-done = f32[8,1,2]{2,1,0:T(1,128)S(1)} async-done(((f32[8,1,2]{2,1,0:T(1,128)}), f32[8,1,2]{2,1,0:T(1,128)S(1)}, u32[]{:S(2)}, u32[]{:S(2)}) %all-to-all-start) | async-done | bytes 96 | tf_op jit(solution)/shard_map/all_to_all | solution.py:56
  31.5 3.4 %all-to-all-start.3 = ((f32[8,2,8,128]{3,2,1,0:T(8,128)}), f32[8,2,8,128]{3,2,1,0:T(8,128)S(1)}, u32[]{:S(2)}, u32[]{:S(2)}) async-start(f32[8,2,8,128]{3,2,1,0:T(8,128)} %convert_bitcast_fusion), calls=%async_computation.3 | async-start | bytes 131072 | tf_op jit(solution)/shard_map/all_to_all | solution.py:59
  34.8 0.0 copy-done.3
  34.9 0.1 copy.35
  35.0 0.1 reshape.130
  35.0 0.0 copy-done
  35.1 1.6 %gather_fusion = f32[16,128,128]{2,1,0:T(8,128)} fusion(f32[16,128,128]{2,1,0:T(8,128)S(1)} %bitcast.47, s32[1024]{0:T(1024)S(1)} %pad_clamp_fusion.1), kind=kCustom, calls=%fused_computation | custom fusion | bytes 2097216 | tf_op jit(solution)/shard_map/gather | solution.py:51
  36.6 5.0 %all-to-all-done.3 = f32[8,2,8,128]{3,2,1,0:T(8,128)S(1)} async-done(((f32[8,2,8,128]{3,2,1,0:T(8,128)}), f32[8,2,8,128]{3,2,1,0:T(8,128)S(1)}, u32[]{:S(2)}, u32[]{:S(2)}) %all-to-all-start.3) | async-done | bytes 65568 | tf_op jit(solution)/shard_map/all_to_all | solution.py:59
  41.7 3.6 %all-to-all-start.1 = ((f32[8,2,128,128]{3,2,1,0:T(8,128)}), f32[8,2,128,128]{3,2,1,0:T(8,128)S(1)}, u32[]{:S(2)}, u32[]{:S(2)}) async-start(f32[8,2,128,128]{3,2,1,0:T(8,128)} %bitcast.4), calls=%async_computation.1 | async-start | bytes 2097152 | tf_op jit(solution)/shard_map/all_to_all | solution.py:52
  45.3 0.1 copy.37
  45.4 0.1 copy.38
  45.4 0.1 reshape.138
  45.5 0.1 copy.33
  45.6 0.1 copy.34
  45.7 0.1 copy.39
  45.8 1.6 %gather_fusion.1 = f32[16,128,128]{2,1,0:T(8,128)} fusion(f32[16,128,128]{2,1,0:T(8,128)S(1)} %bitcast.48, s32[1024]{0:T(1024)S(1)} %pad_clamp_fusion), kind=kCustom, calls=%fused_computation.1 | custom fusion | bytes 2097216 | tf_op jit(solution)/shard_map/gather | solution.py:62
  47.5 20.2 %all-to-all-done.1 = f32[8,2,128,128]{3,2,1,0:T(8,128)S(1)} async-done(((f32[8,2,128,128]{3,2,1,0:T(8,128)}), f32[8,2,128,128]{3,2,1,0:T(8,128)S(1)}, u32[]{:S(2)}, u32[]{:S(2)}) %all-to-all-start.1) | async-done | bytes 1048608 | tf_op jit(solution)/shard_map/all_to_all | solution.py:52
  67.7 0.0 copy-start.1
  67.7 6.1 %fusion.4 = f32[8,2,128,128]{3,2,1,0:T(8,128)S(1)} fusion(f32[8,2,128,128]{3,2,1,0:T(8,128)S(1)} %all-to-all-done.1, f32[8,2,128,128]{3,2,1,0:T(8,128)} %bitcast.49, s32[8,2,128]{2,1,0:T(2,128)S(1)} %bitcast.53, s32[8,2,128]{2,1,0:T(2,128)S(1)} %bitcast.54, s32[8,2,128]{2,1,0:T(2,128)S(1)} %bitcast.55, s32[8,2,128]{2,1,0:T(2,128)S(1)} %bitcast.56, ...), kind=kOutput, calls=%fused_computation.8 | convolution fusion | flops 408420352 | bytes 3211296 | tf_op jit(solution)/shard_map/...id,...jd->...ij/dot_general | solution.py:10
  73.8 0.0 copy-done.1
  73.8 2.2 %fusion.21 = f32[8,2,128,128]{3,2,1,0:T(8,128)} fusion(f32[8,2,128,128]{3,2,1,0:T(8,128)S(1)} %fusion.4, f32[8,2,128,128]{3,2,1,0:T(8,128)S(1)} %bitcast.50), kind=kOutput, calls=%fused_computation.45 | convolution fusion | flops 402653184 | bytes 3145728 | tf_op jit(solution)/shard_map/psij,psjd->psid/dot_general | solution.py:32
  76.0 4.2 %all-to-all-start.4 = ((f32[8,2,128,128]{3,2,1,0:T(8,128)}), f32[8,2,128,128]{3,2,1,0:T(8,128)}, u32[]{:S(2)}, u32[]{:S(2)}) async-start(f32[8,2,128,128]{3,2,1,0:T(8,128)} %fusion.21), calls=%async_computation.4 | async-start | bytes 2097152 | tf_op jit(solution)/shard_map/all_to_all | solution.py:68
  80.2 0.0 reduce-scatter.2.cloned.1.call-start
  80.3 0.1 copy.31
  80.3 0.1 eq.108
  80.4 0.1 convert_element_type.79
  80.5 2.8 %fusion.22 = f32[8,2,128,128]{3,2,1,0:T(8,128)} fusion(f32[8,2,128,128]{3,2,1,0:T(8,128)S(1)} %fusion.4, f32[8,2,128,128]{3,2,1,0:T(8,128)S(1)} %all-to-all-done.1), kind=kOutput, calls=%fused_computation.46 | convolution fusion | flops 402653184 | bytes 3145728 | tf_op jit(solution)/shard_map/psij,psid->psjd/dot_general | solution.py:36
  83.3 20.8 %all-to-all-done.4 = f32[8,2,128,128]{3,2,1,0:T(8,128)} async-done(((f32[8,2,128,128]{3,2,1,0:T(8,128)}), f32[8,2,128,128]{3,2,1,0:T(8,128)}, u32[]{:S(2)}, u32[]{:S(2)}) %all-to-all-start.4) | async-done | bytes 1048608 | tf_op jit(solution)/shard_map/all_to_all | solution.py:68
  104.2 0.0 copy-start.2
  104.2 2.5 %fusion.7 = f32[16,16384]{1,0:T(8,128)S(1)} fusion(f32[2,8,128,128]{3,2,1,0:T(8,128)} %bitcast.22, s32[16]{0:T(128)S(1)} %eq.108), kind=kOutput, calls=%fused_computation.11 | convolution fusion | flops 50331904 | bytes 2097216 | tf_op jit(solution)/shard_map/dot_general | solution.py:26
  106.7 0.0 copy-done.2
  106.7 1.2 convolution_add_fusion
  107.9 1.1 reshape.127
  109.0 0.0 reduce-scatter.2.cloned.1.call-update
  109.1 23.9 %reduce-scatter.2.cloned.1.call-done = f32[512,128]{1,0:T(8,128)} async-done(((f32[2048,128]{1,0:T(8,128)}), f32[512,128]{1,0:T(8,128)}) %reduce-scatter.2.cloned.1.call-update) | async-done | bytes 262160 | tf_op jit(solution)/shard_map/reduce_scatter | solution.py:73
  (10 shorter events, 0.1 us)
Async XLA Ops:
  6.5 28.5 %copy-start = (f32[2048,128]{1,0:T(8,128)S(1)}, f32[2048,128]{1,0:T(8,128)}, u32[]{:S(2)}) copy-start(f32[2048,128]{1,0:T(8,128)} %param.5) | copy-start | bytes 3145732
  8.0 7.4 %copy-start.4 = (s32[1,1,8,2]{2,3,1,0:T(2,128)S(1)}, s32[1,1,8,2]{2,3,1,0:T(2,128)}, u32[]{:S(2)}) copy-start(s32[1,1,8,2]{2,3,1,0:T(2,128)} %param.8) | copy-start | bytes 196
  8.0 13.8 %all-to-all-start.2 = ((f32[8,1,2]{2,1,0:T(1,128)}), f32[8,1,2]{2,1,0:T(1,128)S(1)}, u32[]{:S(2)}, u32[]{:S(2)}) async-start(f32[8,1,2]{2,1,0:T(1,128)} %copy.36), calls=%async_computation.2 | async-start | bytes 8192 | tf_op jit(solution)/shard_map/all_to_all | solution.py:53
  21.8 9.7 %all-to-all-start = ((f32[8,1,2]{2,1,0:T(1,128)}), f32[8,1,2]{2,1,0:T(1,128)S(1)}, u32[]{:S(2)}, u32[]{:S(2)}) async-start(f32[8,1,2]{2,1,0:T(1,128)} %copy.32), calls=%async_computation | async-start | bytes 8192 | tf_op jit(solution)/shard_map/all_to_all | solution.py:56
  26.6 8.3 %copy-start.3 = (s32[1,1,8,2]{2,3,1,0:T(2,128)S(1)}, s32[1,1,8,2]{2,3,1,0:T(2,128)}, u32[]{:S(2)}) copy-start(s32[1,1,8,2]{2,3,1,0:T(2,128)} %param.6) | copy-start | bytes 196
  31.5 10.2 %all-to-all-start.3 = ((f32[8,2,8,128]{3,2,1,0:T(8,128)}), f32[8,2,8,128]{3,2,1,0:T(8,128)S(1)}, u32[]{:S(2)}, u32[]{:S(2)}) async-start(f32[8,2,8,128]{3,2,1,0:T(8,128)} %convert_bitcast_fusion), calls=%async_computation.3 | async-start | bytes 131072 | tf_op jit(solution)/shard_map/all_to_all | solution.py:59
  41.7 26.0 %all-to-all-start.1 = ((f32[8,2,128,128]{3,2,1,0:T(8,128)}), f32[8,2,128,128]{3,2,1,0:T(8,128)S(1)}, u32[]{:S(2)}, u32[]{:S(2)}) async-start(f32[8,2,128,128]{3,2,1,0:T(8,128)} %bitcast.4), calls=%async_computation.1 | async-start | bytes 2097152 | tf_op jit(solution)/shard_map/all_to_all | solution.py:52
  67.7 6.1 %copy-start.1 = (f32[16,128,128]{2,1,0:T(8,128)S(1)}, f32[16,128,128]{2,1,0:T(8,128)}, u32[]{:S(2)}) copy-start(f32[16,128,128]{2,1,0:T(8,128)} %gather_fusion.1) | copy-start | bytes 3145732
  76.0 28.2 %all-to-all-start.4 = ((f32[8,2,128,128]{3,2,1,0:T(8,128)}), f32[8,2,128,128]{3,2,1,0:T(8,128)}, u32[]{:S(2)}, u32[]{:S(2)}) async-start(f32[8,2,128,128]{3,2,1,0:T(8,128)} %fusion.21), calls=%async_computation.4 | async-start | bytes 2097152 | tf_op jit(solution)/shard_map/all_to_all | solution.py:68
  80.2 52.7 %reduce-scatter.2.cloned.1.call-start = ((), (), s32[]{:S(2)}) async-start(), calls=%async_computation.6 | async-start | bytes 1310720 | tf_op jit(solution)/shard_map/reduce_scatter | solution.py:73
  104.2 2.5 %copy-start.2 = (f32[8,2,128,128]{3,2,1,0:T(8,128)S(1)}, f32[8,2,128,128]{3,2,1,0:T(8,128)}, u32[]{:S(2)}) copy-start(f32[8,2,128,128]{3,2,1,0:T(8,128)} %fusion.22) | copy-start | bytes 3145732
Sparse Core Ops, SparseCore 0:
  109.2 23.7 reduce-scatter.1
where the time goes:
time: 140 us
  waiting for transfers between devices  80.6 us (58%)
  starting transfers between devices  21.9 us (16%)
  matrix products  14.8 us (11%)
  between operations  13.5 us (10%)
  local copies, waits for them, and re-layouts  6.69 us (5%)
  other arithmetic  2.32 us (2%)
    reduce_scatter x1, waiting for transfers between devices, body(): lax.psum_scatter(gradient.reshape(block_count * tile_size, latent_width),...  23.9 us
    all_to_all x1, waiting for transfers between devices, body(): lax.all_to_all(left_grad, 'rows', split_axis=0, concat_axis=0, tiled=True)  20.8 us
    all_to_all x1, waiting for transfers between devices, body(): lax.all_to_all(outgoing, 'rows', split_axis=0, concat_axis=0, tiled=True)  20.2 us
    all_to_all x1, starting transfers between devices, body(): lax.all_to_all(right_ids.astype(jnp.float32), 'rows', split_axis=0, conca...  7.41 us
    dot_general x1, matrix products, residual(): jnp.einsum('...id,...jd->...ij', left_rows, right_rows, precision=HIGHEST...  6.11 us
    all_to_all x1, waiting for transfers between devices, body(): lax.all_to_all(right_ids.astype(jnp.float32), 'rows', split_axis=0, conca...  5.7 us
    all_to_all x1, waiting for transfers between devices, body(): lax.all_to_all(edge_ids.astype(jnp.float32), 'rows', split_axis=0, concat...  5.04 us
    all_to_all x1, waiting for transfers between devices, body(): lax.all_to_all(slot_kinds.astype(jnp.float32), 'rows', split_axis=0, conc...  4.92 us
  transfers between devices with their start and end apart: 6, of which 6 were waited for; matrix products, arithmetic and copies ran while one was open for 7% of the time, Pallas kernels for 0%

commit v1 on v0

v1 whole, which is shorter than its diff:
```python
import functools

import jax
import jax.numpy as jnp
from jax import lax
from jax.experimental import pallas as pl
from jax.experimental.pallas import tpu as pltpu
from jax.sharding import PartitionSpec as P

F32 = jnp.float32
BF16 = jnp.bfloat16
SMEM = pl.BlockSpec(memory_space=pltpu.SMEM)
VMEM = pl.BlockSpec(memory_space=pltpu.VMEM)
PARAMS = pltpu.CompilerParams(vmem_limit_bytes=48 * 1024 * 1024)


def halves(value):
    high = value.astype(BF16)
    return high, (value - high.astype(F32)).astype(BF16)


def product(left, right, dims):
    (a, b), (c, d) = left, right
    one = functools.partial(
        lax.dot_general, dimension_numbers=((dims[:1], dims[1:]), ((), ())), preferred_element_type=F32
    )
    return one(a, c) + (one(a, d) + one(b, c))


def natural_target(edges):
    width = edges.shape[-1]
    row = lax.broadcasted_iota(jnp.int32, (width, width), 0).astype(F32)
    hit = row == edges[0:1, :]
    for which in range(1, edges.shape[0]):
        hit = hit | (row == edges[which : which + 1, :])
    return jnp.where(hit, 1.0, 0.0)


def coded_edges(edges_ref, kind_ref, peer, slot):
    edges = edges_ref[peer, slot].astype(F32)
    return jnp.where(kind_ref[peer, slot] == 2, edges, -1.0)


def own_id(left_ref, asked_ref, me, peer, slot):
    return jnp.where(peer >= me, left_ref[peer, slot], asked_ref[peer, slot])


def pack_kernel(shifts, left_ref, asked_ref, kind_ref, latent_ref, edges_ref, *message_refs):
    me = lax.axis_index("rows")
    tile = latent_ref.shape[1]
    for shift, message_ref in zip(shifts, message_refs):
        peer = me ^ shift
        for slot in range(message_ref.shape[0]):
            block = own_id(left_ref, asked_ref, me, peer, slot)
            message_ref[slot, :tile] = latent_ref[block]
            message_ref[slot, tile:] = coded_edges(edges_ref, kind_ref, peer, slot)


def add_peer(shift, total_ref, left_ref, asked_ref, kind_ref, latent_ref, edges_ref, message_ref):
    me = lax.axis_index("rows")
    peer = me ^ shift
    low = peer > me
    quarter = lax.axis_index("pairs") * (total_ref.shape[0] // lax.axis_size("pairs"))
    tile = latent_ref.shape[1]
    for slot in range(message_ref.shape[0]):
        block = own_id(left_ref, asked_ref, me, peer, slot)
        own = halves(latent_ref[block])
        other = halves(message_ref[slot, :tile])
        sent = message_ref[slot, tile:]
        edges = jnp.where(low, coded_edges(edges_ref, kind_ref, peer, slot), sent)
        target = natural_target(edges)
        target = jnp.where(low, target.T, target)
        residue = jax.nn.sigmoid(product(own, other, (1, 1))) - target
        total_ref[block ^ quarter] += product(halves(residue), other, (1, 0))


def add_own(total_ref, left_ref, right_ref, kind_ref, latent_ref, edges_ref):
    me = lax.axis_index("rows")
    quarter = lax.axis_index("pairs") * (total_ref.shape[0] // lax.axis_size("pairs"))
    for slot in range(edges_ref.shape[1]):
        left_block, right_block = left_ref[me, slot], right_ref[me, slot]
        left, right = halves(latent_ref[left_block]), halves(latent_ref[right_block])
        target = natural_target(coded_edges(edges_ref, kind_ref, me, slot))
        residue = halves(jax.nn.sigmoid(product(right, left, (1, 1))) - target)
        total_ref[left_block ^ quarter] += product(residue, right, (0, 0))
        total_ref[right_block ^ quarter] += product(residue, left, (1, 0))


def first_kernel(shifts, left_ref, right_ref, asked_ref, kind_ref, latent_ref, edges_ref, *refs):
    *message_refs, total_ref = refs
    total_ref[...] = jnp.zeros_like(total_ref)
    add_own(total_ref, left_ref, right_ref, kind_ref, latent_ref, edges_ref)
    for shift, message_ref in zip(shifts, message_refs):
        add_peer(shift, total_ref, left_ref, asked_ref, kind_ref, latent_ref, edges_ref, message_ref)


def last_kernel(shifts, left_ref, asked_ref, kind_ref, latent_ref, edges_ref, before_ref, *refs):
    count = len(shifts)
    message_refs, part_refs, total_ref = refs[:count], refs[count:-1], refs[-1]
    total_ref[...] = before_ref[...]
    for shift, message_ref in zip(shifts, message_refs):
        add_peer(shift, total_ref, left_ref, asked_ref, kind_ref, latent_ref, edges_ref, message_ref)
    depth = part_refs[0].shape[0]
    for place, part_ref in enumerate(part_refs):
        part_ref[...] = total_ref[place * depth : (place + 1) * depth]


def estimate(slots, width, moved):
    return pl.CostEstimate(flops=12 * slots * width**3, bytes_accessed=moved, transcendentals=slots * width**2)


def swap(value, axis, shift):
    return lax.ppermute(value, axis, [(at, at ^ shift) for at in range(lax.axis_size(axis))])


def body(latent, left_block, right_block, slot_kind, edge_cols):
    tile, width = edge_cols.shape[-1], latent.shape[1]
    blocks = latent.reshape(-1, tile, width)
    peers, slots = left_block.shape[2:]
    lists = edge_cols.shape[4]
    left_ids = left_block.reshape(peers, slots)
    right_ids = right_block.reshape(peers, slots)
    kinds = slot_kind.reshape(peers, slots)
    edges = edge_cols.reshape(peers, slots, lists, tile)
    asked = lax.all_to_all(right_ids.reshape(peers, 1, slots), "rows", 0, 0, tiled=True).reshape(peers, slots)

    top = peers // 2
    far, near = tuple(range(top, peers)), tuple(range(1, top))
    order = far + near
    message = jax.ShapeDtypeStruct((slots, tile + lists, width), F32)
    total = jax.ShapeDtypeStruct(blocks.shape, F32)
    messages = pl.pallas_call(
        functools.partial(pack_kernel, order),
        out_shape=[message] * len(order),
        in_specs=[SMEM] * 3 + [VMEM] * 2,
        out_specs=[VMEM] * len(order),
        compiler_params=PARAMS,
    )(left_ids, asked, kinds, blocks, edges)
    arrived = {shift: swap(value, "rows", shift) for shift, value in zip(order, messages)}

    before = pl.pallas_call(
        functools.partial(first_kernel, near),
        out_shape=total,
        in_specs=[SMEM] * 4 + [VMEM] * (2 + len(near)),
        out_specs=VMEM,
        compiler_params=PARAMS,
        cost_estimate=estimate(slots * (1 + len(near)), tile, 2 * blocks.size * 4),
    )(left_ids, right_ids, asked, kinds, blocks, edges, *[arrived[shift] for shift in near])
    parts = lax.axis_size("pairs")
    part = jax.ShapeDtypeStruct((blocks.shape[0] // parts, tile, width), F32)
    held = pl.pallas_call(
        functools.partial(last_kernel, far),
        out_shape=[part] * parts,
        in_specs=[SMEM] * 3 + [VMEM] * (3 + len(far)),
        out_specs=[VMEM] * parts,
        scratch_shapes=[pltpu.VMEM(blocks.shape, F32)],
        compiler_params=PARAMS,
        cost_estimate=estimate(slots * len(far), tile, 3 * blocks.size * 4),
    )(left_ids, asked, kinds, blocks, edges, before, *[arrived[shift] for shift in far])
    far_half = held[2] + swap(held[3], "pairs", 1)
    kept = swap(held[1], "pairs", 1)
    result = held[0] + kept + swap(far_half, "pairs", 2)
    return result.reshape(-1, width)


def solution(mesh):
    return jax.shard_map(
        body,
        mesh=mesh,
        in_specs=(
            P("rows", None),
            P("rows", "pairs", None, None),
            P("rows", "pairs", None, None),
            P("rows", "pairs", None, None),
            P("rows", "pairs", None, None, None, None),
        ),
        out_specs=P(("rows", "pairs"), None),
        check_vma=False,
    )
```

time: 140 us -> 58.1 us (0.42)
  the two profiles are of different devices: /device:TPU:0 before, /device:TPU:8 now
where the time goes in v1:
time: 58.1 us; the launch traced here: 57.9 us
  waiting for transfers between devices  27.5 us (47%)
  starting transfers between devices  17.7 us (30%)
  Pallas kernels  6.85 us (12%)
  local copies, waits for them, and re-layouts  5.02 us (9%)
  other arithmetic  0.77 us (1%)
    ppermute x10, waiting for transfers between devices, swap(): lax.ppermute(value, axis, [(at, at ^ shift) for at in range(lax.axis_size...  24.1 us
    ppermute x10, starting transfers between devices, swap(): lax.ppermute(value, axis, [(at, at ^ shift) for at in range(lax.axis_size...  11.4 us
    all_to_all x1, starting transfers between devices, body(): lax.all_to_all(right_ids.reshape(peers, 1, slots), 'rows', 0, 0, tiled=True)  6.28 us
    unnamed x14, local copies, waits for them, and re-layouts  4.11 us
    all_to_all x1, waiting for transfers between devices, body(): lax.all_to_all(right_ids.reshape(peers, 1, slots), 'rows', 0, 0, tiled=True)  3.39 us
    pallas_call x1, Pallas kernels, body(): pl.pallas_call(functools.partial(last_kernel, far), out_shape=[part] * pa...  3.13 us
    pallas_call x1, Pallas kernels, body(): pl.pallas_call(functools.partial(first_kernel, near), out_shape=total, in...  2.91 us
  transfers between devices with their start and end apart: 11, of which 9 were waited for; matrix products, arithmetic and copies ran while one was open for 0% of the time, Pallas kernels for 5%

profile of v1, /device:TPU:8, one launch (start us, length us, event | category | flops | bytes accessed | tf_op | source)
XLA Modules:
  0.0 57.9 jit_solution(11426912935582137760)
XLA Ops:
  0.0 0.0 copy-start.4
  0.0 0.7 %copy-done.4 = s32[1,1,8,2]{2,3,1,0:T(2,128)S(1)} copy-done((s32[1,1,8,2]{2,3,1,0:T(2,128)S(1)}, s32[1,1,8,2]{2,3,1,0:T(2,128)}, u32[]{:S(2)}) %copy-start.4) | copy-done | bytes 88
  0.7 0.7 %copy.16 = s32[8,1,2]{2,1,0:T(1,128)} copy(s32[8,1,2]{0,2,1:T(2,128)S(1)} %bitcast.17) | data formatting | bytes 128 | tf_op jit(solution)/shard_map/reshape;reshape | solution.py:125
  1.4 6.3 %all-to-all-start = ((s32[8,1,2]{2,1,0:T(1,128)}), s32[8,1,2]{2,1,0:T(1,128)S(1)}, u32[]{:S(2)}, u32[]{:S(2)}) async-start(s32[8,1,2]{2,1,0:T(1,128)} %copy.16), calls=%async_computation | async-start | bytes 8192 | tf_op jit(solution)/shard_map/all_to_all | solution.py:125
  7.6 0.0 copy-start.5
  7.6 0.7 %copy-done.5 = s32[1,1,8,2]{2,3,1,0:T(2,128)S(1)} copy-done((s32[1,1,8,2]{2,3,1,0:T(2,128)S(1)}, s32[1,1,8,2]{2,3,1,0:T(2,128)}, u32[]{:S(2)}) %copy-start.5) | copy-done | bytes 88
  8.3 0.1 copy.25.left_ref
  8.4 0.0 copy-start.6
  8.4 0.7 %copy-done.6 = s32[1,1,8,2]{2,3,1,0:T(2,128)S(1)} copy-done((s32[1,1,8,2]{2,3,1,0:T(2,128)S(1)}, s32[1,1,8,2]{2,3,1,0:T(2,128)}, u32[]{:S(2)}) %copy-start.6) | copy-done | bytes 88
  9.1 0.1 copy.27.kind_ref
  9.2 3.4 %all-to-all-done = s32[8,1,2]{2,1,0:T(1,128)S(1)} async-done(((s32[8,1,2]{2,1,0:T(1,128)}), s32[8,1,2]{2,1,0:T(1,128)S(1)}, u32[]{:S(2)}, u32[]{:S(2)}) %all-to-all-start) | async-done | bytes 96 | tf_op jit(solution)/shard_map/all_to_all | solution.py:125
  12.5 0.0 copy-start
  12.5 1.2 %copy-done = f32[2048,128]{1,0:T(8,128)S(1)} copy-done((f32[2048,128]{1,0:T(8,128)S(1)}, f32[2048,128]{1,0:T(8,128)}, u32[]{:S(2)}) %copy-start) | copy-done | bytes 1048600
  13.8 0.0 copy-start.2
  13.8 0.8 %copy-done.2 = s32[1,1,8,2,8,128]{5,4,3,2,1,0:T(8,128)S(1)} copy-done((s32[1,1,8,2,8,128]{5,4,3,2,1,0:T(8,128)S(1)}, s32[1,1,8,2,8,128]{5,4,3,2,1,0:T(8,128)}, u32[]{:S(2)}) %copy-start.2) | copy-done | bytes 65560
  14.6 0.0 copy-start.1
  14.6 0.0 copy-start.3
  14.6 0.8 %shard_map.55 = (f32[2,136,128]{2,1,0:T(8,128)S(1)}, f32[2,136,128]{2,1,0:T(8,128)S(1)}, f32[2,136,128]{2,1,0:T(8,128)S(1)}, f32[2,136,128]{2,1,0:T(8,128)S(1)},...) custom-call(s32[8,2]{1,0:T(8,128)S(1)} %copy.25.left_ref, ...), custom_call_target="tpu_custom_call" | custom-call | tf_op jit(solution)/shard_map/pallas_call | solution.py:132
  15.4 0.7 %collective-permute-start = (f32[2,136,128]{2,1,0:T(8,128)S(1)}, f32[2,136,128]{2,1,0:T(8,128)S(1)}, u32[]{:S(2)}, u32[]{:S(2)}) collective-permute-start(f32[2,136,128]{2,1,0:T(8,128)S(1)} %get-tuple-element.16), channel_id=1, source_target_pairs={{0,4},{4,0},{8,12},{12,8},{16,20},{20,16},{24,28},{28,24},{1,5},{5... | collective-permute-start | bytes 417800 | tf_op jit(solution)/shard_map/ppermute | solution.py:113
  16.1 1.4 %collective-permute-start.1 = (f32[2,136,128]{2,1,0:T(8,128)S(1)}, f32[2,136,128]{2,1,0:T(8,128)S(1)}, u32[]{:S(2)}, u32[]{:S(2)}) collective-permute-start(f32[2,136,128]{2,1,0:T(8,128)S(1)} %get-tuple-element.17), channel_id=1, source_target_pairs={{0,8},{4,12},{8,0},{12,4},{16,24},{20,28},{24,16},{28,20},{1,9},{5... | collective-permute-start | bytes 417800 | tf_op jit(solution)/shard_map/ppermute | solution.py:113
  17.5 1.5 %collective-permute-start.2 = (f32[2,136,128]{2,1,0:T(8,128)S(1)}, f32[2,136,128]{2,1,0:T(8,128)S(1)}, u32[]{:S(2)}, u32[]{:S(2)}) collective-permute-start(f32[2,136,128]{2,1,0:T(8,128)S(1)} %get-tuple-element.18), channel_id=1, source_target_pairs={{0,12},{4,8},{8,4},{12,0},{16,28},{20,24},{24,20},{28,16},{1,13},{... | collective-permute-start | bytes 417800 | tf_op jit(solution)/shard_map/ppermute | solution.py:113
  19.0 0.6 %collective-permute-start.3 = (f32[2,136,128]{2,1,0:T(8,128)S(1)}, f32[2,136,128]{2,1,0:T(8,128)S(1)}, u32[]{:S(2)}, u32[]{:S(2)}) collective-permute-start(f32[2,136,128]{2,1,0:T(8,128)S(1)} %get-tuple-element.19), channel_id=1, source_target_pairs={{0,16},{4,20},{8,24},{12,28},{16,0},{20,4},{24,8},{28,12},{1,17},{... | collective-permute-start | bytes 417800 | tf_op jit(solution)/shard_map/ppermute | solution.py:113
  19.6 2.4 %collective-permute-start.4 = (f32[2,136,128]{2,1,0:T(8,128)S(1)}, f32[2,136,128]{2,1,0:T(8,128)S(1)}, u32[]{:S(2)}, u32[]{:S(2)}) collective-permute-start(f32[2,136,128]{2,1,0:T(8,128)S(1)} %get-tuple-element.20), channel_id=1, source_target_pairs={{0,20},{4,16},{8,28},{12,24},{16,4},{20,0},{24,12},{28,8},{1,21},{... | collective-permute-start | bytes 417800 | tf_op jit(solution)/shard_map/ppermute | solution.py:113
  21.9 0.1 collective-permute-done.refs_0_
  22.0 0.6 %collective-permute-start.5 = (f32[2,136,128]{2,1,0:T(8,128)S(1)}, f32[2,136,128]{2,1,0:T(8,128)S(1)}, u32[]{:S(2)}, u32[]{:S(2)}) collective-permute-start(f32[2,136,128]{2,1,0:T(8,128)S(1)} %get-tuple-element.21), channel_id=1, source_target_pairs={{0,24},{4,28},{8,16},{12,20},{16,8},{20,12},{24,0},{28,4},{1,25},{... | collective-permute-start | bytes 417800 | tf_op jit(solution)/shard_map/ppermute | solution.py:113
  22.6 0.0 collective-permute-done.1.refs_1_
  22.6 2.2 %collective-permute-start.6 = (f32[2,136,128]{2,1,0:T(8,128)S(1)}, f32[2,136,128]{2,1,0:T(8,128)S(1)}, u32[]{:S(2)}, u32[]{:S(2)}) collective-permute-start(f32[2,136,128]{2,1,0:T(8,128)S(1)} %get-tuple-element.22), channel_id=1, source_target_pairs={{0,28},{4,24},{8,20},{12,16},{16,12},{20,8},{24,4},{28,0},{1,29},{... | collective-permute-start | bytes 417800 | tf_op jit(solution)/shard_map/ppermute | solution.py:113
  24.8 0.1 copy.22.right_ref
  24.9 1.6 %collective-permute-done.2.refs_2_ = f32[2,136,128]{2,1,0:T(8,128)S(1)} collective-permute-done((f32[2,136,128]{2,1,0:T(8,128)S(1)}, f32[2,136,128]{2,1,0:T(8,128)S(1)}, u32[]{:S(2)}, u32[]{:S(2)}) %collective-permute-start.2) | collective-permute-done | bytes 139296 | tf_op jit(solution)/shard_map/ppermute | solution.py:113
  26.5 0.0 copy-done.1
  26.6 0.0 copy-done.3
  26.6 2.9 %shard_map.56.before_ref = f32[16,128,128]{2,1,0:T(8,128)S(1)} custom-call(s32[8,2]{1,0:T(8,128)S(1)} %copy.25.left_ref, s32[8,2]{1,0:T(8,128)S(1)} %copy.22.right_ref, s32[8,2]{1,0:T(8,128)S(1)} %bitcast.15, s32[8,2]{1,0:T(8,128)S(1)} %copy.27.kind_ref, f32[16,128,128]{2,1,0:T(8,128)S(1)} %bitcast.9, s32[8,2,8,128]{3,2,1,0:T(8,128)S(1)} %bitcast.12, ...), custom_call_target="tpu_custom_call" | custom-call | flops 201326592 | bytes 2097152 | tf_op jit(solution)/shard_map/pallas_call | solution.py:141
  29.5 5.9 %collective-permute-done.3.refs_0_ = f32[2,136,128]{2,1,0:T(8,128)S(1)} collective-permute-done((f32[2,136,128]{2,1,0:T(8,128)S(1)}, f32[2,136,128]{2,1,0:T(8,128)S(1)}, u32[]{:S(2)}, u32[]{:S(2)}) %collective-permute-start.3) | collective-permute-done | bytes 139296 | tf_op jit(solution)/shard_map/ppermute | solution.py:113
  35.3 3.0 %collective-permute-done.4.refs_1_ = f32[2,136,128]{2,1,0:T(8,128)S(1)} collective-permute-done((f32[2,136,128]{2,1,0:T(8,128)S(1)}, f32[2,136,128]{2,1,0:T(8,128)S(1)}, u32[]{:S(2)}, u32[]{:S(2)}) %collective-permute-start.4) | collective-permute-done | bytes 139296 | tf_op jit(solution)/shard_map/ppermute | solution.py:113
  38.3 4.1 %collective-permute-done.5.refs_2_ = f32[2,136,128]{2,1,0:T(8,128)S(1)} collective-permute-done((f32[2,136,128]{2,1,0:T(8,128)S(1)}, f32[2,136,128]{2,1,0:T(8,128)S(1)}, u32[]{:S(2)}, u32[]{:S(2)}) %collective-permute-start.5) | collective-permute-done | bytes 139296 | tf_op jit(solution)/shard_map/ppermute | solution.py:113
  42.4 1.5 %collective-permute-done.6.refs_3_ = f32[2,136,128]{2,1,0:T(8,128)S(1)} collective-permute-done((f32[2,136,128]{2,1,0:T(8,128)S(1)}, f32[2,136,128]{2,1,0:T(8,128)S(1)}, u32[]{:S(2)}, u32[]{:S(2)}) %collective-permute-start.6) | collective-permute-done | bytes 139296 | tf_op jit(solution)/shard_map/ppermute | solution.py:113
  43.9 3.1 %shard_map.57 = (f32[4,128,128]{2,1,0:T(8,128)S(1)}, f32[4,128,128]{2,1,0:T(8,128)S(1)}, f32[4,128,128]{2,1,0:T(8,128)S(1)}, f32[4,128,128]{2,1,0:T(8,128)S(1)}) custom-call(s32[8,2]{1,0:T(8,128)S(1)} %copy.25.left_ref, s32[8,2]{1,0:T(8,128)S(1)} %bitcast.16, s32[8,2]{1,0:T(8,128)S(1)} %copy.27.kind_ref, f32[16,128,128]{2,1,0:T(8,128)S(1)} %bitcast.10, ...), custom_call_target="tpu_custom_call" | custom-call | flops 201326592 | bytes 3145728 | tf_op jit(solution)/shard_map/pallas_call | solution.py:151
  47.1 0.1 collective-permute-start.8
  47.1 0.5 collective-permute-start.7
  47.6 1.0 %collective-permute-done.8 = f32[4,128,128]{2,1,0:T(8,128)S(1)} collective-permute-done((f32[4,128,128]{2,1,0:T(8,128)S(1)}, f32[4,128,128]{2,1,0:T(8,128)S(1)}, u32[]{:S(2)}, u32[]{:S(2)}) %collective-permute-start.8) | collective-permute-done | bytes 262176 | tf_op jit(solution)/shard_map/ppermute | solution.py:113
  48.7 1.6 %collective-permute-start.9 = (f32[4,128,128]{2,1,0:T(8,128)S(1)}, f32[4,128,128]{2,1,0:T(8,128)S(1)}, u32[]{:S(2)}, u32[]{:S(2)}) collective-permute-start(f32[4,128,128]{2,1,0:T(8,128)S(1)} %add.10), channel_id=1, source_target_pairs={{0,2},{1,3},{2,0},{3,1},{4,6},{5,7},{6,4},{7,5},{8,10},{9,11},{10,... | collective-permute-start | bytes 786440 | tf_op jit(solution)/shard_map/ppermute | solution.py:113
  50.3 0.0 collective-permute-done.7
  50.3 6.9 %collective-permute-done.9 = f32[4,128,128]{2,1,0:T(8,128)S(1)} collective-permute-done((f32[4,128,128]{2,1,0:T(8,128)S(1)}, f32[4,128,128]{2,1,0:T(8,128)S(1)}, u32[]{:S(2)}, u32[]{:S(2)}) %collective-permute-start.9) | collective-permute-done | bytes 262176 | tf_op jit(solution)/shard_map/ppermute | solution.py:113
  57.1 0.7 %add_add_fusion = f32[4,128,128]{2,1,0:T(8,128)} fusion(f32[4,128,128]{2,1,0:T(8,128)S(1)} %collective-permute-done.9, f32[4,128,128]{2,1,0:T(8,128)S(1)} %get-tuple-element.23, f32[4,128,128]{2,1,0:T(8,128)S(1)} %collective-permute-done.7), kind=kLoop, calls=%fused_computation | loop fusion | flops 131072 | bytes 1048576 | tf_op jit(solution)/shard_map/add | solution.py:162
  (1 shorter events, 0.0 us)
Async XLA Ops:
  0.0 0.7 %copy-start.4 = (s32[1,1,8,2]{2,3,1,0:T(2,128)S(1)}, s32[1,1,8,2]{2,3,1,0:T(2,128)}, u32[]{:S(2)}) copy-start(s32[1,1,8,2]{2,3,1,0:T(2,128)} %param.7) | copy-start | bytes 196
  1.4 11.2 %all-to-all-start = ((s32[8,1,2]{2,1,0:T(1,128)}), s32[8,1,2]{2,1,0:T(1,128)S(1)}, u32[]{:S(2)}, u32[]{:S(2)}) async-start(s32[8,1,2]{2,1,0:T(1,128)} %copy.16), calls=%async_computation | async-start | bytes 8192 | tf_op jit(solution)/shard_map/all_to_all | solution.py:125
  7.6 0.7 %copy-start.5 = (s32[1,1,8,2]{2,3,1,0:T(2,128)S(1)}, s32[1,1,8,2]{2,3,1,0:T(2,128)}, u32[]{:S(2)}) copy-start(s32[1,1,8,2]{2,3,1,0:T(2,128)} %param.6) | copy-start | bytes 196
  8.4 0.7 %copy-start.6 = (s32[1,1,8,2]{2,3,1,0:T(2,128)S(1)}, s32[1,1,8,2]{2,3,1,0:T(2,128)}, u32[]{:S(2)}) copy-start(s32[1,1,8,2]{2,3,1,0:T(2,128)} %param.8) | copy-start | bytes 196
  12.5 1.2 %copy-start = (f32[2048,128]{1,0:T(8,128)S(1)}, f32[2048,128]{1,0:T(8,128)}, u32[]{:S(2)}) copy-start(f32[2048,128]{1,0:T(8,128)} %param.5) | copy-start | bytes 3145732
  13.8 0.8 %copy-start.2 = (s32[1,1,8,2,8,128]{5,4,3,2,1,0:T(8,128)S(1)}, s32[1,1,8,2,8,128]{5,4,3,2,1,0:T(8,128)}, u32[]{:S(2)}) copy-start(s32[1,1,8,2,8,128]{5,4,3,2,1,0:T(8,128)} %param.9) | copy-start | bytes 196612
  14.6 11.9 %copy-start.1 = (f32[2048,128]{1,0:T(8,128)S(1)}, f32[2048,128]{1,0:T(8,128)}, u32[]{:S(2)}) copy-start(f32[2048,128]{1,0:T(8,128)} %param.5) | copy-start | bytes 3145732
  14.6 11.9 %copy-start.3 = (s32[1,1,8,2,8,128]{5,4,3,2,1,0:T(8,128)S(1)}, s32[1,1,8,2,8,128]{5,4,3,2,1,0:T(8,128)}, u32[]{:S(2)}) copy-start(s32[1,1,8,2,8,128]{5,4,3,2,1,0:T(8,128)} %param.9) | copy-start | bytes 196612
  15.4 6.6 %collective-permute-start = (f32[2,136,128]{2,1,0:T(8,128)S(1)}, f32[2,136,128]{2,1,0:T(8,128)S(1)}, u32[]{:S(2)}, u32[]{:S(2)}) collective-permute-start(f32[2,136,128]{2,1,0:T(8,128)S(1)} %get-tuple-element.16), channel_id=1, source_target_pairs={{0,4},{4,0},{8,12},{12,8},{16,20},{20,16},{24,28},{28,24},{1,5},{5... | collective-permute-start | bytes 417800 | tf_op jit(solution)/shard_map/ppermute | solution.py:113
  16.1 6.5 %collective-permute-start.1 = (f32[2,136,128]{2,1,0:T(8,128)S(1)}, f32[2,136,128]{2,1,0:T(8,128)S(1)}, u32[]{:S(2)}, u32[]{:S(2)}) collective-permute-start(f32[2,136,128]{2,1,0:T(8,128)S(1)} %get-tuple-element.17), channel_id=1, source_target_pairs={{0,8},{4,12},{8,0},{12,4},{16,24},{20,28},{24,16},{28,20},{1,9},{5... | collective-permute-start | bytes 417800 | tf_op jit(solution)/shard_map/ppermute | solution.py:113
  17.5 9.0 %collective-permute-start.2 = (f32[2,136,128]{2,1,0:T(8,128)S(1)}, f32[2,136,128]{2,1,0:T(8,128)S(1)}, u32[]{:S(2)}, u32[]{:S(2)}) collective-permute-start(f32[2,136,128]{2,1,0:T(8,128)S(1)} %get-tuple-element.18), channel_id=1, source_target_pairs={{0,12},{4,8},{8,4},{12,0},{16,28},{20,24},{24,20},{28,16},{1,13},{... | collective-permute-start | bytes 417800 | tf_op jit(solution)/shard_map/ppermute | solution.py:113
  19.0 16.4 %collective-permute-start.3 = (f32[2,136,128]{2,1,0:T(8,128)S(1)}, f32[2,136,128]{2,1,0:T(8,128)S(1)}, u32[]{:S(2)}, u32[]{:S(2)}) collective-permute-start(f32[2,136,128]{2,1,0:T(8,128)S(1)} %get-tuple-element.19), channel_id=1, source_target_pairs={{0,16},{4,20},{8,24},{12,28},{16,0},{20,4},{24,8},{28,12},{1,17},{... | collective-permute-start | bytes 417800 | tf_op jit(solution)/shard_map/ppermute | solution.py:113
  19.6 18.8 %collective-permute-start.4 = (f32[2,136,128]{2,1,0:T(8,128)S(1)}, f32[2,136,128]{2,1,0:T(8,128)S(1)}, u32[]{:S(2)}, u32[]{:S(2)}) collective-permute-start(f32[2,136,128]{2,1,0:T(8,128)S(1)} %get-tuple-element.20), channel_id=1, source_target_pairs={{0,20},{4,16},{8,28},{12,24},{16,4},{20,0},{24,12},{28,8},{1,21},{... | collective-permute-start | bytes 417800 | tf_op jit(solution)/shard_map/ppermute | solution.py:113
  22.0 20.4 %collective-permute-start.5 = (f32[2,136,128]{2,1,0:T(8,128)S(1)}, f32[2,136,128]{2,1,0:T(8,128)S(1)}, u32[]{:S(2)}, u32[]{:S(2)}) collective-permute-start(f32[2,136,128]{2,1,0:T(8,128)S(1)} %get-tuple-element.21), channel_id=1, source_target_pairs={{0,24},{4,28},{8,16},{12,20},{16,8},{20,12},{24,0},{28,4},{1,25},{... | collective-permute-start | bytes 417800 | tf_op jit(solution)/shard_map/ppermute | solution.py:113
  22.6 21.3 %collective-permute-start.6 = (f32[2,136,128]{2,1,0:T(8,128)S(1)}, f32[2,136,128]{2,1,0:T(8,128)S(1)}, u32[]{:S(2)}, u32[]{:S(2)}) collective-permute-start(f32[2,136,128]{2,1,0:T(8,128)S(1)} %get-tuple-element.22), channel_id=1, source_target_pairs={{0,28},{4,24},{8,20},{12,16},{16,12},{20,8},{24,4},{28,0},{1,29},{... | collective-permute-start | bytes 417800 | tf_op jit(solution)/shard_map/ppermute | solution.py:113
  47.1 1.6 %collective-permute-start.8 = (f32[4,128,128]{2,1,0:T(8,128)S(1)}, f32[4,128,128]{2,1,0:T(8,128)S(1)}, u32[]{:S(2)}, u32[]{:S(2)}) collective-permute-start(f32[4,128,128]{2,1,0:T(8,128)S(1)} %get-tuple-element.26), channel_id=1, source_target_pairs={{0,1},{1,0},{2,3},{3,2},{4,5},{5,4},{6,7},{7,6},{8,9},{9,8},{10,11... | collective-permute-start | bytes 786440 | tf_op jit(solution)/shard_map/ppermute | solution.py:113
  47.1 3.1 %collective-permute-start.7 = (f32[4,128,128]{2,1,0:T(8,128)S(1)}, f32[4,128,128]{2,1,0:T(8,128)S(1)}, u32[]{:S(2)}, u32[]{:S(2)}) collective-permute-start(f32[4,128,128]{2,1,0:T(8,128)S(1)} %get-tuple-element.24), channel_id=1, source_target_pairs={{0,1},{1,0},{2,3},{3,2},{4,5},{5,4},{6,7},{7,6},{8,9},{9,8},{10,11... | collective-permute-start | bytes 786440 | tf_op jit(solution)/shard_map/ppermute | solution.py:113
  48.7 8.4 %collective-permute-start.9 = (f32[4,128,128]{2,1,0:T(8,128)S(1)}, f32[4,128,128]{2,1,0:T(8,128)S(1)}, u32[]{:S(2)}, u32[]{:S(2)}) collective-permute-start(f32[4,128,128]{2,1,0:T(8,128)S(1)} %add.10), channel_id=1, source_target_pairs={{0,2},{1,3},{2,0},{3,1},{4,6},{5,7},{6,4},{7,5},{8,10},{9,11},{10,... | collective-permute-start | bytes 786440 | tf_op jit(solution)/shard_map/ppermute | solution.py:113

commit v2 on v1

v2 whole, which is shorter than its diff:
```python
import functools

import jax
import jax.numpy as jnp
from jax import lax
from jax.experimental import pallas as pl
from jax.experimental.pallas import tpu as pltpu
from jax.sharding import PartitionSpec as P

F32 = jnp.float32
BF16 = jnp.bfloat16
SMEM = pl.BlockSpec(memory_space=pltpu.SMEM)
VMEM = pl.BlockSpec(memory_space=pltpu.VMEM)
HBM = pl.BlockSpec(memory_space=pltpu.HBM)
PARAMS = pltpu.CompilerParams(vmem_limit_bytes=16 * 1024 * 1024)


def halves(value):
    high = value.astype(BF16)
    return high, (value - high.astype(F32)).astype(BF16)


def product(left, right, left_dim, right_dim):
    deep = jnp.concatenate(left, left_dim)
    both = [jnp.concatenate([half, half], right_dim) for half in right]
    wide = jnp.concatenate(both, 1 - right_dim)
    sums = lax.dot_general(
        deep, wide, (((left_dim,), (right_dim,)), ((), ())), preferred_element_type=F32
    )
    width = sums.shape[1] // 2
    return sums[:, :width] + sums[:, width:]


def natural_target(edges):
    width = edges.shape[-1]
    row = lax.broadcasted_iota(jnp.int32, (width, width), 0).astype(F32)
    hit = row == edges[0:1, :]
    for which in range(1, edges.shape[0]):
        hit = hit | (row == edges[which : which + 1, :])
    return jnp.where(hit, 1.0, 0.0)


def own_id(ids_ref, asked_ref, place, me, peer, slot):
    return jnp.where(peer > me, ids_ref[0, slot, peer], asked_ref[place, slot, me])


def pack_kernel(shifts, places, ids_ref, asked_ref, latent_ref, coded_ref, *message_refs):
    me = lax.axis_index("rows")
    tile = latent_ref.shape[1]
    for shift, place, message_ref in zip(shifts, places, message_refs):
        peer = me ^ shift
        for slot in range(message_ref.shape[0]):
            block = own_id(ids_ref, asked_ref, place, me, peer, slot)
            message_ref[slot, :tile] = latent_ref[block]
            message_ref[slot, tile:] = coded_ref[peer, slot]


def add_peer(shift, place, total_ref, ids_ref, asked_ref, latent_ref, coded_ref, message_ref):
    me = lax.axis_index("rows")
    peer = me ^ shift
    low = peer > me
    quarter = lax.axis_index("pairs") * (total_ref.shape[0] // lax.axis_size("pairs"))
    tile = latent_ref.shape[1]
    for slot in range(message_ref.shape[0]):
        block = own_id(ids_ref, asked_ref, place, me, peer, slot)
        own = halves(latent_ref[block])
        other = halves(message_ref[slot, :tile])
        edges = jnp.where(low, coded_ref[peer, slot], message_ref[slot, tile:])
        target = natural_target(edges)
        target = jnp.where(low, target.T, target)
        residue = jax.nn.sigmoid(product(own, other, 1, 1)) - target
        total_ref[block ^ quarter] += product(halves(residue), other, 1, 0)


def setup_kernel(latent_ref, left_ref, right_ref, kind_ref, edges_ref, rows_ref, ids_ref, coded_ref, kinds_ref, ints_ref, sems):
    copies = [
        pltpu.make_async_copy(source, target, sems.at[at])
        for at, (source, target) in enumerate(
            (
                (kind_ref, kinds_ref),
                (edges_ref, ints_ref),
                (left_ref, ids_ref.at[0]),
                (right_ref, ids_ref.at[1]),
                (latent_ref, rows_ref),
            )
        )
    ]
    for copy in copies:
        copy.start()
    for copy in copies[:2]:
        copy.wait()
    peers, slots = edges_ref.shape[:2]
    for peer in range(peers):
        for slot in range(slots):
            edges = ints_ref[peer, slot].astype(F32)
            kind = jnp.broadcast_to(kinds_ref[slot : slot + 1, peer : peer + 1], edges.shape)
            coded_ref[peer, slot] = jnp.where(kind == 2, edges, -1.0)
    for copy in copies[2:]:
        copy.wait()


def add_own(total_ref, ids_ref, latent_ref, coded_ref):
    me = lax.axis_index("rows")
    quarter = lax.axis_index("pairs") * (total_ref.shape[0] // lax.axis_size("pairs"))
    for slot in range(coded_ref.shape[1]):
        left_block, right_block = ids_ref[0, slot, me], ids_ref[1, slot, me]
        left, right = halves(latent_ref[left_block]), halves(latent_ref[right_block])
        target = natural_target(coded_ref[me, slot])
        residue = halves(jax.nn.sigmoid(product(right, left, 1, 1)) - target)
        total_ref[left_block ^ quarter] += product(residue, right, 0, 0)
        total_ref[right_block ^ quarter] += product(residue, left, 1, 0)


def first_kernel(shifts, places, ids_ref, asked_ref, latent_ref, coded_ref, *refs):
    *message_refs, total_ref = refs
    total_ref[...] = jnp.zeros_like(total_ref)
    add_own(total_ref, ids_ref, latent_ref, coded_ref)
    for shift, place, message_ref in zip(shifts, places, message_refs):
        add_peer(shift, place, total_ref, ids_ref, asked_ref, latent_ref, coded_ref, message_ref)


def middle_kernel(shifts, places, ids_ref, asked_ref, latent_ref, coded_ref, before_ref, *refs):
    *message_refs, total_ref = refs
    total_ref[...] = before_ref[...]
    for shift, place, message_ref in zip(shifts, places, message_refs):
        add_peer(shift, place, total_ref, ids_ref, asked_ref, latent_ref, coded_ref, message_ref)


def last_kernel(shifts, places, ids_ref, asked_ref, latent_ref, coded_ref, before_ref, *refs):
    count = len(shifts)
    message_refs, part_refs, total_ref = refs[:count], refs[count:-1], refs[-1]
    total_ref[...] = before_ref[...]
    for shift, place, message_ref in zip(shifts, places, message_refs):
        add_peer(shift, place, total_ref, ids_ref, asked_ref, latent_ref, coded_ref, message_ref)
    for place, part_ref in enumerate(part_refs):
        depth = part_ref.shape[0]
        part_ref[...] = total_ref[place * depth : (place + 1) * depth]


def shift_groups(order, top):
    near, far = [at for at in order if at < top], [at for at in order if at >= top]
    near, far, first, last = near[1:], far[1:-2], near[:1] + far[:1], far[-2:]
    middle = [part[at : at + 2] for part in (near, far) for at in range(0, len(part), 2)]
    return [first] + middle + [last]


def estimate(slots, width, moved):
    return pl.CostEstimate(flops=12 * slots * width**3, bytes_accessed=moved, transcendentals=slots * width**2)


def swap(value, axis, shift):
    return lax.ppermute(value, axis, [(at, at ^ shift) for at in range(lax.axis_size(axis))])


def body(latent, left_block, right_block, slot_kind, edge_cols):
    tile, width = edge_cols.shape[-1], latent.shape[1]
    blocks = latent.reshape(-1, tile, width)
    peers, slots = left_block.shape[2:]
    lists = edge_cols.shape[4]

    def table(value):
        return value.reshape(peers, slots).T

    edges = edge_cols.reshape(peers, slots, lists, tile)
    blocks, ids, coded = pl.pallas_call(
        setup_kernel,
        out_shape=(
            jax.ShapeDtypeStruct(blocks.shape, F32),
            jax.ShapeDtypeStruct((2, slots, peers), jnp.int32),
            jax.ShapeDtypeStruct(edges.shape, F32),
        ),
        in_specs=[HBM] * 5,
        out_specs=(VMEM,) * 3,
        scratch_shapes=[
            pltpu.VMEM((slots, peers), jnp.int32),
            pltpu.VMEM(edges.shape, jnp.int32),
            pltpu.SemaphoreType.DMA((5,)),
        ],
        compiler_params=PARAMS,
    )(blocks, table(left_block), table(right_block), table(slot_kind), edges)

    message = jax.ShapeDtypeStruct((slots, tile + lists, width), F32)
    asked, where, arrived = right_block, [0], {}
    bit = peers // 2
    while bit:
        if len(where) == 1:
            asked = jnp.concatenate([ids[1:], table(swap(asked, "rows", bit))[None]])
        else:
            asked = jnp.concatenate([asked, swap(asked, "rows", bit)])
        where = where + [at ^ bit for at in where]
        shifts = [at for at in reversed(range(1, peers)) if at & -at == bit]
        sent = pl.pallas_call(
            functools.partial(pack_kernel, shifts, [where.index(at) for at in shifts]),
            out_shape=[message] * len(shifts),
            in_specs=[SMEM] * 2 + [VMEM] * 2,
            out_specs=[VMEM] * len(shifts),
            compiler_params=PARAMS,
        )(ids, asked, blocks, coded)
        for shift, value in zip(shifts, sent):
            arrived[shift] = swap(value, "rows", shift)
        bit //= 2

    whole = jax.ShapeDtypeStruct(blocks.shape, F32)
    parts = lax.axis_size("pairs")
    part = jax.ShapeDtypeStruct((blocks.shape[0] // parts, tile, width), F32)
    groups = shift_groups(list(arrived), peers // 2)
    total = ()
    for group in groups:
        first, last = group is groups[0], group is groups[-1]
        total = pl.pallas_call(
            functools.partial(
                first_kernel if first else last_kernel if last else middle_kernel,
                group,
                [where.index(at) for at in group],
            ),
            out_shape=[part] * parts if last else [whole],
            in_specs=[SMEM] * 2 + [VMEM] * (2 + len(total) + len(group)),
            out_specs=[VMEM] * (parts if last else 1),
            scratch_shapes=[pltpu.VMEM(blocks.shape, F32)] if last else [],
            input_output_aliases={} if first or last else {4: 0},
            compiler_params=PARAMS,
            cost_estimate=estimate(slots * len(group), tile, 3 * blocks.size * 4),
        )(ids, asked, blocks, coded, *total, *[arrived[at] for at in group])
    held = total
    far_half = held[2] + swap(held[3], "pairs", 1)
    kept = swap(held[1], "pairs", 1)
    result = held[0] + kept + swap(far_half, "pairs", 2)
    return result.reshape(-1, width)


def solution(mesh):
    return jax.shard_map(
        body,
        mesh=mesh,
        in_specs=(
            P("rows", None),
            P("rows", "pairs", None, None),
            P("rows", "pairs", None, None),
            P("rows", "pairs", None, None),
            P("rows", "pairs", None, None, None, None),
        ),
        out_specs=P(("rows", "pairs"), None),
        check_vma=False,
    )
```

time: 58.1 us -> 51.1 us (0.88)
  the two profiles are of different devices: /device:TPU:8 before, /device:TPU:0 now
where the time goes in v2:
time: 51.1 us; the launch traced here: 50.9 us
  starting transfers between devices  19.3 us (38%)
  waiting for transfers between devices  18.9 us (37%)
  Pallas kernels  9.03 us (18%)
  local copies, waits for them, and re-layouts  2.78 us (5%)
  other arithmetic  0.8 us (2%)
    ppermute x13, starting transfers between devices, swap(): lax.ppermute(value, axis, [(at, at ^ shift) for at in range(lax.axis_size...  19.3 us
    ppermute x13, waiting for transfers between devices, swap(): lax.ppermute(value, axis, [(at, at ^ shift) for at in range(lax.axis_size...  18.9 us
    pallas_call x4, Pallas kernels, body(): pl.pallas_call(functools.partial(first_kernel if first else last_kernel i...  6.7 us
    unnamed x10, local copies, waits for them, and re-layouts  2.78 us
    pallas_call x3, Pallas kernels, body(): pl.pallas_call(functools.partial(pack_kernel, shifts, [where.index(at) fo...  2.03 us
  transfers between devices with their start and end apart: 13, of which 7 were waited for; matrix products, arithmetic and copies ran while one was open for 0% of the time, Pallas kernels for 14%

profile of v2, /device:TPU:0, one launch (start us, length us, event | category | flops | bytes accessed | tf_op | source)
XLA Modules:
  0.0 50.9 jit_solution(7535243049578196063)
XLA Ops:
  0.0 4.0 %collective-permute-start = (s32[1,1,8,2]{2,3,1,0:T(2,128)}, s32[1,1,8,2]{2,3,1,0:T(2,128)S(1)}, u32[]{:S(2)}, u32[]{:S(2)}) collective-permute-start(s32[1,1,8,2]{2,3,1,0:T(2,128)} %param.7), channel_id=1, source_target_pairs={{0,16},{4,20},{8,24},{12,28},{16,0},{20,4},{24,8},{28,12},{1,17},{... | collective-permute-start | bytes 200 | tf_op jit(solution)/shard_map/ppermute | solution.py:152
  4.0 0.0 copy-start.3
  4.0 0.0 copy-start.4
  4.0 0.0 copy-start.2
  4.0 0.7 %copy-done.3 = s32[1,1,8,2]{2,3,1,0:T(2,128)S(1)} copy-done((s32[1,1,8,2]{2,3,1,0:T(2,128)S(1)}, s32[1,1,8,2]{2,3,1,0:T(2,128)}, u32[]{:S(2)}) %copy-start.3) | copy-done | bytes 88
  4.7 0.0 copy-done.4
  4.8 0.0 copy-done.2
  4.8 0.0 copy-start
  4.8 1.2 %copy-done = f32[2048,128]{1,0:T(8,128)S(1)} copy-done((f32[2048,128]{1,0:T(8,128)S(1)}, f32[2048,128]{1,0:T(8,128)}, u32[]{:S(2)}) %copy-start) | copy-done | bytes 1048600
  6.0 0.0 copy-start.1
  6.0 0.8 %copy-done.1 = s32[1,1,8,2,8,128]{5,4,3,2,1,0:T(8,128)S(1)} copy-done((s32[1,1,8,2,8,128]{5,4,3,2,1,0:T(8,128)S(1)}, s32[1,1,8,2,8,128]{5,4,3,2,1,0:T(8,128)}, u32[]{:S(2)}) %copy-start.1) | copy-done | bytes 65560
  6.8 0.3 shard_map.55
  7.1 0.0 collective-permute-done
  7.2 1.6 %collective-permute-start.1 = (s32[2,2,8]{2,1,0:T(2,128)S(1)}, s32[2,2,8]{2,1,0:T(2,128)S(1)}, u32[]{:S(2)}, u32[]{:S(2)}) collective-permute-start(s32[2,2,8]{2,1,0:T(2,128)S(1)} %pad_add_fusion.2.asked_ref), channel_id=1, source_target_pairs={{0,8},{4,12},{8,0},{12,4},{16,24},{20,28},{24,16},{28,20},{1,9},{5... | collective-permute-start | bytes 392 | tf_op jit(solution)/shard_map/ppermute | solution.py:152
  8.8 0.6 %shard_map.57 = f32[2,136,128]{2,1,0:T(8,128)S(1)} custom-call(s32[2,2,8]{2,1,0:T(2,128)S(1)} %get-tuple-element.18.ids_ref, s32[2,2,8]{2,1,0:T(2,128)S(1)} %pad_add_fusion.2.asked_ref, f32[16,128,128]{2,1,0:T(8,128)S(1)} %get-tuple-element.19.latent_ref, f32[8,2,8,128]{3,2,1,0:T(8,128)S(1)} %get-tuple-element.20.coded_ref), custom_call_target="tpu_custom_call" | custom-call | tf_op jit(solution)/shard_map/pallas_call | solution.py:192
  9.4 1.6 %collective-permute-start.4 = (f32[2,136,128]{2,1,0:T(8,128)S(1)}, f32[2,136,128]{2,1,0:T(8,128)S(1)}, u32[]{:S(2)}, u32[]{:S(2)}) collective-permute-start(f32[2,136,128]{2,1,0:T(8,128)S(1)} %shard_map.57), channel_id=1, source_target_pairs={{0,16},{4,20},{8,24},{12,28},{16,0},{20,4},{24,8},{28,12},{1,17},{... | collective-permute-start | bytes 417800 | tf_op jit(solution)/shard_map/ppermute | solution.py:152
  11.0 0.0 collective-permute-done.1
  11.0 0.7 %shard_map.56 = (f32[2,136,128]{2,1,0:T(8,128)S(1)}, f32[2,136,128]{2,1,0:T(8,128)S(1)}) custom-call(s32[2,2,8]{2,1,0:T(2,128)S(1)} %get-tuple-element.18.ids_ref, s32[4,2,8]{2,1,0:T(2,128)S(1)} %pad_add_fusion.1.asked_ref, f32[16,128,128]{2,1,0:T(8,128)S(1)} %get-tuple-element.19.latent_ref, f32[8,2,8,128]{3,2,1,0:T(8,128)S(1)} %get-tuple-element.20.coded_ref), custom_call_target="tpu_custom_call" | custom-call | tf_op jit(solution)/shard_map/pallas_call | solution.py:192
  11.7 1.5 %collective-permute-start.3 = (f32[2,136,128]{2,1,0:T(8,128)S(1)}, f32[2,136,128]{2,1,0:T(8,128)S(1)}, u32[]{:S(2)}, u32[]{:S(2)}) collective-permute-start(f32[2,136,128]{2,1,0:T(8,128)S(1)} %get-tuple-element.21), channel_id=1, source_target_pairs={{0,8},{4,12},{8,0},{12,4},{16,24},{20,28},{24,16},{28,20},{1,9},{5... | collective-permute-start | bytes 417800 | tf_op jit(solution)/shard_map/ppermute | solution.py:152
  13.1 1.5 %collective-permute-start.2 = (s32[4,2,8]{2,1,0:T(2,128)S(1)}, s32[4,2,8]{2,1,0:T(2,128)S(1)}, u32[]{:S(2)}, u32[]{:S(2)}) collective-permute-start(s32[4,2,8]{2,1,0:T(2,128)S(1)} %pad_add_fusion.1.asked_ref), channel_id=1, source_target_pairs={{0,4},{4,0},{8,12},{12,8},{16,20},{20,16},{24,28},{28,24},{1,5},{5... | collective-permute-start | bytes 776 | tf_op jit(solution)/shard_map/ppermute | solution.py:152
  14.7 2.1 %collective-permute-done.2 = s32[4,2,8]{2,1,0:T(2,128)S(1)} collective-permute-done((s32[4,2,8]{2,1,0:T(2,128)S(1)}, s32[4,2,8]{2,1,0:T(2,128)S(1)}, u32[]{:S(2)}, u32[]{:S(2)}) %collective-permute-start.2) | collective-permute-done | bytes 288 | tf_op jit(solution)/shard_map/ppermute | solution.py:152
  16.7 0.7 %shard_map.59 = (f32[2,136,128]{2,1,0:T(8,128)S(1)}, f32[2,136,128]{2,1,0:T(8,128)S(1)}, f32[2,136,128]{2,1,0:T(8,128)S(1)}, f32[2,136,128]{2,1,0:T(8,128)S(1)}) custom-call(s32[2,2,8]{2,1,0:T(2,128)S(1)} %get-tuple-element.18.ids_ref, s32[8,2,8]{2,1,0:T(2,128)S(1)} %pad_add_fusion.asked_ref, f32[16,128,128]{2,1,0:T(8,128)S(1)} %get-tuple-element.19.latent_ref, ...), custom_call_target="tpu_custom_call" | custom-call | tf_op jit(solution)/shard_map/pallas_call | solution.py:192
  17.5 1.7 %collective-permute-start.5 = (f32[2,136,128]{2,1,0:T(8,128)S(1)}, f32[2,136,128]{2,1,0:T(8,128)S(1)}, u32[]{:S(2)}, u32[]{:S(2)}) collective-permute-start(f32[2,136,128]{2,1,0:T(8,128)S(1)} %get-tuple-element.22), channel_id=1, source_target_pairs={{0,12},{4,8},{8,4},{12,0},{16,28},{20,24},{24,20},{28,16},{1,13},{... | collective-permute-start | bytes 417800 | tf_op jit(solution)/shard_map/ppermute | solution.py:152
  19.2 0.5 collective-permute-start.6
  19.7 2.5 %collective-permute-start.7 = (f32[2,136,128]{2,1,0:T(8,128)S(1)}, f32[2,136,128]{2,1,0:T(8,128)S(1)}, u32[]{:S(2)}, u32[]{:S(2)}) collective-permute-start(f32[2,136,128]{2,1,0:T(8,128)S(1)} %get-tuple-element.24), channel_id=1, source_target_pairs={{0,24},{4,28},{8,16},{12,20},{16,8},{20,12},{24,0},{28,4},{1,25},{... | collective-permute-start | bytes 417800 | tf_op jit(solution)/shard_map/ppermute | solution.py:152
  22.2 0.0 collective-permute-done.4.refs_1_
  22.2 2.3 %collective-permute-start.8 = (f32[2,136,128]{2,1,0:T(8,128)S(1)}, f32[2,136,128]{2,1,0:T(8,128)S(1)}, u32[]{:S(2)}, u32[]{:S(2)}) collective-permute-start(f32[2,136,128]{2,1,0:T(8,128)S(1)} %get-tuple-element.25), channel_id=1, source_target_pairs={{0,28},{4,24},{8,20},{12,16},{16,12},{20,8},{24,4},{28,0},{1,29},{... | collective-permute-start | bytes 417800 | tf_op jit(solution)/shard_map/ppermute | solution.py:152
  24.4 0.0 collective-permute-done.3.refs_0_
  24.4 0.0 collective-permute-start.9
  24.5 1.9 %shard_map.58.before_ref = f32[16,128,128]{2,1,0:T(8,128)S(1)} custom-call(s32[2,2,8]{2,1,0:T(2,128)S(1)} %get-tuple-element.18.ids_ref, s32[8,2,8]{2,1,0:T(2,128)S(1)} %pad_add_fusion.asked_ref, f32[16,128,128]{2,1,0:T(8,128)S(1)} %get-tuple-element.19.latent_ref, f32[8,2,8,128]{3,2,1,0:T(8,128)S(1)} %get-tuple-element.20.coded_ref, ...), custom_call_target="tpu_custom_call" | custom-call | flops 100663296 | bytes 3145728 | tf_op jit(solution)/shard_map/pallas_call | solution.py:210
  26.4 0.0 collective-permute-done.5.refs_0_
  26.4 0.9 %collective-permute-done.6.refs_1_ = f32[2,136,128]{2,1,0:T(8,128)S(1)} collective-permute-done((f32[2,136,128]{2,1,0:T(8,128)S(1)}, f32[2,136,128]{2,1,0:T(8,128)S(1)}, u32[]{:S(2)}, u32[]{:S(2)}) %collective-permute-start.6) | collective-permute-done | bytes 139296 | tf_op jit(solution)/shard_map/ppermute | solution.py:152
  27.3 1.7 %shard_map.60.before_ref = f32[16,128,128]{2,1,0:T(8,128)S(1)} custom-call(s32[2,2,8]{2,1,0:T(2,128)S(1)} %get-tuple-element.18.ids_ref, s32[8,2,8]{2,1,0:T(2,128)S(1)} %pad_add_fusion.asked_ref, f32[16,128,128]{2,1,0:T(8,128)S(1)} %get-tuple-element.19.latent_ref, f32[8,2,8,128]{3,2,1,0:T(8,128)S(1)} %get-tuple-element.20.coded_ref, ...), custom_call_target="tpu_custom_call", output_to_operand_aliasing={{}: (4, {})} | custom-call | flops 100663296 | bytes 3145728 | tf_op jit(solution)/shard_map/pallas_call | solution.py:210
  29.0 0.1 collective-permute-done.7.refs_0_
  29.1 1.3 %shard_map.61.before_ref = f32[16,128,128]{2,1,0:T(8,128)S(1)} custom-call(s32[2,2,8]{2,1,0:T(2,128)S(1)} %get-tuple-element.18.ids_ref, s32[8,2,8]{2,1,0:T(2,128)S(1)} %pad_add_fusion.asked_ref, f32[16,128,128]{2,1,0:T(8,128)S(1)} %get-tuple-element.19.latent_ref, f32[8,2,8,128]{3,2,1,0:T(8,128)S(1)} %get-tuple-element.20.coded_ref, ...), custom_call_target="tpu_custom_call", output_to_operand_aliasing={{}: (4, {})} | custom-call | flops 50331648 | bytes 3145728 | tf_op jit(solution)/shard_map/pallas_call | solution.py:210
  30.5 0.2 collective-permute-done.8.refs_0_
  30.7 7.6 %collective-permute-done.9.refs_1_ = f32[2,136,128]{2,1,0:T(8,128)S(1)} collective-permute-done((f32[2,136,128]{2,1,0:T(8,128)S(1)}, f32[2,136,128]{2,1,0:T(8,128)S(1)}, u32[]{:S(2)}, u32[]{:S(2)}) %collective-permute-start.9) | collective-permute-done | bytes 139296 | tf_op jit(solution)/shard_map/ppermute | solution.py:152
  38.4 1.7 %shard_map.62 = (f32[4,128,128]{2,1,0:T(8,128)S(1)}, f32[4,128,128]{2,1,0:T(8,128)S(1)}, f32[4,128,128]{2,1,0:T(8,128)S(1)}, f32[4,128,128]{2,1,0:T(8,128)S(1)}) custom-call(s32[2,2,8]{2,1,0:T(2,128)S(1)} %get-tuple-element.18.ids_ref, s32[8,2,8]{2,1,0:T(2,128)S(1)} %pad_add_fusion.asked_ref, f32[16,128,128]{2,1,0:T(8,128)S(1)} %get-tuple-element.19.latent_ref, ...), custom_call_target="tpu_custom_call" | custom-call | flops 100663296 | bytes 3145728 | tf_op jit(solution)/shard_map/pallas_call | solution.py:210
  40.1 0.1 collective-permute-start.11
  40.2 0.5 collective-permute-start.10
  40.7 1.0 %collective-permute-done.11 = f32[4,128,128]{2,1,0:T(8,128)S(1)} collective-permute-done((f32[4,128,128]{2,1,0:T(8,128)S(1)}, f32[4,128,128]{2,1,0:T(8,128)S(1)}, u32[]{:S(2)}, u32[]{:S(2)}) %collective-permute-start.11) | collective-permute-done | bytes 262176 | tf_op jit(solution)/shard_map/ppermute | solution.py:152
  41.7 1.6 %collective-permute-start.12 = (f32[4,128,128]{2,1,0:T(8,128)S(1)}, f32[4,128,128]{2,1,0:T(8,128)S(1)}, u32[]{:S(2)}, u32[]{:S(2)}) collective-permute-start(f32[4,128,128]{2,1,0:T(8,128)S(1)} %add.10), channel_id=1, source_target_pairs={{0,2},{1,3},{2,0},{3,1},{4,6},{5,7},{6,4},{7,5},{8,10},{9,11},{10,... | collective-permute-start | bytes 786440 | tf_op jit(solution)/shard_map/ppermute | solution.py:152
  43.3 0.0 collective-permute-done.10
  43.3 6.9 %collective-permute-done.12 = f32[4,128,128]{2,1,0:T(8,128)S(1)} collective-permute-done((f32[4,128,128]{2,1,0:T(8,128)S(1)}, f32[4,128,128]{2,1,0:T(8,128)S(1)}, u32[]{:S(2)}, u32[]{:S(2)}) %collective-permute-start.12) | collective-permute-done | bytes 262176 | tf_op jit(solution)/shard_map/ppermute | solution.py:152
  50.1 0.8 %add_add_fusion = f32[4,128,128]{2,1,0:T(8,128)} fusion(f32[4,128,128]{2,1,0:T(8,128)S(1)} %collective-permute-done.12, f32[4,128,128]{2,1,0:T(8,128)S(1)} %get-tuple-element.27, f32[4,128,128]{2,1,0:T(8,128)S(1)} %collective-permute-done.10), kind=kLoop, calls=%fused_computation | loop fusion | flops 131072 | bytes 1048576 | tf_op jit(solution)/shard_map/add | solution.py:227
  (5 shorter events, 0.1 us)
Async XLA Ops:
  0.0 7.1 %collective-permute-start = (s32[1,1,8,2]{2,3,1,0:T(2,128)}, s32[1,1,8,2]{2,3,1,0:T(2,128)S(1)}, u32[]{:S(2)}, u32[]{:S(2)}) collective-permute-start(s32[1,1,8,2]{2,3,1,0:T(2,128)} %param.7), channel_id=1, source_target_pairs={{0,16},{4,20},{8,24},{12,28},{16,0},{20,4},{24,8},{28,12},{1,17},{... | collective-permute-start | bytes 200 | tf_op jit(solution)/shard_map/ppermute | solution.py:152
  4.0 0.7 %copy-start.3 = (s32[1,1,8,2]{2,3,1,0:T(2,128)S(1)}, s32[1,1,8,2]{2,3,1,0:T(2,128)}, u32[]{:S(2)}) copy-start(s32[1,1,8,2]{2,3,1,0:T(2,128)} %param.8) | copy-start | bytes 196
  4.0 0.7 %copy-start.4 = (s32[1,1,8,2]{2,3,1,0:T(2,128)S(1)}, s32[1,1,8,2]{2,3,1,0:T(2,128)}, u32[]{:S(2)}) copy-start(s32[1,1,8,2]{2,3,1,0:T(2,128)} %param.7) | copy-start | bytes 196
  4.0 0.7 %copy-start.2 = (s32[1,1,8,2]{2,3,1,0:T(2,128)S(1)}, s32[1,1,8,2]{2,3,1,0:T(2,128)}, u32[]{:S(2)}) copy-start(s32[1,1,8,2]{2,3,1,0:T(2,128)} %param.6) | copy-start | bytes 196
  4.8 1.2 %copy-start = (f32[2048,128]{1,0:T(8,128)S(1)}, f32[2048,128]{1,0:T(8,128)}, u32[]{:S(2)}) copy-start(f32[2048,128]{1,0:T(8,128)} %param.5) | copy-start | bytes 3145732
  6.0 0.8 %copy-start.1 = (s32[1,1,8,2,8,128]{5,4,3,2,1,0:T(8,128)S(1)}, s32[1,1,8,2,8,128]{5,4,3,2,1,0:T(8,128)}, u32[]{:S(2)}) copy-start(s32[1,1,8,2,8,128]{5,4,3,2,1,0:T(8,128)} %param.9) | copy-start | bytes 196612
  7.2 3.8 %collective-permute-start.1 = (s32[2,2,8]{2,1,0:T(2,128)S(1)}, s32[2,2,8]{2,1,0:T(2,128)S(1)}, u32[]{:S(2)}, u32[]{:S(2)}) collective-permute-start(s32[2,2,8]{2,1,0:T(2,128)S(1)} %pad_add_fusion.2.asked_ref), channel_id=1, source_target_pairs={{0,8},{4,12},{8,0},{12,4},{16,24},{20,28},{24,16},{28,20},{1,9},{5... | collective-permute-start | bytes 392 | tf_op jit(solution)/shard_map/ppermute | solution.py:152
  9.4 12.8 %collective-permute-start.4 = (f32[2,136,128]{2,1,0:T(8,128)S(1)}, f32[2,136,128]{2,1,0:T(8,128)S(1)}, u32[]{:S(2)}, u32[]{:S(2)}) collective-permute-start(f32[2,136,128]{2,1,0:T(8,128)S(1)} %shard_map.57), channel_id=1, source_target_pairs={{0,16},{4,20},{8,24},{12,28},{16,0},{20,4},{24,8},{28,12},{1,17},{... | collective-permute-start | bytes 417800 | tf_op jit(solution)/shard_map/ppermute | solution.py:152
  11.7 12.8 %collective-permute-start.3 = (f32[2,136,128]{2,1,0:T(8,128)S(1)}, f32[2,136,128]{2,1,0:T(8,128)S(1)}, u32[]{:S(2)}, u32[]{:S(2)}) collective-permute-start(f32[2,136,128]{2,1,0:T(8,128)S(1)} %get-tuple-element.21), channel_id=1, source_target_pairs={{0,8},{4,12},{8,0},{12,4},{16,24},{20,28},{24,16},{28,20},{1,9},{5... | collective-permute-start | bytes 417800 | tf_op jit(solution)/shard_map/ppermute | solution.py:152
  13.1 3.6 %collective-permute-start.2 = (s32[4,2,8]{2,1,0:T(2,128)S(1)}, s32[4,2,8]{2,1,0:T(2,128)S(1)}, u32[]{:S(2)}, u32[]{:S(2)}) collective-permute-start(s32[4,2,8]{2,1,0:T(2,128)S(1)} %pad_add_fusion.1.asked_ref), channel_id=1, source_target_pairs={{0,4},{4,0},{8,12},{12,8},{16,20},{20,16},{24,28},{28,24},{1,5},{5... | collective-permute-start | bytes 776 | tf_op jit(solution)/shard_map/ppermute | solution.py:152
  17.5 8.9 %collective-permute-start.5 = (f32[2,136,128]{2,1,0:T(8,128)S(1)}, f32[2,136,128]{2,1,0:T(8,128)S(1)}, u32[]{:S(2)}, u32[]{:S(2)}) collective-permute-start(f32[2,136,128]{2,1,0:T(8,128)S(1)} %get-tuple-element.22), channel_id=1, source_target_pairs={{0,12},{4,8},{8,4},{12,0},{16,28},{20,24},{24,20},{28,16},{1,13},{... | collective-permute-start | bytes 417800 | tf_op jit(solution)/shard_map/ppermute | solution.py:152
  19.2 8.1 %collective-permute-start.6 = (f32[2,136,128]{2,1,0:T(8,128)S(1)}, f32[2,136,128]{2,1,0:T(8,128)S(1)}, u32[]{:S(2)}, u32[]{:S(2)}) collective-permute-start(f32[2,136,128]{2,1,0:T(8,128)S(1)} %get-tuple-element.23), channel_id=1, source_target_pairs={{0,4},{4,0},{8,12},{12,8},{16,20},{20,16},{24,28},{28,24},{1,5},{5... | collective-permute-start | bytes 417800 | tf_op jit(solution)/shard_map/ppermute | solution.py:152
  19.7 9.5 %collective-permute-start.7 = (f32[2,136,128]{2,1,0:T(8,128)S(1)}, f32[2,136,128]{2,1,0:T(8,128)S(1)}, u32[]{:S(2)}, u32[]{:S(2)}) collective-permute-start(f32[2,136,128]{2,1,0:T(8,128)S(1)} %get-tuple-element.24), channel_id=1, source_target_pairs={{0,24},{4,28},{8,16},{12,20},{16,8},{20,12},{24,0},{28,4},{1,25},{... | collective-permute-start | bytes 417800 | tf_op jit(solution)/shard_map/ppermute | solution.py:152
  22.2 8.5 %collective-permute-start.8 = (f32[2,136,128]{2,1,0:T(8,128)S(1)}, f32[2,136,128]{2,1,0:T(8,128)S(1)}, u32[]{:S(2)}, u32[]{:S(2)}) collective-permute-start(f32[2,136,128]{2,1,0:T(8,128)S(1)} %get-tuple-element.25), channel_id=1, source_target_pairs={{0,28},{4,24},{8,20},{12,16},{16,12},{20,8},{24,4},{28,0},{1,29},{... | collective-permute-start | bytes 417800 | tf_op jit(solution)/shard_map/ppermute | solution.py:152
  24.4 13.9 %collective-permute-start.9 = (f32[2,136,128]{2,1,0:T(8,128)S(1)}, f32[2,136,128]{2,1,0:T(8,128)S(1)}, u32[]{:S(2)}, u32[]{:S(2)}) collective-permute-start(f32[2,136,128]{2,1,0:T(8,128)S(1)} %get-tuple-element.26), channel_id=1, source_target_pairs={{0,20},{4,16},{8,28},{12,24},{16,4},{20,0},{24,12},{28,8},{1,21},{... | collective-permute-start | bytes 417800 | tf_op jit(solution)/shard_map/ppermute | solution.py:152
  40.1 1.6 %collective-permute-start.11 = (f32[4,128,128]{2,1,0:T(8,128)S(1)}, f32[4,128,128]{2,1,0:T(8,128)S(1)}, u32[]{:S(2)}, u32[]{:S(2)}) collective-permute-start(f32[4,128,128]{2,1,0:T(8,128)S(1)} %get-tuple-element.30), channel_id=1, source_target_pairs={{0,1},{1,0},{2,3},{3,2},{4,5},{5,4},{6,7},{7,6},{8,9},{9,8},{10,11... | collective-permute-start | bytes 786440 | tf_op jit(solution)/shard_map/ppermute | solution.py:152
  40.2 3.1 %collective-permute-start.10 = (f32[4,128,128]{2,1,0:T(8,128)S(1)}, f32[4,128,128]{2,1,0:T(8,128)S(1)}, u32[]{:S(2)}, u32[]{:S(2)}) collective-permute-start(f32[4,128,128]{2,1,0:T(8,128)S(1)} %get-tuple-element.28), channel_id=1, source_target_pairs={{0,1},{1,0},{2,3},{3,2},{4,5},{5,4},{6,7},{7,6},{8,9},{9,8},{10,11... | collective-permute-start | bytes 786440 | tf_op jit(solution)/shard_map/ppermute | solution.py:152
  41.7 8.4 %collective-permute-start.12 = (f32[4,128,128]{2,1,0:T(8,128)S(1)}, f32[4,128,128]{2,1,0:T(8,128)S(1)}, u32[]{:S(2)}, u32[]{:S(2)}) collective-permute-start(f32[4,128,128]{2,1,0:T(8,128)S(1)} %add.10), channel_id=1, source_target_pairs={{0,2},{1,3},{2,0},{3,1},{4,6},{5,7},{6,4},{7,5},{8,10},{9,11},{10,... | collective-permute-start | bytes 786440 | tf_op jit(solution)/shard_map/ppermute | solution.py:152

commit v3 on v2

--- a/solution.py
+++ b/solution.py
@@ -12,6 +12,7 @@
 SMEM = pl.BlockSpec(memory_space=pltpu.SMEM)
 VMEM = pl.BlockSpec(memory_space=pltpu.VMEM)
 HBM = pl.BlockSpec(memory_space=pltpu.HBM)
+WAIT_FLOPS = 10**10
 PARAMS = pltpu.CompilerParams(vmem_limit_bytes=16 * 1024 * 1024)
 
 
@@ -70,6 +71,10 @@
         target = jnp.where(low, target.T, target)
         residue = jax.nn.sigmoid(product(own, other, 1, 1)) - target
         total_ref[block ^ quarter] += product(halves(residue), other, 1, 0)
+
+
+def copy_kernel(source_ref, target_ref):
+    target_ref[...] = source_ref[...]
 
 
 def setup_kernel(latent_ref, left_ref, right_ref, kind_ref, edges_ref, rows_ref, ids_ref, coded_ref, kinds_ref, ints_ref, sems):
@@ -137,11 +142,15 @@
         part_ref[...] = total_ref[place * depth : (place + 1) * depth]
 
 
-def shift_groups(order, top):
-    near, far = [at for at in order if at < top], [at for at in order if at >= top]
-    near, far, first, last = near[1:], far[1:-2], near[:1] + far[:1], far[-2:]
-    middle = [part[at : at + 2] for part in (near, far) for at in range(0, len(part), 2)]
-    return [first] + middle + [last]
+def shift_groups(peers):
+    top = peers // 2
+    sequence, bit = [], top
+    while bit:
+        stage = [at for at in reversed(range(1, peers)) if at & -at == bit]
+        sequence += sorted(stage, key=lambda at: (at < top) != (bit == 1))
+        bit //= 2
+    middle = sequence[1:-2]
+    return [sequence[:1]] + [middle[at : at + 2] for at in range(0, len(middle), 2)] + [[at] for at in sequence[-2:]]
 
 
 def estimate(slots, width, moved):
@@ -162,6 +171,14 @@
         return value.reshape(peers, slots).T
 
     edges = edge_cols.reshape(peers, slots, lists, tile)
+    own_asked = pl.pallas_call(
+        copy_kernel,
+        out_shape=jax.ShapeDtypeStruct((slots, peers), jnp.int32),
+        in_specs=[VMEM],
+        out_specs=VMEM,
+        compiler_params=PARAMS,
+        cost_estimate=pl.CostEstimate(flops=WAIT_FLOPS, bytes_accessed=4096, transcendentals=0),
+    )(table(right_block))
     blocks, ids, coded = pl.pallas_call(
         setup_kernel,
         out_shape=(
@@ -177,14 +194,14 @@
             pltpu.SemaphoreType.DMA((5,)),
         ],
         compiler_params=PARAMS,
-    )(blocks, table(left_block), table(right_block), table(slot_kind), edges)
+    )(blocks, table(left_block), own_asked, table(slot_kind), edges)
 
     message = jax.ShapeDtypeStruct((slots, tile + lists, width), F32)
-    asked, where, arrived = right_block, [0], {}
+    asked, where, arrived = own_asked, [0], {}
     bit = peers // 2
     while bit:
         if len(where) == 1:
-            asked = jnp.concatenate([ids[1:], table(swap(asked, "rows", bit))[None]])
+            asked = jnp.concatenate([ids[1:], swap(asked, "rows", bit)[None]])
         else:
             asked = jnp.concatenate([asked, swap(asked, "rows", bit)])
         where = where + [at ^ bit for at in where]
@@ -203,7 +220,7 @@
     whole = jax.ShapeDtypeStruct(blocks.shape, F32)
     parts = lax.axis_size("pairs")
     part = jax.ShapeDtypeStruct((blocks.shape[0] // parts, tile, width), F32)
-    groups = shift_groups(list(arrived), peers // 2)
+    groups = shift_groups(peers)
     total = ()
     for group in groups:
         first, last = group is groups[0], group is groups[-1]

time: 51.1 us -> 47.9 us (0.937)
  waiting for transfers between devices: 18.9 us -> 11.8 us
  starting transfers between devices: 19.3 us -> 23.7 us
  local copies, waits for them, and re-layouts: 2.78 us -> 1.36 us
  Pallas kernels: 9.03 us -> 9.99 us
    ppermute x13, waiting for transfers between devices: 18.9 us -> 11.8 us  [swap(): lax.ppermute(value, axis, [(at, at ^ shift) for at in range(lax.axis_size...]
    ppermute x13, starting transfers between devices: 19.3 us -> 23.7 us  [swap(): lax.ppermute(value, axis, [(at, at ^ shift) for at in range(lax.axis_size...]
    unnamed x10, local copies, waits for them, and re-layouts: 2.78 us -> 1.36 us
    pallas_call x4 -> x5, Pallas kernels: 6.7 us -> 7.66 us  [body(): pl.pallas_call(functools.partial(first_kernel if first else last_kernel i...]
  transfers between devices with their start and end apart: 13 -> 13, of which waited for: 7 -> 5; matrix products, arithmetic and copies ran while one was open for 0% -> 0% of each run, Pallas kernels for 14% -> 18%
where the time goes in v3:
time: 47.9 us; the launch traced here: 47.8 us
  starting transfers between devices  23.7 us (49%)
  waiting for transfers between devices  11.8 us (25%)
  Pallas kernels  9.99 us (21%)
  local copies, waits for them, and re-layouts  1.36 us (3%)
  other arithmetic  0.79 us (2%)
    ppermute x13, starting transfers between devices, swap(): lax.ppermute(value, axis, [(at, at ^ shift) for at in range(lax.axis_size...  23.7 us
    ppermute x13, waiting for transfers between devices, swap(): lax.ppermute(value, axis, [(at, at ^ shift) for at in range(lax.axis_size...  11.8 us
    pallas_call x5, Pallas kernels, body(): pl.pallas_call(functools.partial(first_kernel if first else last_kernel i...  7.66 us
    pallas_call x3, Pallas kernels, body(): pl.pallas_call(functools.partial(pack_kernel, shifts, [where.index(at) fo...  2.03 us
    unnamed x10, local copies, waits for them, and re-layouts  1.36 us
  transfers between devices with their start and end apart: 13, of which 5 were waited for; matrix products, arithmetic and copies ran while one was open for 0% of the time, Pallas kernels for 18%

profile of v3, /device:TPU:0, one launch (start us, length us, event | category | flops | bytes accessed | tf_op | source)
XLA Modules:
  0.0 47.8 jit_solution(4806123805830565756)
XLA Ops:
  0.0 0.0 copy-start.4
  0.0 0.7 %copy-done.4 = s32[1,1,8,2]{2,3,1,0:T(2,128)S(1)} copy-done((s32[1,1,8,2]{2,3,1,0:T(2,128)S(1)}, s32[1,1,8,2]{2,3,1,0:T(2,128)}, u32[]{:S(2)}) %copy-start.4) | copy-done | bytes 88
  0.7 0.0 copy-start
  0.7 0.0 copy-start.1
  0.7 0.0 copy-start.3
  0.7 4.1 %collective-permute-start = (s32[2,8]{1,0:T(2,128)S(1)}, s32[2,8]{1,0:T(2,128)S(1)}, u32[]{:S(2)}, u32[]{:S(2)}) collective-permute-start(s32[2,8]{1,0:T(2,128)S(1)} %shard_map.55.right_ref), channel_id=1, source_target_pairs={{0,16},{4,20},{8,24},{12,28},{16,0},{20,4},{24,8},{28,12},{1,17},{... | collective-permute-start | bytes 200 | tf_op jit(solution)/shard_map/ppermute | solution.py:161
  4.8 0.0 copy-start.2
  4.8 0.0 copy-done
  4.8 0.0 copy-done.1
  4.8 0.0 copy-done.3
  4.8 0.7 %copy-done.2 = s32[1,1,8,2]{2,3,1,0:T(2,128)S(1)} copy-done((s32[1,1,8,2]{2,3,1,0:T(2,128)S(1)}, s32[1,1,8,2]{2,3,1,0:T(2,128)}, u32[]{:S(2)}) %copy-start.2) | copy-done | bytes 88
  5.5 0.3 shard_map.56
  5.8 0.6 %collective-permute-done = s32[2,8]{1,0:T(2,128)S(1)} collective-permute-done((s32[2,8]{1,0:T(2,128)S(1)}, s32[2,8]{1,0:T(2,128)S(1)}, u32[]{:S(2)}, u32[]{:S(2)}) %collective-permute-start) | collective-permute-done | bytes 96 | tf_op jit(solution)/shard_map/ppermute | solution.py:161
  6.3 1.9 %collective-permute-start.1 = (s32[2,2,8]{2,1,0:T(2,128)S(1)}, s32[2,2,8]{2,1,0:T(2,128)S(1)}, u32[]{:S(2)}, u32[]{:S(2)}) collective-permute-start(s32[2,2,8]{2,1,0:T(2,128)S(1)} %pad_add_fusion.2.asked_ref), channel_id=1, source_target_pairs={{0,8},{4,12},{8,0},{12,4},{16,24},{20,28},{24,16},{28,20},{1,9},{5... | collective-permute-start | bytes 392 | tf_op jit(solution)/shard_map/ppermute | solution.py:161
  8.3 0.6 %shard_map.57 = f32[2,136,128]{2,1,0:T(8,128)S(1)} custom-call(s32[2,2,8]{2,1,0:T(2,128)S(1)} %get-tuple-element.18.ids_ref, s32[2,2,8]{2,1,0:T(2,128)S(1)} %pad_add_fusion.2.asked_ref, f32[16,128,128]{2,1,0:T(8,128)S(1)} %get-tuple-element.19.latent_ref, f32[8,2,8,128]{3,2,1,0:T(8,128)S(1)} %get-tuple-element.20.coded_ref), custom_call_target="tpu_custom_call" | custom-call | tf_op jit(solution)/shard_map/pallas_call | solution.py:209
  8.9 2.7 %collective-permute-start.3 = (f32[2,136,128]{2,1,0:T(8,128)S(1)}, f32[2,136,128]{2,1,0:T(8,128)S(1)}, u32[]{:S(2)}, u32[]{:S(2)}) collective-permute-start(f32[2,136,128]{2,1,0:T(8,128)S(1)} %shard_map.57), channel_id=1, source_target_pairs={{0,16},{4,20},{8,24},{12,28},{16,0},{20,4},{24,8},{28,12},{1,17},{... | collective-permute-start | bytes 417800 | tf_op jit(solution)/shard_map/ppermute | solution.py:161
  11.5 0.0 collective-permute-done.1
  11.5 0.7 %shard_map.59 = (f32[2,136,128]{2,1,0:T(8,128)S(1)}, f32[2,136,128]{2,1,0:T(8,128)S(1)}) custom-call(s32[2,2,8]{2,1,0:T(2,128)S(1)} %get-tuple-element.18.ids_ref, s32[4,2,8]{2,1,0:T(2,128)S(1)} %pad_add_fusion.1.asked_ref, f32[16,128,128]{2,1,0:T(8,128)S(1)} %get-tuple-element.19.latent_ref, f32[8,2,8,128]{3,2,1,0:T(8,128)S(1)} %get-tuple-element.20.coded_ref), custom_call_target="tpu_custom_call" | custom-call | tf_op jit(solution)/shard_map/pallas_call | solution.py:209
  12.2 2.6 %collective-permute-start.4 = (f32[2,136,128]{2,1,0:T(8,128)S(1)}, f32[2,136,128]{2,1,0:T(8,128)S(1)}, u32[]{:S(2)}, u32[]{:S(2)}) collective-permute-start(f32[2,136,128]{2,1,0:T(8,128)S(1)} %get-tuple-element.21), channel_id=1, source_target_pairs={{0,24},{4,28},{8,16},{12,20},{16,8},{20,12},{24,0},{28,4},{1,25},{... | collective-permute-start | bytes 417800 | tf_op jit(solution)/shard_map/ppermute | solution.py:161
  14.8 1.5 %collective-permute-start.2 = (s32[4,2,8]{2,1,0:T(2,128)S(1)}, s32[4,2,8]{2,1,0:T(2,128)S(1)}, u32[]{:S(2)}, u32[]{:S(2)}) collective-permute-start(s32[4,2,8]{2,1,0:T(2,128)S(1)} %pad_add_fusion.1.asked_ref), channel_id=1, source_target_pairs={{0,4},{4,0},{8,12},{12,8},{16,20},{20,16},{24,28},{28,24},{1,5},{5... | collective-permute-start | bytes 776 | tf_op jit(solution)/shard_map/ppermute | solution.py:161
  16.3 0.0 collective-permute-start.5
  16.3 2.1 %collective-permute-done.2 = s32[4,2,8]{2,1,0:T(2,128)S(1)} collective-permute-done((s32[4,2,8]{2,1,0:T(2,128)S(1)}, s32[4,2,8]{2,1,0:T(2,128)S(1)}, u32[]{:S(2)}, u32[]{:S(2)}) %collective-permute-start.2) | collective-permute-done | bytes 288 | tf_op jit(solution)/shard_map/ppermute | solution.py:161
  18.5 0.7 %shard_map.61 = (f32[2,136,128]{2,1,0:T(8,128)S(1)}, f32[2,136,128]{2,1,0:T(8,128)S(1)}, f32[2,136,128]{2,1,0:T(8,128)S(1)}, f32[2,136,128]{2,1,0:T(8,128)S(1)}) custom-call(s32[2,2,8]{2,1,0:T(2,128)S(1)} %get-tuple-element.18.ids_ref, s32[8,2,8]{2,1,0:T(2,128)S(1)} %pad_add_fusion.asked_ref, f32[16,128,128]{2,1,0:T(8,128)S(1)} %get-tuple-element.19.latent_ref, ...), custom_call_target="tpu_custom_call" | custom-call | tf_op jit(solution)/shard_map/pallas_call | solution.py:209
  19.2 0.4 collective-permute-start.6
  19.6 1.3 %collective-permute-start.7 = (f32[2,136,128]{2,1,0:T(8,128)S(1)}, f32[2,136,128]{2,1,0:T(8,128)S(1)}, u32[]{:S(2)}, u32[]{:S(2)}) collective-permute-start(f32[2,136,128]{2,1,0:T(8,128)S(1)} %get-tuple-element.24), channel_id=1, source_target_pairs={{0,4},{4,0},{8,12},{12,8},{16,20},{20,16},{24,28},{28,24},{1,5},{5... | collective-permute-start | bytes 417800 | tf_op jit(solution)/shard_map/ppermute | solution.py:161
  20.8 0.0 collective-permute-done.3.refs_0_
  20.9 3.6 %collective-permute-start.8 = (f32[2,136,128]{2,1,0:T(8,128)S(1)}, f32[2,136,128]{2,1,0:T(8,128)S(1)}, u32[]{:S(2)}, u32[]{:S(2)}) collective-permute-start(f32[2,136,128]{2,1,0:T(8,128)S(1)} %get-tuple-element.25), channel_id=1, source_target_pairs={{0,28},{4,24},{8,20},{12,16},{16,12},{20,8},{24,4},{28,0},{1,29},{... | collective-permute-start | bytes 417800 | tf_op jit(solution)/shard_map/ppermute | solution.py:161
  24.4 0.0 collective-permute-done.4.refs_0_
  24.4 3.7 %collective-permute-start.9 = (f32[2,136,128]{2,1,0:T(8,128)S(1)}, f32[2,136,128]{2,1,0:T(8,128)S(1)}, u32[]{:S(2)}, u32[]{:S(2)}) collective-permute-start(f32[2,136,128]{2,1,0:T(8,128)S(1)} %get-tuple-element.26), channel_id=1, source_target_pairs={{0,20},{4,16},{8,28},{12,24},{16,4},{20,0},{24,12},{28,8},{1,21},{... | collective-permute-start | bytes 417800 | tf_op jit(solution)/shard_map/ppermute | solution.py:161
  28.1 1.5 %shard_map.58.before_ref = f32[16,128,128]{2,1,0:T(8,128)S(1)} custom-call(s32[2,2,8]{2,1,0:T(2,128)S(1)} %get-tuple-element.18.ids_ref, s32[8,2,8]{2,1,0:T(2,128)S(1)} %pad_add_fusion.asked_ref, f32[16,128,128]{2,1,0:T(8,128)S(1)} %get-tuple-element.19.latent_ref, f32[8,2,8,128]{3,2,1,0:T(8,128)S(1)} %get-tuple-element.20.coded_ref, ...), custom_call_target="tpu_custom_call" | custom-call | flops 50331648 | bytes 3145728 | tf_op jit(solution)/shard_map/pallas_call | solution.py:227
  29.6 0.0 collective-permute-done.5.refs_1_
  29.6 1.8 %shard_map.60.before_ref = f32[16,128,128]{2,1,0:T(8,128)S(1)} custom-call(s32[2,2,8]{2,1,0:T(2,128)S(1)} %get-tuple-element.18.ids_ref, s32[8,2,8]{2,1,0:T(2,128)S(1)} %pad_add_fusion.asked_ref, f32[16,128,128]{2,1,0:T(8,128)S(1)} %get-tuple-element.19.latent_ref, f32[8,2,8,128]{3,2,1,0:T(8,128)S(1)} %get-tuple-element.20.coded_ref, ...), custom_call_target="tpu_custom_call", output_to_operand_aliasing={{}: (4, {})} | custom-call | flops 100663296 | bytes 3145728 | tf_op jit(solution)/shard_map/pallas_call | solution.py:227
  31.3 0.0 collective-permute-done.6.refs_0_
  31.3 0.0 collective-permute-done.7.refs_1_
  31.4 1.8 %shard_map.62.before_ref = f32[16,128,128]{2,1,0:T(8,128)S(1)} custom-call(s32[2,2,8]{2,1,0:T(2,128)S(1)} %get-tuple-element.18.ids_ref, s32[8,2,8]{2,1,0:T(2,128)S(1)} %pad_add_fusion.asked_ref, f32[16,128,128]{2,1,0:T(8,128)S(1)} %get-tuple-element.19.latent_ref, f32[8,2,8,128]{3,2,1,0:T(8,128)S(1)} %get-tuple-element.20.coded_ref, ...), custom_call_target="tpu_custom_call", output_to_operand_aliasing={{}: (4, {})} | custom-call | flops 100663296 | bytes 3145728 | tf_op jit(solution)/shard_map/pallas_call | solution.py:227
  33.1 0.0 collective-permute-done.8.refs_0_
  33.1 1.3 %shard_map.63.before_ref = f32[16,128,128]{2,1,0:T(8,128)S(1)} custom-call(s32[2,2,8]{2,1,0:T(2,128)S(1)} %get-tuple-element.18.ids_ref, s32[8,2,8]{2,1,0:T(2,128)S(1)} %pad_add_fusion.asked_ref, f32[16,128,128]{2,1,0:T(8,128)S(1)} %get-tuple-element.19.latent_ref, f32[8,2,8,128]{3,2,1,0:T(8,128)S(1)} %get-tuple-element.20.coded_ref, ...), custom_call_target="tpu_custom_call", output_to_operand_aliasing={{}: (4, {})} | custom-call | flops 50331648 | bytes 3145728 | tf_op jit(solution)/shard_map/pallas_call | solution.py:227
  34.5 1.2 %collective-permute-done.9.refs_0_ = f32[2,136,128]{2,1,0:T(8,128)S(1)} collective-permute-done((f32[2,136,128]{2,1,0:T(8,128)S(1)}, f32[2,136,128]{2,1,0:T(8,128)S(1)}, u32[]{:S(2)}, u32[]{:S(2)}) %collective-permute-start.9) | collective-permute-done | bytes 139296 | tf_op jit(solution)/shard_map/ppermute | solution.py:161
  35.7 1.3 %shard_map.64 = (f32[4,128,128]{2,1,0:T(8,128)S(1)}, f32[4,128,128]{2,1,0:T(8,128)S(1)}, f32[4,128,128]{2,1,0:T(8,128)S(1)}, f32[4,128,128]{2,1,0:T(8,128)S(1)}) custom-call(s32[2,2,8]{2,1,0:T(2,128)S(1)} %get-tuple-element.18.ids_ref, s32[8,2,8]{2,1,0:T(2,128)S(1)} %pad_add_fusion.asked_ref, f32[16,128,128]{2,1,0:T(8,128)S(1)} %get-tuple-element.19.latent_ref, ...), custom_call_target="tpu_custom_call" | custom-call | flops 50331648 | bytes 3145728 | tf_op jit(solution)/shard_map/pallas_call | solution.py:227
  37.0 0.1 collective-permute-start.11
  37.1 0.5 %collective-permute-start.10 = (f32[4,128,128]{2,1,0:T(8,128)S(1)}, f32[4,128,128]{2,1,0:T(8,128)S(1)}, u32[]{:S(2)}, u32[]{:S(2)}) collective-permute-start(f32[4,128,128]{2,1,0:T(8,128)S(1)} %get-tuple-element.28), channel_id=1, source_target_pairs={{0,1},{1,0},{2,3},{3,2},{4,5},{5,4},{6,7},{7,6},{8,9},{9,8},{10,11... | collective-permute-start | bytes 786440 | tf_op jit(solution)/shard_map/ppermute | solution.py:161
  37.6 1.0 %collective-permute-done.11 = f32[4,128,128]{2,1,0:T(8,128)S(1)} collective-permute-done((f32[4,128,128]{2,1,0:T(8,128)S(1)}, f32[4,128,128]{2,1,0:T(8,128)S(1)}, u32[]{:S(2)}, u32[]{:S(2)}) %collective-permute-start.11) | collective-permute-done | bytes 262176 | tf_op jit(solution)/shard_map/ppermute | solution.py:161
  38.6 1.6 %collective-permute-start.12 = (f32[4,128,128]{2,1,0:T(8,128)S(1)}, f32[4,128,128]{2,1,0:T(8,128)S(1)}, u32[]{:S(2)}, u32[]{:S(2)}) collective-permute-start(f32[4,128,128]{2,1,0:T(8,128)S(1)} %add.10), channel_id=1, source_target_pairs={{0,2},{1,3},{2,0},{3,1},{4,6},{5,7},{6,4},{7,5},{8,10},{9,11},{10,... | collective-permute-start | bytes 786440 | tf_op jit(solution)/shard_map/ppermute | solution.py:161
  40.2 0.0 collective-permute-done.10
  40.2 6.9 %collective-permute-done.12 = f32[4,128,128]{2,1,0:T(8,128)S(1)} collective-permute-done((f32[4,128,128]{2,1,0:T(8,128)S(1)}, f32[4,128,128]{2,1,0:T(8,128)S(1)}, u32[]{:S(2)}, u32[]{:S(2)}) %collective-permute-start.12) | collective-permute-done | bytes 262176 | tf_op jit(solution)/shard_map/ppermute | solution.py:161
  47.0 0.7 %add_add_fusion = f32[4,128,128]{2,1,0:T(8,128)} fusion(f32[4,128,128]{2,1,0:T(8,128)S(1)} %collective-permute-done.12, f32[4,128,128]{2,1,0:T(8,128)S(1)} %get-tuple-element.27, f32[4,128,128]{2,1,0:T(8,128)S(1)} %collective-permute-done.10), kind=kLoop, calls=%fused_computation | loop fusion | flops 131072 | bytes 1048576 | tf_op jit(solution)/shard_map/add | solution.py:244
  (6 shorter events, 0.0 us)
Async XLA Ops:
  0.0 0.7 %copy-start.4 = (s32[1,1,8,2]{2,3,1,0:T(2,128)S(1)}, s32[1,1,8,2]{2,3,1,0:T(2,128)}, u32[]{:S(2)}) copy-start(s32[1,1,8,2]{2,3,1,0:T(2,128)} %param.7) | copy-start | bytes 196
  0.7 4.1 %copy-start = (f32[2048,128]{1,0:T(8,128)S(1)}, f32[2048,128]{1,0:T(8,128)}, u32[]{:S(2)}) copy-start(f32[2048,128]{1,0:T(8,128)} %param.5) | copy-start | bytes 3145732
  0.7 4.1 %copy-start.1 = (s32[1,1,8,2,8,128]{5,4,3,2,1,0:T(8,128)S(1)}, s32[1,1,8,2,8,128]{5,4,3,2,1,0:T(8,128)}, u32[]{:S(2)}) copy-start(s32[1,1,8,2,8,128]{5,4,3,2,1,0:T(8,128)} %param.9) | copy-start | bytes 196612
  0.7 4.1 %copy-start.3 = (s32[1,1,8,2]{2,3,1,0:T(2,128)S(1)}, s32[1,1,8,2]{2,3,1,0:T(2,128)}, u32[]{:S(2)}) copy-start(s32[1,1,8,2]{2,3,1,0:T(2,128)} %param.8) | copy-start | bytes 196
  0.7 5.7 %collective-permute-start = (s32[2,8]{1,0:T(2,128)S(1)}, s32[2,8]{1,0:T(2,128)S(1)}, u32[]{:S(2)}, u32[]{:S(2)}) collective-permute-start(s32[2,8]{1,0:T(2,128)S(1)} %shard_map.55.right_ref), channel_id=1, source_target_pairs={{0,16},{4,20},{8,24},{12,28},{16,0},{20,4},{24,8},{28,12},{1,17},{... | collective-permute-start | bytes 200 | tf_op jit(solution)/shard_map/ppermute | solution.py:161
  4.8 0.7 %copy-start.2 = (s32[1,1,8,2]{2,3,1,0:T(2,128)S(1)}, s32[1,1,8,2]{2,3,1,0:T(2,128)}, u32[]{:S(2)}) copy-start(s32[1,1,8,2]{2,3,1,0:T(2,128)} %param.6) | copy-start | bytes 196
  6.3 5.2 %collective-permute-start.1 = (s32[2,2,8]{2,1,0:T(2,128)S(1)}, s32[2,2,8]{2,1,0:T(2,128)S(1)}, u32[]{:S(2)}, u32[]{:S(2)}) collective-permute-start(s32[2,2,8]{2,1,0:T(2,128)S(1)} %pad_add_fusion.2.asked_ref), channel_id=1, source_target_pairs={{0,8},{4,12},{8,0},{12,4},{16,24},{20,28},{24,16},{28,20},{1,9},{5... | collective-permute-start | bytes 392 | tf_op jit(solution)/shard_map/ppermute | solution.py:161
  8.9 12.0 %collective-permute-start.3 = (f32[2,136,128]{2,1,0:T(8,128)S(1)}, f32[2,136,128]{2,1,0:T(8,128)S(1)}, u32[]{:S(2)}, u32[]{:S(2)}) collective-permute-start(f32[2,136,128]{2,1,0:T(8,128)S(1)} %shard_map.57), channel_id=1, source_target_pairs={{0,16},{4,20},{8,24},{12,28},{16,0},{20,4},{24,8},{28,12},{1,17},{... | collective-permute-start | bytes 417800 | tf_op jit(solution)/shard_map/ppermute | solution.py:161
  12.2 12.2 %collective-permute-start.4 = (f32[2,136,128]{2,1,0:T(8,128)S(1)}, f32[2,136,128]{2,1,0:T(8,128)S(1)}, u32[]{:S(2)}, u32[]{:S(2)}) collective-permute-start(f32[2,136,128]{2,1,0:T(8,128)S(1)} %get-tuple-element.21), channel_id=1, source_target_pairs={{0,24},{4,28},{8,16},{12,20},{16,8},{20,12},{24,0},{28,4},{1,25},{... | collective-permute-start | bytes 417800 | tf_op jit(solution)/shard_map/ppermute | solution.py:161
  14.8 3.6 %collective-permute-start.2 = (s32[4,2,8]{2,1,0:T(2,128)S(1)}, s32[4,2,8]{2,1,0:T(2,128)S(1)}, u32[]{:S(2)}, u32[]{:S(2)}) collective-permute-start(s32[4,2,8]{2,1,0:T(2,128)S(1)} %pad_add_fusion.1.asked_ref), channel_id=1, source_target_pairs={{0,4},{4,0},{8,12},{12,8},{16,20},{20,16},{24,28},{28,24},{1,5},{5... | collective-permute-start | bytes 776 | tf_op jit(solution)/shard_map/ppermute | solution.py:161
  16.3 13.2 %collective-permute-start.5 = (f32[2,136,128]{2,1,0:T(8,128)S(1)}, f32[2,136,128]{2,1,0:T(8,128)S(1)}, u32[]{:S(2)}, u32[]{:S(2)}) collective-permute-start(f32[2,136,128]{2,1,0:T(8,128)S(1)} %get-tuple-element.22), channel_id=1, source_target_pairs={{0,8},{4,12},{8,0},{12,4},{16,24},{20,28},{24,16},{28,20},{1,9},{5... | collective-permute-start | bytes 417800 | tf_op jit(solution)/shard_map/ppermute | solution.py:161
  19.2 12.1 %collective-permute-start.6 = (f32[2,136,128]{2,1,0:T(8,128)S(1)}, f32[2,136,128]{2,1,0:T(8,128)S(1)}, u32[]{:S(2)}, u32[]{:S(2)}) collective-permute-start(f32[2,136,128]{2,1,0:T(8,128)S(1)} %get-tuple-element.23), channel_id=1, source_target_pairs={{0,12},{4,8},{8,4},{12,0},{16,28},{20,24},{24,20},{28,16},{1,13},{... | collective-permute-start | bytes 417800 | tf_op jit(solution)/shard_map/ppermute | solution.py:161
  19.6 11.8 %collective-permute-start.7 = (f32[2,136,128]{2,1,0:T(8,128)S(1)}, f32[2,136,128]{2,1,0:T(8,128)S(1)}, u32[]{:S(2)}, u32[]{:S(2)}) collective-permute-start(f32[2,136,128]{2,1,0:T(8,128)S(1)} %get-tuple-element.24), channel_id=1, source_target_pairs={{0,4},{4,0},{8,12},{12,8},{16,20},{20,16},{24,28},{28,24},{1,5},{5... | collective-permute-start | bytes 417800 | tf_op jit(solution)/shard_map/ppermute | solution.py:161
  20.9 12.3 %collective-permute-start.8 = (f32[2,136,128]{2,1,0:T(8,128)S(1)}, f32[2,136,128]{2,1,0:T(8,128)S(1)}, u32[]{:S(2)}, u32[]{:S(2)}) collective-permute-start(f32[2,136,128]{2,1,0:T(8,128)S(1)} %get-tuple-element.25), channel_id=1, source_target_pairs={{0,28},{4,24},{8,20},{12,16},{16,12},{20,8},{24,4},{28,0},{1,29},{... | collective-permute-start | bytes 417800 | tf_op jit(solution)/shard_map/ppermute | solution.py:161
  24.4 11.3 %collective-permute-start.9 = (f32[2,136,128]{2,1,0:T(8,128)S(1)}, f32[2,136,128]{2,1,0:T(8,128)S(1)}, u32[]{:S(2)}, u32[]{:S(2)}) collective-permute-start(f32[2,136,128]{2,1,0:T(8,128)S(1)} %get-tuple-element.26), channel_id=1, source_target_pairs={{0,20},{4,16},{8,28},{12,24},{16,4},{20,0},{24,12},{28,8},{1,21},{... | collective-permute-start | bytes 417800 | tf_op jit(solution)/shard_map/ppermute | solution.py:161
  37.0 1.6 %collective-permute-start.11 = (f32[4,128,128]{2,1,0:T(8,128)S(1)}, f32[4,128,128]{2,1,0:T(8,128)S(1)}, u32[]{:S(2)}, u32[]{:S(2)}) collective-permute-start(f32[4,128,128]{2,1,0:T(8,128)S(1)} %get-tuple-element.30), channel_id=1, source_target_pairs={{0,1},{1,0},{2,3},{3,2},{4,5},{5,4},{6,7},{7,6},{8,9},{9,8},{10,11... | collective-permute-start | bytes 786440 | tf_op jit(solution)/shard_map/ppermute | solution.py:161
  37.1 3.1 %collective-permute-start.10 = (f32[4,128,128]{2,1,0:T(8,128)S(1)}, f32[4,128,128]{2,1,0:T(8,128)S(1)}, u32[]{:S(2)}, u32[]{:S(2)}) collective-permute-start(f32[4,128,128]{2,1,0:T(8,128)S(1)} %get-tuple-element.28), channel_id=1, source_target_pairs={{0,1},{1,0},{2,3},{3,2},{4,5},{5,4},{6,7},{7,6},{8,9},{9,8},{10,11... | collective-permute-start | bytes 786440 | tf_op jit(solution)/shard_map/ppermute | solution.py:161
  38.6 8.4 %collective-permute-start.12 = (f32[4,128,128]{2,1,0:T(8,128)S(1)}, f32[4,128,128]{2,1,0:T(8,128)S(1)}, u32[]{:S(2)}, u32[]{:S(2)}) collective-permute-start(f32[4,128,128]{2,1,0:T(8,128)S(1)} %add.10), channel_id=1, source_target_pairs={{0,2},{1,3},{2,0},{3,1},{4,6},{5,7},{6,4},{7,5},{8,10},{9,11},{10,... | collective-permute-start | bytes 786440 | tf_op jit(solution)/shard_map/ppermute | solution.py:161

commit v4 on v3

--- a/solution.py
+++ b/solution.py
@@ -45,63 +45,74 @@
     return jnp.where(peer > me, ids_ref[0, slot, peer], asked_ref[place, slot, me])
 
 
-def pack_kernel(shifts, places, ids_ref, asked_ref, latent_ref, coded_ref, *message_refs):
+def pack_kernel(shifts, places, ids_ref, asked_ref, latent_ref, coded_ref, passed_ref, *message_refs):
     me = lax.axis_index("rows")
     tile = latent_ref.shape[1]
+    top, _, lists, _ = passed_ref.shape
     for shift, place, message_ref in zip(shifts, places, message_refs):
         peer = me ^ shift
         for slot in range(message_ref.shape[0]):
             block = own_id(ids_ref, asked_ref, place, me, peer, slot)
             message_ref[slot, :tile] = latent_ref[block]
-            message_ref[slot, tile:] = coded_ref[peer, slot]
-
-
-def add_peer(shift, place, total_ref, ids_ref, asked_ref, latent_ref, coded_ref, message_ref):
+            if shift < top:
+                message_ref[slot, tile : tile + lists] = coded_ref[peer, slot]
+                message_ref[slot, tile + lists :] = passed_ref[lax.rem(peer, top), slot]
+
+
+def sent_edges(shift, coded_ref, carrier_ref, me, slot):
+    _, _, lists, tile = coded_ref.shape
+    top = coded_ref.shape[0] // 2
+    if shift == top:
+        return carrier_ref[lax.rem(me, top), slot]
+    start = tile if shift < top else tile + lists
+    return carrier_ref[slot, start : start + lists]
+
+
+def slot_target(shift, coded_ref, carrier_ref, slot):
     me = lax.axis_index("rows")
     peer = me ^ shift
     low = peer > me
+    target = natural_target(jnp.where(low, coded_ref[peer, slot], sent_edges(shift, coded_ref, carrier_ref, me, slot)))
+    return jnp.where(low, target.T, target)
+
+
+def add_peer(shift, place, total_ref, ids_ref, asked_ref, latent_ref, coded_ref, message_ref, carrier_ref):
+    me = lax.axis_index("rows")
+    peer = me ^ shift
     quarter = lax.axis_index("pairs") * (total_ref.shape[0] // lax.axis_size("pairs"))
     tile = latent_ref.shape[1]
     for slot in range(message_ref.shape[0]):
         block = own_id(ids_ref, asked_ref, place, me, peer, slot)
         own = halves(latent_ref[block])
         other = halves(message_ref[slot, :tile])
-        edges = jnp.where(low, coded_ref[peer, slot], message_ref[slot, tile:])
-        target = natural_target(edges)
-        target = jnp.where(low, target.T, target)
+        target = slot_target(shift, coded_ref, carrier_ref, slot)
         residue = jax.nn.sigmoid(product(own, other, 1, 1)) - target
         total_ref[block ^ quarter] += product(halves(residue), other, 1, 0)
 
 
-def copy_kernel(source_ref, target_ref):
-    target_ref[...] = source_ref[...]
-
-
-def setup_kernel(latent_ref, left_ref, right_ref, kind_ref, edges_ref, rows_ref, ids_ref, coded_ref, kinds_ref, ints_ref, sems):
+def tables_kernel(left_ref, right_ref, kind_ref, asked_ref, ids_ref, kinds_ref):
+    asked_ref[...] = right_ref[...]
+    ids_ref[0] = left_ref[...]
+    ids_ref[1] = right_ref[...]
+    kinds_ref[...] = kind_ref[...]
+
+
+def setup_kernel(kinds_ref, latent_ref, edges_ref, rows_ref, coded_ref, far_ref, ints_ref, sems):
     copies = [
         pltpu.make_async_copy(source, target, sems.at[at])
-        for at, (source, target) in enumerate(
-            (
-                (kind_ref, kinds_ref),
-                (edges_ref, ints_ref),
-                (left_ref, ids_ref.at[0]),
-                (right_ref, ids_ref.at[1]),
-                (latent_ref, rows_ref),
-            )
-        )
+        for at, (source, target) in enumerate(((edges_ref, ints_ref), (latent_ref, rows_ref)))
     ]
     for copy in copies:
         copy.start()
-    for copy in copies[:2]:
-        copy.wait()
+    copies[0].wait()
     peers, slots = edges_ref.shape[:2]
     for peer in range(peers):
         for slot in range(slots):
             edges = ints_ref[peer, slot].astype(F32)
             kind = jnp.broadcast_to(kinds_ref[slot : slot + 1, peer : peer + 1], edges.shape)
             coded_ref[peer, slot] = jnp.where(kind == 2, edges, -1.0)
-    for copy in copies[2:]:
-        copy.wait()
+    far_ref[...] = coded_ref[far_ref.shape[0] :]
+    copies[1].wait()
 
 
 def add_own(total_ref, ids_ref, latent_ref, coded_ref):
@@ -116,27 +127,32 @@
         total_ref[right_block ^ quarter] += product(residue, left, 1, 0)
 
 
-def first_kernel(shifts, places, ids_ref, asked_ref, latent_ref, coded_ref, *refs):
-    *message_refs, total_ref = refs
+def add_peers(shifts, places, total_ref, *refs):
+    fixed, refs = refs[:4], refs[4:]
+    count = len(shifts)
+    for shift, place, message_ref, carrier_ref in zip(shifts, places, refs[:count], refs[count:]):
+        add_peer(shift, place, total_ref, *fixed, message_ref, carrier_ref)
+
+
+def first_kernel(shifts, places, *refs):
+    *refs, total_ref = refs
+    ids_ref, _, latent_ref, coded_ref = refs[:4]
     total_ref[...] = jnp.zeros_like(total_ref)
     add_own(total_ref, ids_ref, latent_ref, coded_ref)
-    for shift, place, message_ref in zip(shifts, places, message_refs):
-        add_peer(shift, place, total_ref, ids_ref, asked_ref, latent_ref, coded_ref, message_ref)
-
-
-def middle_kernel(shifts, places, ids_ref, asked_ref, latent_ref, coded_ref, before_ref, *refs):
-    *message_refs, total_ref = refs
+    add_peers(shifts, places, total_ref, *refs)
+
+
+def middle_kernel(shifts, places, before_ref, *refs):
+    *refs, total_ref = refs
     total_ref[...] = before_ref[...]
-    for shift, place, message_ref in zip(shifts, places, message_refs):
-        add_peer(shift, place, total_ref, ids_ref, asked_ref, latent_ref, coded_ref, message_ref)
-
-
-def last_kernel(shifts, places, ids_ref, asked_ref, latent_ref, coded_ref, before_ref, *refs):
-    count = len(shifts)
-    message_refs, part_refs, total_ref = refs[:count], refs[count:-1], refs[-1]
+    add_peers(shifts, places, total_ref, *refs)
+
+
+def last_kernel(shifts, places, before_ref, *refs):
+    count = 4 + 2 * len(shifts)
+    refs, part_refs, total_ref = refs[:count], refs[count:-1], refs[-1]
     total_ref[...] = before_ref[...]
-    for shift, place, message_ref in zip(shifts, places, message_refs):
-        add_peer(shift, place, total_ref, ids_ref, asked_ref, latent_ref, coded_ref, message_ref)
+    add_peers(shifts, places, total_ref, *refs)
     for place, part_ref in enumerate(part_refs):
         depth = part_ref.shape[0]
         part_ref[...] = total_ref[place * depth : (place + 1) * depth]
@@ -171,34 +187,37 @@
         return value.reshape(peers, slots).T
 
     edges = edge_cols.reshape(peers, slots, lists, tile)
-    own_asked = pl.pallas_call(
-        copy_kernel,
-        out_shape=jax.ShapeDtypeStruct((slots, peers), jnp.int32),
-        in_specs=[VMEM],
-        out_specs=VMEM,
+    top = peers // 2
+    small = jax.ShapeDtypeStruct((slots, peers), jnp.int32)
+    own_asked, ids, kinds = pl.pallas_call(
+        tables_kernel,
+        out_shape=(small, jax.ShapeDtypeStruct((2, slots, peers), jnp.int32), small),
+        in_specs=[VMEM] * 3,
+        out_specs=(VMEM,) * 3,
         compiler_params=PARAMS,
         cost_estimate=pl.CostEstimate(flops=WAIT_FLOPS, bytes_accessed=4096, transcendentals=0),
-    )(table(right_block))
-    blocks, ids, coded = pl.pallas_call(
+    )(table(left_block), table(right_block), table(slot_kind))
+    blocks, coded, far_coded = pl.pallas_call(
         setup_kernel,
         out_shape=(
             jax.ShapeDtypeStruct(blocks.shape, F32),
-            jax.ShapeDtypeStruct((2, slots, peers), jnp.int32),
             jax.ShapeDtypeStruct(edges.shape, F32),
+            jax.ShapeDtypeStruct((top, *edges.shape[1:]), F32),
         ),
-        in_specs=[HBM] * 5,
+        in_specs=[VMEM] + [HBM] * 2,
         out_specs=(VMEM,) * 3,
         scratch_shapes=[
-            pltpu.VMEM((slots, peers), jnp.int32),
             pltpu.VMEM(edges.shape, jnp.int32),
-            pltpu.SemaphoreType.DMA((5,)),
+            pltpu.SemaphoreType.DMA((2,)),
         ],
         compiler_params=PARAMS,
-    )(blocks, table(left_block), own_asked, table(slot_kind), edges)
-
-    message = jax.ShapeDtypeStruct((slots, tile + lists, width), F32)
+    )(kinds, blocks, edges)
+
+    passed = swap(far_coded, "rows", top)
+    near_message = jax.ShapeDtypeStruct((slots, tile + 2 * lists, width), F32)
+    far_message = jax.ShapeDtypeStruct((slots, tile, width), F32)
     asked, where, arrived = own_asked, [0], {}
-    bit = peers // 2
+    bit = top
     while bit:
         if len(where) == 1:
             asked = jnp.concatenate([ids[1:], swap(asked, "rows", bit)[None]])
@@ -208,11 +227,11 @@
         shifts = [at for at in reversed(range(1, peers)) if at & -at == bit]
         sent = pl.pallas_call(
             functools.partial(pack_kernel, shifts, [where.index(at) for at in shifts]),
-            out_shape=[message] * len(shifts),
-            in_specs=[SMEM] * 2 + [VMEM] * 2,
+            out_shape=[far_message if at >= top else near_message for at in shifts],
+            in_specs=[SMEM] * 2 + [VMEM] * 3,
             out_specs=[VMEM] * len(shifts),
             compiler_params=PARAMS,
-        )(ids, asked, blocks, coded)
+        )(ids, asked, blocks, coded, passed if bit < top else coded[:top])
         for shift, value in zip(shifts, sent):
             arrived[shift] = swap(value, "rows", shift)
         bit //= 2
@@ -221,6 +240,7 @@
     parts = lax.axis_size("pairs")
     part = jax.ShapeDtypeStruct((blocks.shape[0] // parts, tile, width), F32)
     groups = shift_groups(peers)
+    carrier = {at: passed if at == top else arrived[at % top] for at in arrived}
     total = ()
     for group in groups:
         first, last = group is groups[0], group is groups[-1]
@@ -231,13 +251,13 @@
                 [where.index(at) for at in group],
             ),
             out_shape=[part] * parts if last else [whole],
-            in_specs=[SMEM] * 2 + [VMEM] * (2 + len(total) + len(group)),
+            in_specs=[VMEM] * len(total) + [SMEM] * 2 + [VMEM] * (2 + 2 * len(group)),
             out_specs=[VMEM] * (parts if last else 1),
             scratch_shapes=[pltpu.VMEM(blocks.shape, F32)] if last else [],
-            input_output_aliases={} if first or last else {4: 0},
+            input_output_aliases={} if first or last else {0: 0},
             compiler_params=PARAMS,
             cost_estimate=estimate(slots * len(group), tile, 3 * blocks.size * 4),
-        )(ids, asked, blocks, coded, *total, *[arrived[at] for at in group])
+        )(*total, ids, asked, blocks, coded, *[arrived[at] for at in group], *[carrier[at] for at in group])
     held = total
     far_half = held[2] + swap(held[3], "pairs", 1)
     kept = swap(held[1], "pairs", 1)

time: 47.9 us -> 47.1 us (0.983)
  waiting for transfers between devices: 11.8 us -> 9.3 us
  starting transfers between devices: 23.7 us -> 26 us
  local copies, waits for them, and re-layouts: 1.36 us -> 0.72 us
    ppermute x13 -> x14, waiting for transfers between devices: 11.8 us -> 9.3 us  [swap(): lax.ppermute(value, axis, [(at, at ^ shift) for at in range(lax.axis_size...]
    ppermute x13 -> x14, starting transfers between devices: 23.7 us -> 26 us  [swap(): lax.ppermute(value, axis, [(at, at ^ shift) for at in range(lax.axis_size...]
    unnamed x10, local copies, waits for them, and re-layouts: 1.36 us -> 0.72 us
  transfers between devices with their start and end apart: 13 -> 14, of which waited for: 5 -> 4; matrix products, arithmetic and copies ran while one was open for 0% -> 0% of each run, Pallas kernels for 18% -> 18%
where the time goes in v4:
time: 47.1 us; the launch traced here: 46.9 us
  starting transfers between devices  26 us (55%)
  Pallas kernels  9.97 us (21%)
  waiting for transfers between devices  9.3 us (20%)
  other arithmetic  0.8 us (2%)
  local copies, waits for them, and re-layouts  0.72 us (2%)
    ppermute x14, starting transfers between devices, swap(): lax.ppermute(value, axis, [(at, at ^ shift) for at in range(lax.axis_size...  26 us
    ppermute x14, waiting for transfers between devices, swap(): lax.ppermute(value, axis, [(at, at ^ shift) for at in range(lax.axis_size...  9.3 us
    pallas_call x5, Pallas kernels, body(): pl.pallas_call(functools.partial(first_kernel if first else last_kernel i...  7.66 us
    pallas_call x3, Pallas kernels, body(): pl.pallas_call(functools.partial(pack_kernel, shifts, [where.index(at) fo...  2.03 us
  transfers between devices with their start and end apart: 14, of which 4 were waited for; matrix products, arithmetic and copies ran while one was open for 0% of the time, Pallas kernels for 18%

profile of v4, /device:TPU:0, one launch (start us, length us, event | category | flops | bytes accessed | tf_op | source)
XLA Modules:
  0.0 46.9 jit_solution(3171756259424969856)
XLA Ops:
  0.0 0.0 copy-start.3
  0.0 0.0 copy-start.4
  0.0 0.0 copy-start.2
  0.0 0.7 %copy-done.3 = s32[1,1,8,2]{2,3,1,0:T(2,128)S(1)} copy-done((s32[1,1,8,2]{2,3,1,0:T(2,128)S(1)}, s32[1,1,8,2]{2,3,1,0:T(2,128)}, u32[]{:S(2)}) %copy-start.3) | copy-done | bytes 88
  0.7 0.0 copy-done.4
  0.7 0.0 copy-done.2
  0.7 0.0 copy-start
  0.7 0.0 copy-start.1
  0.7 4.1 %collective-permute-start = (s32[2,8]{1,0:T(2,128)S(1)}, s32[2,8]{1,0:T(2,128)S(1)}, u32[]{:S(2)}, u32[]{:S(2)}) collective-permute-start(s32[2,8]{1,0:T(2,128)S(1)} %get-tuple-element.22), channel_id=1, source_target_pairs={{0,16},{4,20},{8,24},{12,28},{16,0},{20,4},{24,8},{28,12},{1,17},{... | collective-permute-start | bytes 200 | tf_op jit(solution)/shard_map/ppermute | solution.py:177
  4.8 0.0 copy-done
  4.8 0.0 copy-done.1
  4.8 0.3 shard_map.56
  5.1 1.2 %collective-permute-start.4 = (f32[4,2,8,128]{3,2,1,0:T(8,128)S(1)}, f32[4,2,8,128]{3,2,1,0:T(8,128)S(1)}, u32[]{:S(2)}, u32[]{:S(2)}) collective-permute-start(f32[4,2,8,128]{3,2,1,0:T(8,128)S(1)} %get-tuple-element.26), channel_id=1, source_target_pairs={{0,16},{4,20},{8,24},{12,28},{16,0},{20,4},{24,8},{28,12},{1,17},{... | collective-permute-start | bytes 98312 | tf_op jit(solution)/shard_map/ppermute | solution.py:177
  6.3 0.0 collective-permute-done
  6.4 1.9 %collective-permute-start.1 = (s32[2,2,8]{2,1,0:T(2,128)S(1)}, s32[2,2,8]{2,1,0:T(2,128)S(1)}, u32[]{:S(2)}, u32[]{:S(2)}) collective-permute-start(s32[2,2,8]{2,1,0:T(2,128)S(1)} %pad_add_fusion.2.asked_ref), channel_id=1, source_target_pairs={{0,8},{4,12},{8,0},{12,4},{16,24},{20,28},{24,16},{28,20},{1,9},{5... | collective-permute-start | bytes 392 | tf_op jit(solution)/shard_map/ppermute | solution.py:177
  8.3 0.6 %shard_map.57 = f32[2,128,128]{2,1,0:T(8,128)S(1)} custom-call(s32[2,2,8]{2,1,0:T(2,128)S(1)} %get-tuple-element.21.ids_ref.refs_0_, s32[2,2,8]{2,1,0:T(2,128)S(1)} %pad_add_fusion.2.asked_ref, f32[16,128,128]{2,1,0:T(8,128)S(1)} %get-tuple-element.24.latent_ref.refs_2_, f32[8,2,8,128]{3,2,1,0:T(8,128)S(1)} %get-tuple-element.25.coded_ref.refs_3_, ...), custom_call_target="tpu_custom_call" | custom-call | tf_op jit(solution)/shard_map/pallas_call | solution.py:228
  8.9 2.7 %collective-permute-start.3 = (f32[2,128,128]{2,1,0:T(8,128)S(1)}, f32[2,128,128]{2,1,0:T(8,128)S(1)}, u32[]{:S(2)}, u32[]{:S(2)}) collective-permute-start(f32[2,128,128]{2,1,0:T(8,128)S(1)} %shard_map.57), channel_id=1, source_target_pairs={{0,16},{4,20},{8,24},{12,28},{16,0},{20,4},{24,8},{28,12},{1,17},{... | collective-permute-start | bytes 393224 | tf_op jit(solution)/shard_map/ppermute | solution.py:177
  11.6 0.0 collective-permute-done.1
  11.6 1.6 %collective-permute-start.2 = (s32[4,2,8]{2,1,0:T(2,128)S(1)}, s32[4,2,8]{2,1,0:T(2,128)S(1)}, u32[]{:S(2)}, u32[]{:S(2)}) collective-permute-start(s32[4,2,8]{2,1,0:T(2,128)S(1)} %pad_add_fusion.1.asked_ref), channel_id=1, source_target_pairs={{0,4},{4,0},{8,12},{12,8},{16,20},{20,16},{24,28},{28,24},{1,5},{5... | collective-permute-start | bytes 776 | tf_op jit(solution)/shard_map/ppermute | solution.py:177
  13.2 0.0 collective-permute-done.4.refs_5_.passed_ref
  13.2 0.7 %shard_map.59 = (f32[2,128,128]{2,1,0:T(8,128)S(1)}, f32[2,144,128]{2,1,0:T(8,128)S(1)}) custom-call(s32[2,2,8]{2,1,0:T(2,128)S(1)} %get-tuple-element.21.ids_ref.refs_0_, s32[4,2,8]{2,1,0:T(2,128)S(1)} %pad_add_fusion.1.asked_ref, f32[16,128,128]{2,1,0:T(8,128)S(1)} %get-tuple-element.24.latent_ref.refs_2_, ...), custom_call_target="tpu_custom_call" | custom-call | tf_op jit(solution)/shard_map/pallas_call | solution.py:228
  13.8 2.5 %collective-permute-start.5 = (f32[2,128,128]{2,1,0:T(8,128)S(1)}, f32[2,128,128]{2,1,0:T(8,128)S(1)}, u32[]{:S(2)}, u32[]{:S(2)}) collective-permute-start(f32[2,128,128]{2,1,0:T(8,128)S(1)} %get-tuple-element.27), channel_id=1, source_target_pairs={{0,24},{4,28},{8,16},{12,20},{16,8},{20,12},{24,0},{28,4},{1,25},{... | collective-permute-start | bytes 393224 | tf_op jit(solution)/shard_map/ppermute | solution.py:177
  16.4 0.0 collective-permute-start.6
  16.4 0.0 collective-permute-done.2
  16.4 0.8 %shard_map.61 = (f32[2,128,128]{2,1,0:T(8,128)S(1)}, f32[2,128,128]{2,1,0:T(8,128)S(1)}, f32[2,144,128]{2,1,0:T(8,128)S(1)}, f32[2,144,128]{2,1,0:T(8,128)S(1)}) custom-call(s32[2,2,8]{2,1,0:T(2,128)S(1)} %get-tuple-element.21.ids_ref.refs_0_, s32[8,2,8]{2,1,0:T(2,128)S(1)} %pad_add_fusion.refs_1_.asked_ref, ...), custom_call_target="tpu_custom_call" | custom-call | tf_op jit(solution)/shard_map/pallas_call | solution.py:228
  17.1 2.0 %collective-permute-start.7 = (f32[2,144,128]{2,1,0:T(8,128)S(1)}, f32[2,144,128]{2,1,0:T(8,128)S(1)}, u32[]{:S(2)}, u32[]{:S(2)}) collective-permute-start(f32[2,144,128]{2,1,0:T(8,128)S(1)} %get-tuple-element.29), channel_id=1, source_target_pairs={{0,12},{4,8},{8,4},{12,0},{16,28},{20,24},{24,20},{28,16},{1,13},{... | collective-permute-start | bytes 442376 | tf_op jit(solution)/shard_map/ppermute | solution.py:177
  19.2 1.5 %collective-permute-start.8 = (f32[2,144,128]{2,1,0:T(8,128)S(1)}, f32[2,144,128]{2,1,0:T(8,128)S(1)}, u32[]{:S(2)}, u32[]{:S(2)}) collective-permute-start(f32[2,144,128]{2,1,0:T(8,128)S(1)} %get-tuple-element.30), channel_id=1, source_target_pairs={{0,4},{4,0},{8,12},{12,8},{16,20},{20,16},{24,28},{28,24},{1,5},{5... | collective-permute-start | bytes 442376 | tf_op jit(solution)/shard_map/ppermute | solution.py:177
  20.7 0.0 collective-permute-done.3.refs_4_
  20.7 2.7 %collective-permute-start.9 = (f32[2,128,128]{2,1,0:T(8,128)S(1)}, f32[2,128,128]{2,1,0:T(8,128)S(1)}, u32[]{:S(2)}, u32[]{:S(2)}) collective-permute-start(f32[2,128,128]{2,1,0:T(8,128)S(1)} %get-tuple-element.31), channel_id=1, source_target_pairs={{0,28},{4,24},{8,20},{12,16},{16,12},{20,8},{24,4},{28,0},{1,29},{... | collective-permute-start | bytes 393224 | tf_op jit(solution)/shard_map/ppermute | solution.py:177
  23.4 0.0 collective-permute-done.5.refs_4_
  23.4 3.5 %collective-permute-start.10 = (f32[2,128,128]{2,1,0:T(8,128)S(1)}, f32[2,128,128]{2,1,0:T(8,128)S(1)}, u32[]{:S(2)}, u32[]{:S(2)}) collective-permute-start(f32[2,128,128]{2,1,0:T(8,128)S(1)} %get-tuple-element.32), channel_id=1, source_target_pairs={{0,20},{4,16},{8,28},{12,24},{16,4},{20,0},{24,12},{28,8},{1,21},{... | collective-permute-start | bytes 393224 | tf_op jit(solution)/shard_map/ppermute | solution.py:177
  26.8 1.5 %shard_map.58.before_ref = f32[16,128,128]{2,1,0:T(8,128)S(1)} custom-call(s32[2,2,8]{2,1,0:T(2,128)S(1)} %get-tuple-element.21.ids_ref.refs_0_, s32[8,2,8]{2,1,0:T(2,128)S(1)} %pad_add_fusion.refs_1_.asked_ref, f32[16,128,128]{2,1,0:T(8,128)S(1)} %get-tuple-element.24.latent_ref.refs_2_, f32[8,2,8,128]{3,2,1,0:T(8,128)S(1)} %get-tuple-element.25.coded_ref.refs_3_, ...), custom_call_target="tpu_custom_call" | custom-call | flops 50331648 | bytes 3145728 | tf_op jit(solution)/shard_map/pallas_call | solution.py:247
  28.3 0.0 collective-permute-done.6.refs_5_.refs_6_.refs_7_
  28.3 1.8 %shard_map.60.before_ref = f32[16,128,128]{2,1,0:T(8,128)S(1)} custom-call(f32[16,128,128]{2,1,0:T(8,128)S(1)} %shard_map.58.before_ref, s32[2,2,8]{2,1,0:T(2,128)S(1)} %get-tuple-element.21.ids_ref.refs_0_, s32[8,2,8]{2,1,0:T(2,128)S(1)} %pad_add_fusion.refs_1_.asked_ref, ...), custom_call_target="tpu_custom_call", output_to_operand_aliasing={{}: (0, {})} | custom-call | flops 100663296 | bytes 3145728 | tf_op jit(solution)/shard_map/pallas_call | solution.py:247
  30.1 0.0 collective-permute-done.7.refs_4_.refs_6_.refs_5_
  30.1 0.2 collective-permute-done.8.refs_5_.refs_7_
  30.3 1.7 %shard_map.62.before_ref = f32[16,128,128]{2,1,0:T(8,128)S(1)} custom-call(f32[16,128,128]{2,1,0:T(8,128)S(1)} %shard_map.60.before_ref, s32[2,2,8]{2,1,0:T(2,128)S(1)} %get-tuple-element.21.ids_ref.refs_0_, s32[8,2,8]{2,1,0:T(2,128)S(1)} %pad_add_fusion.refs_1_.asked_ref, ...), custom_call_target="tpu_custom_call", output_to_operand_aliasing={{}: (0, {})} | custom-call | flops 100663296 | bytes 3145728 | tf_op jit(solution)/shard_map/pallas_call | solution.py:247
  32.0 0.0 collective-permute-done.9.refs_4_
  32.0 1.3 %shard_map.63.before_ref = f32[16,128,128]{2,1,0:T(8,128)S(1)} custom-call(f32[16,128,128]{2,1,0:T(8,128)S(1)} %shard_map.62.before_ref, s32[2,2,8]{2,1,0:T(2,128)S(1)} %get-tuple-element.21.ids_ref.refs_0_, s32[8,2,8]{2,1,0:T(2,128)S(1)} %pad_add_fusion.refs_1_.asked_ref, ...), custom_call_target="tpu_custom_call", output_to_operand_aliasing={{}: (0, {})} | custom-call | flops 50331648 | bytes 3145728 | tf_op jit(solution)/shard_map/pallas_call | solution.py:247
  33.4 1.4 %collective-permute-done.10.refs_4_ = f32[2,128,128]{2,1,0:T(8,128)S(1)} collective-permute-done((f32[2,128,128]{2,1,0:T(8,128)S(1)}, f32[2,128,128]{2,1,0:T(8,128)S(1)}, u32[]{:S(2)}, u32[]{:S(2)}) %collective-permute-start.10) | collective-permute-done | bytes 131104 | tf_op jit(solution)/shard_map/ppermute | solution.py:177
  34.8 1.3 %shard_map.64 = (f32[4,128,128]{2,1,0:T(8,128)S(1)}, f32[4,128,128]{2,1,0:T(8,128)S(1)}, f32[4,128,128]{2,1,0:T(8,128)S(1)}, f32[4,128,128]{2,1,0:T(8,128)S(1)}) custom-call(f32[16,128,128]{2,1,0:T(8,128)S(1)} %shard_map.63.before_ref, s32[2,2,8]{2,1,0:T(2,128)S(1)} %get-tuple-element.21.ids_ref.refs_0_, s32[8,2,8]{2,1,0:T(2,128)S(1)} %pad_add_fusion.refs_1_.asked_ref, ...), custom_call_target="tpu_custom_call" | custom-call | flops 50331648 | bytes 3145728 | tf_op jit(solution)/shard_map/pallas_call | solution.py:247
  36.1 0.1 collective-permute-start.12
  36.2 0.5 %collective-permute-start.11 = (f32[4,128,128]{2,1,0:T(8,128)S(1)}, f32[4,128,128]{2,1,0:T(8,128)S(1)}, u32[]{:S(2)}, u32[]{:S(2)}) collective-permute-start(f32[4,128,128]{2,1,0:T(8,128)S(1)} %get-tuple-element.34), channel_id=1, source_target_pairs={{0,1},{1,0},{2,3},{3,2},{4,5},{5,4},{6,7},{7,6},{8,9},{9,8},{10,11... | collective-permute-start | bytes 786440 | tf_op jit(solution)/shard_map/ppermute | solution.py:177
  36.7 1.0 %collective-permute-done.12 = f32[4,128,128]{2,1,0:T(8,128)S(1)} collective-permute-done((f32[4,128,128]{2,1,0:T(8,128)S(1)}, f32[4,128,128]{2,1,0:T(8,128)S(1)}, u32[]{:S(2)}, u32[]{:S(2)}) %collective-permute-start.12) | collective-permute-done | bytes 262176 | tf_op jit(solution)/shard_map/ppermute | solution.py:177
  37.8 1.8 %collective-permute-start.13 = (f32[4,128,128]{2,1,0:T(8,128)S(1)}, f32[4,128,128]{2,1,0:T(8,128)S(1)}, u32[]{:S(2)}, u32[]{:S(2)}) collective-permute-start(f32[4,128,128]{2,1,0:T(8,128)S(1)} %add.10), channel_id=1, source_target_pairs={{0,2},{1,3},{2,0},{3,1},{4,6},{5,7},{6,4},{7,5},{8,10},{9,11},{10,... | collective-permute-start | bytes 786440 | tf_op jit(solution)/shard_map/ppermute | solution.py:177
  39.5 0.0 collective-permute-done.11
  39.5 6.7 %collective-permute-done.13 = f32[4,128,128]{2,1,0:T(8,128)S(1)} collective-permute-done((f32[4,128,128]{2,1,0:T(8,128)S(1)}, f32[4,128,128]{2,1,0:T(8,128)S(1)}, u32[]{:S(2)}, u32[]{:S(2)}) %collective-permute-start.13) | collective-permute-done | bytes 262176 | tf_op jit(solution)/shard_map/ppermute | solution.py:177
  46.2 0.8 %add_add_fusion = f32[4,128,128]{2,1,0:T(8,128)} fusion(f32[4,128,128]{2,1,0:T(8,128)S(1)} %collective-permute-done.13, f32[4,128,128]{2,1,0:T(8,128)S(1)} %get-tuple-element.33, f32[4,128,128]{2,1,0:T(8,128)S(1)} %collective-permute-done.11), kind=kLoop, calls=%fused_computation | loop fusion | flops 131072 | bytes 1048576 | tf_op jit(solution)/shard_map/add | solution.py:264
  (7 shorter events, 0.1 us)
Async XLA Ops:
  0.0 0.7 %copy-start.3 = (s32[1,1,8,2]{2,3,1,0:T(2,128)S(1)}, s32[1,1,8,2]{2,3,1,0:T(2,128)}, u32[]{:S(2)}) copy-start(s32[1,1,8,2]{2,3,1,0:T(2,128)} %param.7) | copy-start | bytes 196
  0.0 0.7 %copy-start.4 = (s32[1,1,8,2]{2,3,1,0:T(2,128)S(1)}, s32[1,1,8,2]{2,3,1,0:T(2,128)}, u32[]{:S(2)}) copy-start(s32[1,1,8,2]{2,3,1,0:T(2,128)} %param.8) | copy-start | bytes 196
  0.0 0.7 %copy-start.2 = (s32[1,1,8,2]{2,3,1,0:T(2,128)S(1)}, s32[1,1,8,2]{2,3,1,0:T(2,128)}, u32[]{:S(2)}) copy-start(s32[1,1,8,2]{2,3,1,0:T(2,128)} %param.6) | copy-start | bytes 196
  0.7 4.1 %copy-start = (f32[2048,128]{1,0:T(8,128)S(1)}, f32[2048,128]{1,0:T(8,128)}, u32[]{:S(2)}) copy-start(f32[2048,128]{1,0:T(8,128)} %param.5) | copy-start | bytes 3145732
  0.7 4.1 %copy-start.1 = (s32[1,1,8,2,8,128]{5,4,3,2,1,0:T(8,128)S(1)}, s32[1,1,8,2,8,128]{5,4,3,2,1,0:T(8,128)}, u32[]{:S(2)}) copy-start(s32[1,1,8,2,8,128]{5,4,3,2,1,0:T(8,128)} %param.9) | copy-start | bytes 196612
  0.7 5.6 %collective-permute-start = (s32[2,8]{1,0:T(2,128)S(1)}, s32[2,8]{1,0:T(2,128)S(1)}, u32[]{:S(2)}, u32[]{:S(2)}) collective-permute-start(s32[2,8]{1,0:T(2,128)S(1)} %get-tuple-element.22), channel_id=1, source_target_pairs={{0,16},{4,20},{8,24},{12,28},{16,0},{20,4},{24,8},{28,12},{1,17},{... | collective-permute-start | bytes 200 | tf_op jit(solution)/shard_map/ppermute | solution.py:177
  5.1 8.0 %collective-permute-start.4 = (f32[4,2,8,128]{3,2,1,0:T(8,128)S(1)}, f32[4,2,8,128]{3,2,1,0:T(8,128)S(1)}, u32[]{:S(2)}, u32[]{:S(2)}) collective-permute-start(f32[4,2,8,128]{3,2,1,0:T(8,128)S(1)} %get-tuple-element.26), channel_id=1, source_target_pairs={{0,16},{4,20},{8,24},{12,28},{16,0},{20,4},{24,8},{28,12},{1,17},{... | collective-permute-start | bytes 98312 | tf_op jit(solution)/shard_map/ppermute | solution.py:177
  6.4 5.2 %collective-permute-start.1 = (s32[2,2,8]{2,1,0:T(2,128)S(1)}, s32[2,2,8]{2,1,0:T(2,128)S(1)}, u32[]{:S(2)}, u32[]{:S(2)}) collective-permute-start(s32[2,2,8]{2,1,0:T(2,128)S(1)} %pad_add_fusion.2.asked_ref), channel_id=1, source_target_pairs={{0,8},{4,12},{8,0},{12,4},{16,24},{20,28},{24,16},{28,20},{1,9},{5... | collective-permute-start | bytes 392 | tf_op jit(solution)/shard_map/ppermute | solution.py:177
  8.9 11.8 %collective-permute-start.3 = (f32[2,128,128]{2,1,0:T(8,128)S(1)}, f32[2,128,128]{2,1,0:T(8,128)S(1)}, u32[]{:S(2)}, u32[]{:S(2)}) collective-permute-start(f32[2,128,128]{2,1,0:T(8,128)S(1)} %shard_map.57), channel_id=1, source_target_pairs={{0,16},{4,20},{8,24},{12,28},{16,0},{20,4},{24,8},{28,12},{1,17},{... | collective-permute-start | bytes 393224 | tf_op jit(solution)/shard_map/ppermute | solution.py:177
  11.6 4.8 %collective-permute-start.2 = (s32[4,2,8]{2,1,0:T(2,128)S(1)}, s32[4,2,8]{2,1,0:T(2,128)S(1)}, u32[]{:S(2)}, u32[]{:S(2)}) collective-permute-start(s32[4,2,8]{2,1,0:T(2,128)S(1)} %pad_add_fusion.1.asked_ref), channel_id=1, source_target_pairs={{0,4},{4,0},{8,12},{12,8},{16,20},{20,16},{24,28},{28,24},{1,5},{5... | collective-permute-start | bytes 776 | tf_op jit(solution)/shard_map/ppermute | solution.py:177
  13.8 9.5 %collective-permute-start.5 = (f32[2,128,128]{2,1,0:T(8,128)S(1)}, f32[2,128,128]{2,1,0:T(8,128)S(1)}, u32[]{:S(2)}, u32[]{:S(2)}) collective-permute-start(f32[2,128,128]{2,1,0:T(8,128)S(1)} %get-tuple-element.27), channel_id=1, source_target_pairs={{0,24},{4,28},{8,16},{12,20},{16,8},{20,12},{24,0},{28,4},{1,25},{... | collective-permute-start | bytes 393224 | tf_op jit(solution)/shard_map/ppermute | solution.py:177
  16.4 12.0 %collective-permute-start.6 = (f32[2,144,128]{2,1,0:T(8,128)S(1)}, f32[2,144,128]{2,1,0:T(8,128)S(1)}, u32[]{:S(2)}, u32[]{:S(2)}) collective-permute-start(f32[2,144,128]{2,1,0:T(8,128)S(1)} %get-tuple-element.28), channel_id=1, source_target_pairs={{0,8},{4,12},{8,0},{12,4},{16,24},{20,28},{24,16},{28,20},{1,9},{5... | collective-permute-start | bytes 442376 | tf_op jit(solution)/shard_map/ppermute | solution.py:177
  17.1 13.0 %collective-permute-start.7 = (f32[2,144,128]{2,1,0:T(8,128)S(1)}, f32[2,144,128]{2,1,0:T(8,128)S(1)}, u32[]{:S(2)}, u32[]{:S(2)}) collective-permute-start(f32[2,144,128]{2,1,0:T(8,128)S(1)} %get-tuple-element.29), channel_id=1, source_target_pairs={{0,12},{4,8},{8,4},{12,0},{16,28},{20,24},{24,20},{28,16},{1,13},{... | collective-permute-start | bytes 442376 | tf_op jit(solution)/shard_map/ppermute | solution.py:177
  19.2 11.1 %collective-permute-start.8 = (f32[2,144,128]{2,1,0:T(8,128)S(1)}, f32[2,144,128]{2,1,0:T(8,128)S(1)}, u32[]{:S(2)}, u32[]{:S(2)}) collective-permute-start(f32[2,144,128]{2,1,0:T(8,128)S(1)} %get-tuple-element.30), channel_id=1, source_target_pairs={{0,4},{4,0},{8,12},{12,8},{16,20},{20,16},{24,28},{28,24},{1,5},{5... | collective-permute-start | bytes 442376 | tf_op jit(solution)/shard_map/ppermute | solution.py:177
  20.7 11.3 %collective-permute-start.9 = (f32[2,128,128]{2,1,0:T(8,128)S(1)}, f32[2,128,128]{2,1,0:T(8,128)S(1)}, u32[]{:S(2)}, u32[]{:S(2)}) collective-permute-start(f32[2,128,128]{2,1,0:T(8,128)S(1)} %get-tuple-element.31), channel_id=1, source_target_pairs={{0,28},{4,24},{8,20},{12,16},{16,12},{20,8},{24,4},{28,0},{1,29},{... | collective-permute-start | bytes 393224 | tf_op jit(solution)/shard_map/ppermute | solution.py:177
  23.4 11.4 %collective-permute-start.10 = (f32[2,128,128]{2,1,0:T(8,128)S(1)}, f32[2,128,128]{2,1,0:T(8,128)S(1)}, u32[]{:S(2)}, u32[]{:S(2)}) collective-permute-start(f32[2,128,128]{2,1,0:T(8,128)S(1)} %get-tuple-element.32), channel_id=1, source_target_pairs={{0,20},{4,16},{8,28},{12,24},{16,4},{20,0},{24,12},{28,8},{1,21},{... | collective-permute-start | bytes 393224 | tf_op jit(solution)/shard_map/ppermute | solution.py:177
  36.1 1.6 %collective-permute-start.12 = (f32[4,128,128]{2,1,0:T(8,128)S(1)}, f32[4,128,128]{2,1,0:T(8,128)S(1)}, u32[]{:S(2)}, u32[]{:S(2)}) collective-permute-start(f32[4,128,128]{2,1,0:T(8,128)S(1)} %get-tuple-element.36), channel_id=1, source_target_pairs={{0,1},{1,0},{2,3},{3,2},{4,5},{5,4},{6,7},{7,6},{8,9},{9,8},{10,11... | collective-permute-start | bytes 786440 | tf_op jit(solution)/shard_map/ppermute | solution.py:177
  36.2 3.3 %collective-permute-start.11 = (f32[4,128,128]{2,1,0:T(8,128)S(1)}, f32[4,128,128]{2,1,0:T(8,128)S(1)}, u32[]{:S(2)}, u32[]{:S(2)}) collective-permute-start(f32[4,128,128]{2,1,0:T(8,128)S(1)} %get-tuple-element.34), channel_id=1, source_target_pairs={{0,1},{1,0},{2,3},{3,2},{4,5},{5,4},{6,7},{7,6},{8,9},{9,8},{10,11... | collective-permute-start | bytes 786440 | tf_op jit(solution)/shard_map/ppermute | solution.py:177
  37.8 8.4 %collective-permute-start.13 = (f32[4,128,128]{2,1,0:T(8,128)S(1)}, f32[4,128,128]{2,1,0:T(8,128)S(1)}, u32[]{:S(2)}, u32[]{:S(2)}) collective-permute-start(f32[4,128,128]{2,1,0:T(8,128)S(1)} %add.10), channel_id=1, source_target_pairs={{0,2},{1,3},{2,0},{3,1},{4,6},{5,7},{6,4},{7,5},{8,10},{9,11},{10,... | collective-permute-start | bytes 786440 | tf_op jit(solution)/shard_map/ppermute | solution.py:177

commit v5 on v4

--- a/solution.py
+++ b/solution.py
@@ -9,7 +9,6 @@
 
 F32 = jnp.float32
 BF16 = jnp.bfloat16
-SMEM = pl.BlockSpec(memory_space=pltpu.SMEM)
 VMEM = pl.BlockSpec(memory_space=pltpu.VMEM)
 HBM = pl.BlockSpec(memory_space=pltpu.HBM)
 WAIT_FLOPS = 10**10
@@ -41,8 +40,17 @@
     return jnp.where(hit, 1.0, 0.0)
 
 
-def own_id(ids_ref, asked_ref, place, me, peer, slot):
-    return jnp.where(peer > me, ids_ref[0, slot, peer], asked_ref[place, slot, me])
+def picked(table, column):
+    columns = lax.broadcasted_iota(jnp.int32, table.shape, 1)
+    hits = jnp.where(columns == column, table, 0).astype(F32)
+    return [jnp.sum(hits[slot : slot + 1]).astype(jnp.int32) for slot in range(table.shape[0])]
+
+
+def own_blocks(shift, place, ids_ref, asked_ref):
+    me = lax.axis_index("rows")
+    peer = me ^ shift
+    low = peer > me
+    return picked(jnp.where(low, ids_ref[0], asked_ref[place]), jnp.where(low, peer, me))
 
 
 def pack_kernel(shifts, places, ids_ref, asked_ref, latent_ref, coded_ref, passed_ref, *message_refs):
@@ -51,8 +59,7 @@
     top, _, lists, _ = passed_ref.shape
     for shift, place, message_ref in zip(shifts, places, message_refs):
         peer = me ^ shift
-        for slot in range(message_ref.shape[0]):
-            block = own_id(ids_ref, asked_ref, place, me, peer, slot)
+        for slot, block in enumerate(own_blocks(shift, place, ids_ref, asked_ref)):
             message_ref[slot, :tile] = latent_ref[block]
             if shift < top:
                 message_ref[slot, tile : tile + lists] = coded_ref[peer, slot]
@@ -76,14 +83,11 @@
     return jnp.where(low, target.T, target)
 
 
-def add_peer(shift, place, total_ref, ids_ref, asked_ref, latent_ref, coded_ref, message_ref, carrier_ref):
-    me = lax.axis_index("rows")
-    peer = me ^ shift
+def add_peer(shift, place, total_ref, ids_ref, asked_ref, coded_ref, sent_ref, message_ref, carrier_ref):
     quarter = lax.axis_index("pairs") * (total_ref.shape[0] // lax.axis_size("pairs"))
-    tile = latent_ref.shape[1]
-    for slot in range(message_ref.shape[0]):
-        block = own_id(ids_ref, asked_ref, place, me, peer, slot)
-        own = halves(latent_ref[block])
+    tile = coded_ref.shape[-1]
+    for slot, block in enumerate(own_blocks(shift, place, ids_ref, asked_ref)):
+        own = halves(sent_ref[slot, :tile])
         other = halves(message_ref[slot, :tile])
         target = slot_target(shift, coded_ref, carrier_ref, slot)
         residue = jax.nn.sigmoid(product(own, other, 1, 1)) - target
@@ -118,8 +122,8 @@
 def add_own(total_ref, ids_ref, latent_ref, coded_ref):
     me = lax.axis_index("rows")
     quarter = lax.axis_index("pairs") * (total_ref.shape[0] // lax.axis_size("pairs"))
-    for slot in range(coded_ref.shape[1]):
-        left_block, right_block = ids_ref[0, slot, me], ids_ref[1, slot, me]
+    ids = zip(picked(ids_ref[0], me), picked(ids_ref[1], me))
+    for slot, (left_block, right_block) in enumerate(ids):
         left, right = halves(latent_ref[left_block]), halves(latent_ref[right_block])
         target = natural_target(coded_ref[me, slot])
         residue = halves(jax.nn.sigmoid(product(right, left, 1, 1)) - target)
@@ -128,15 +132,14 @@
 
 
 def add_peers(shifts, places, total_ref, *refs):
-    fixed, refs = refs[:4], refs[4:]
-    count = len(shifts)
-    for shift, place, message_ref, carrier_ref in zip(shifts, places, refs[:count], refs[count:]):
-        add_peer(shift, place, total_ref, *fixed, message_ref, carrier_ref)
-
-
-def first_kernel(shifts, places, *refs):
+    fixed, refs = refs[:3], refs[3:]
+    for at, (shift, place) in enumerate(zip(shifts, places)):
+        add_peer(shift, place, total_ref, *fixed, *refs[3 * at : 3 * at + 3])
+
+
+def first_kernel(shifts, places, latent_ref, *refs):
     *refs, total_ref = refs
-    ids_ref, _, latent_ref, coded_ref = refs[:4]
+    ids_ref, _, coded_ref = refs[:3]
     total_ref[...] = jnp.zeros_like(total_ref)
     add_own(total_ref, ids_ref, latent_ref, coded_ref)
     add_peers(shifts, places, total_ref, *refs)
@@ -149,7 +152,7 @@
 
 
 def last_kernel(shifts, places, before_ref, *refs):
-    count = 4 + 2 * len(shifts)
+    count = 3 + 3 * len(shifts)
     refs, part_refs, total_ref = refs[:count], refs[count:-1], refs[-1]
     total_ref[...] = before_ref[...]
     add_peers(shifts, places, total_ref, *refs)
@@ -216,7 +219,7 @@
     passed = swap(far_coded, "rows", top)
     near_message = jax.ShapeDtypeStruct((slots, tile + 2 * lists, width), F32)
     far_message = jax.ShapeDtypeStruct((slots, tile, width), F32)
-    asked, where, arrived = own_asked, [0], {}
+    asked, where, leaving, arrived = own_asked, [0], {}, {}
     bit = top
     while bit:
         if len(where) == 1:
@@ -228,12 +231,12 @@
         sent = pl.pallas_call(
             functools.partial(pack_kernel, shifts, [where.index(at) for at in shifts]),
             out_shape=[far_message if at >= top else near_message for at in shifts],
-            in_specs=[SMEM] * 2 + [VMEM] * 3,
+            in_specs=[VMEM] * 5,
             out_specs=[VMEM] * len(shifts),
             compiler_params=PARAMS,
         )(ids, asked, blocks, coded, passed if bit < top else coded[:top])
         for shift, value in zip(shifts, sent):
-            arrived[shift] = swap(value, "rows", shift)
+            leaving[shift], arrived[shift] = value, swap(value, "rows", shift)
         bit //= 2
 
     whole = jax.ShapeDtypeStruct(blocks.shape, F32)
@@ -241,9 +244,10 @@
     part = jax.ShapeDtypeStruct((blocks.shape[0] // parts, tile, width), F32)
     groups = shift_groups(peers)
     carrier = {at: passed if at == top else arrived[at % top] for at in arrived}
-    total = ()
+    total = [blocks]
     for group in groups:
         first, last = group is groups[0], group is groups[-1]
+        messages = [value for at in group for value in (leaving[at], arrived[at], carrier[at])]
         total = pl.pallas_call(
             functools.partial(
                 first_kernel if first else last_kernel if last else middle_kernel,
@@ -251,13 +255,13 @@
                 [where.index(at) for at in group],
             ),
             out_shape=[part] * parts if last else [whole],
-            in_specs=[VMEM] * len(total) + [SMEM] * 2 + [VMEM] * (2 + 2 * len(group)),
+            in_specs=[VMEM] * (4 + len(messages)),
             out_specs=[VMEM] * (parts if last else 1),
             scratch_shapes=[pltpu.VMEM(blocks.shape, F32)] if last else [],
             input_output_aliases={} if first or last else {0: 0},
             compiler_params=PARAMS,
             cost_estimate=estimate(slots * len(group), tile, 3 * blocks.size * 4),
-        )(*total, ids, asked, blocks, coded, *[arrived[at] for at in group], *[carrier[at] for at in group])
+        )(*total, ids, asked, coded, *messages)
     held = total
     far_half = held[2] + swap(held[3], "pairs", 1)
     kept = swap(held[1], "pairs", 1)

time: 47.1 us -> 46.1 us (0.979)
  Pallas kernels: 9.97 us -> 5.05 us
  waiting for transfers between devices: 9.3 us -> 12.5 us
  starting transfers between devices: 26 us -> 26.7 us
    pallas_call x5, Pallas kernels: 7.66 us -> 4.32 us  [body(): pl.pallas_call(functools.partial(first_kernel if first else last_kernel i...]
    ppermute x14, waiting for transfers between devices: 9.3 us -> 12.5 us  [swap(): lax.ppermute(value, axis, [(at, at ^ shift) for at in range(lax.axis_size...]
    pallas_call x3, Pallas kernels: 2.03 us -> 0.45 us  [body(): pl.pallas_call(functools.partial(pack_kernel, shifts, [where.index(at) fo...]
    ppermute x14, starting transfers between devices: 26 us -> 26.7 us  [swap(): lax.ppermute(value, axis, [(at, at ^ shift) for at in range(lax.axis_size...]
  transfers between devices with their start and end apart: 14 -> 14, of which waited for: 4 -> 4; matrix products, arithmetic and copies ran while one was open for 0% -> 0% of each run, Pallas kernels for 18% -> 10%
where the time goes in v5:
time: 46.1 us; the launch traced here: 45.9 us
  starting transfers between devices  26.7 us (58%)
  waiting for transfers between devices  12.5 us (27%)
  Pallas kernels  5.05 us (11%)
  other arithmetic  0.8 us (2%)
  local copies, waits for them, and re-layouts  0.72 us (2%)
    ppermute x14, starting transfers between devices, swap(): lax.ppermute(value, axis, [(at, at ^ shift) for at in range(lax.axis_size...  26.7 us
    ppermute x14, waiting for transfers between devices, swap(): lax.ppermute(value, axis, [(at, at ^ shift) for at in range(lax.axis_size...  12.5 us
    pallas_call x5, Pallas kernels, body(): pl.pallas_call(functools.partial(first_kernel if first else last_kernel i...  4.32 us
  transfers between devices with their start and end apart: 14, of which 4 were waited for; matrix products, arithmetic and copies ran while one was open for 0% of the time, Pallas kernels for 10%

profile of v5, /device:TPU:0, one launch (start us, length us, event | category | flops | bytes accessed | tf_op | source)
XLA Modules:
  0.0 45.9 jit_solution(10521609169547405824)
XLA Ops:
  0.0 0.0 copy-start.3
  0.0 0.0 copy-start.4
  0.0 0.0 copy-start.2
  0.0 0.7 %copy-done.3 = s32[1,1,8,2]{2,3,1,0:T(2,128)S(1)} copy-done((s32[1,1,8,2]{2,3,1,0:T(2,128)S(1)}, s32[1,1,8,2]{2,3,1,0:T(2,128)}, u32[]{:S(2)}) %copy-start.3) | copy-done | bytes 88
  0.7 0.0 copy-done.4
  0.7 0.0 copy-done.2
  0.7 0.0 copy-start
  0.7 0.0 copy-start.1
  0.7 4.1 %collective-permute-start = (s32[2,8]{1,0:T(2,128)S(1)}, s32[2,8]{1,0:T(2,128)S(1)}, u32[]{:S(2)}, u32[]{:S(2)}) collective-permute-start(s32[2,8]{1,0:T(2,128)S(1)} %get-tuple-element.24), channel_id=1, source_target_pairs={{0,16},{4,20},{8,24},{12,28},{16,0},{20,4},{24,8},{28,12},{1,17},{... | collective-permute-start | bytes 200 | tf_op jit(solution)/shard_map/ppermute | solution.py:180
  4.8 0.0 copy-done
  4.8 0.0 copy-done.1
  4.8 0.3 shard_map.56
  5.1 1.2 %collective-permute-start.4 = (f32[4,2,8,128]{3,2,1,0:T(8,128)S(1)}, f32[4,2,8,128]{3,2,1,0:T(8,128)S(1)}, u32[]{:S(2)}, u32[]{:S(2)}) collective-permute-start(f32[4,2,8,128]{3,2,1,0:T(8,128)S(1)} %get-tuple-element.26), channel_id=1, source_target_pairs={{0,16},{4,20},{8,24},{12,28},{16,0},{20,4},{24,8},{28,12},{1,17},{... | collective-permute-start | bytes 98312 | tf_op jit(solution)/shard_map/ppermute | solution.py:180
  6.3 0.0 collective-permute-done
  6.4 1.9 %collective-permute-start.1 = (s32[2,2,8]{2,1,0:T(2,128)S(1)}, s32[2,2,8]{2,1,0:T(2,128)S(1)}, u32[]{:S(2)}, u32[]{:S(2)}) collective-permute-start(s32[2,2,8]{2,1,0:T(2,128)S(1)} %pad_add_fusion.2.asked_ref), channel_id=1, source_target_pairs={{0,8},{4,12},{8,0},{12,4},{16,24},{20,28},{24,16},{28,20},{1,9},{5... | collective-permute-start | bytes 392 | tf_op jit(solution)/shard_map/ppermute | solution.py:180
  8.3 0.1 shard_map.57.refs_3_
  8.4 2.7 %collective-permute-start.3 = (f32[2,128,128]{2,1,0:T(8,128)S(1)}, f32[2,128,128]{2,1,0:T(8,128)S(1)}, u32[]{:S(2)}, u32[]{:S(2)}) collective-permute-start(f32[2,128,128]{2,1,0:T(8,128)S(1)} %shard_map.57.refs_3_), channel_id=1, source_target_pairs={{0,16},{4,20},{8,24},{12,28},{16,0},{20,4},{24,8},{28,12},{1,17},{... | collective-permute-start | bytes 393224 | tf_op jit(solution)/shard_map/ppermute | solution.py:180
  11.1 0.0 collective-permute-done.1
  11.1 1.6 %collective-permute-start.2 = (s32[4,2,8]{2,1,0:T(2,128)S(1)}, s32[4,2,8]{2,1,0:T(2,128)S(1)}, u32[]{:S(2)}, u32[]{:S(2)}) collective-permute-start(s32[4,2,8]{2,1,0:T(2,128)S(1)} %pad_add_fusion.1.asked_ref), channel_id=1, source_target_pairs={{0,4},{4,0},{8,12},{12,8},{16,20},{20,16},{24,28},{28,24},{1,5},{5... | collective-permute-start | bytes 776 | tf_op jit(solution)/shard_map/ppermute | solution.py:180
  12.7 0.0 collective-permute-done.4.refs_5_.passed_ref
  12.7 0.1 shard_map.59
  12.8 2.8 %collective-permute-start.5 = (f32[2,128,128]{2,1,0:T(8,128)S(1)}, f32[2,128,128]{2,1,0:T(8,128)S(1)}, u32[]{:S(2)}, u32[]{:S(2)}) collective-permute-start(f32[2,128,128]{2,1,0:T(8,128)S(1)} %get-tuple-element.27.refs_3_), channel_id=1, source_target_pairs={{0,24},{4,28},{8,16},{12,20},{16,8},{20,12},{24,0},{28,4},{1,25},{... | collective-permute-start | bytes 393224 | tf_op jit(solution)/shard_map/ppermute | solution.py:180
  15.7 0.0 collective-permute-start.6
  15.7 0.0 collective-permute-done.2
  15.7 0.2 shard_map.61
  15.8 2.0 %collective-permute-start.7 = (f32[2,144,128]{2,1,0:T(8,128)S(1)}, f32[2,144,128]{2,1,0:T(8,128)S(1)}, u32[]{:S(2)}, u32[]{:S(2)}) collective-permute-start(f32[2,144,128]{2,1,0:T(8,128)S(1)} %get-tuple-element.29.refs_3_), channel_id=1, source_target_pairs={{0,12},{4,8},{8,4},{12,0},{16,28},{20,24},{24,20},{28,16},{1,13},{... | collective-permute-start | bytes 442376 | tf_op jit(solution)/shard_map/ppermute | solution.py:180
  17.9 1.5 %collective-permute-start.8 = (f32[2,144,128]{2,1,0:T(8,128)S(1)}, f32[2,144,128]{2,1,0:T(8,128)S(1)}, u32[]{:S(2)}, u32[]{:S(2)}) collective-permute-start(f32[2,144,128]{2,1,0:T(8,128)S(1)} %get-tuple-element.30.refs_6_), channel_id=1, source_target_pairs={{0,4},{4,0},{8,12},{12,8},{16,20},{20,16},{24,28},{28,24},{1,5},{5... | collective-permute-start | bytes 442376 | tf_op jit(solution)/shard_map/ppermute | solution.py:180
  19.4 0.0 collective-permute-done.3.refs_4_
  19.4 3.7 %collective-permute-start.9 = (f32[2,128,128]{2,1,0:T(8,128)S(1)}, f32[2,128,128]{2,1,0:T(8,128)S(1)}, u32[]{:S(2)}, u32[]{:S(2)}) collective-permute-start(f32[2,128,128]{2,1,0:T(8,128)S(1)} %get-tuple-element.31.refs_3_), channel_id=1, source_target_pairs={{0,28},{4,24},{8,20},{12,16},{16,12},{20,8},{24,4},{28,0},{1,29},{... | collective-permute-start | bytes 393224 | tf_op jit(solution)/shard_map/ppermute | solution.py:180
  23.1 0.0 collective-permute-done.5.refs_4_
  23.1 3.1 %collective-permute-start.10 = (f32[2,128,128]{2,1,0:T(8,128)S(1)}, f32[2,128,128]{2,1,0:T(8,128)S(1)}, u32[]{:S(2)}, u32[]{:S(2)}) collective-permute-start(f32[2,128,128]{2,1,0:T(8,128)S(1)} %get-tuple-element.32.refs_3_), channel_id=1, source_target_pairs={{0,20},{4,16},{8,28},{12,24},{16,4},{20,0},{24,12},{28,8},{1,21},{... | collective-permute-start | bytes 393224 | tf_op jit(solution)/shard_map/ppermute | solution.py:180
  26.2 0.9 %shard_map.58.before_ref = f32[16,128,128]{2,1,0:T(8,128)S(1)} custom-call(f32[16,128,128]{2,1,0:T(8,128)S(1)} %get-tuple-element.22.latent_ref, s32[2,2,8]{2,1,0:T(2,128)S(1)} %get-tuple-element.23.ids_ref.refs_0_, s32[8,2,8]{2,1,0:T(2,128)S(1)} %pad_add_fusion.refs_1_.asked_ref, f32[8,2,8,128]{3,2,1,0:T(8,128)S(1)} %get-tuple-element.25.coded_ref.refs_2_, ...), custom_call_target="tpu_custom_call" | custom-call | flops 50331648 | bytes 3145728 | tf_op jit(solution)/shard_map/pallas_call | solution.py:251
  27.1 0.0 collective-permute-done.6.refs_5_.refs_7_.refs_8_
  27.1 1.1 %shard_map.60.before_ref = f32[16,128,128]{2,1,0:T(8,128)S(1)} custom-call(f32[16,128,128]{2,1,0:T(8,128)S(1)} %shard_map.58.before_ref, s32[2,2,8]{2,1,0:T(2,128)S(1)} %get-tuple-element.23.ids_ref.refs_0_, s32[8,2,8]{2,1,0:T(2,128)S(1)} %pad_add_fusion.refs_1_.asked_ref, ...), custom_call_target="tpu_custom_call", output_to_operand_aliasing={{}: (0, {})} | custom-call | flops 100663296 | bytes 3145728 | tf_op jit(solution)/shard_map/pallas_call | solution.py:251
  28.2 1.3 %collective-permute-done.7.refs_4_.refs_5_ = f32[2,144,128]{2,1,0:T(8,128)S(1)} collective-permute-done((f32[2,144,128]{2,1,0:T(8,128)S(1)}, f32[2,144,128]{2,1,0:T(8,128)S(1)}, u32[]{:S(2)}, u32[]{:S(2)}) %collective-permute-start.7) | collective-permute-done | bytes 147488 | tf_op jit(solution)/shard_map/ppermute | solution.py:180
  29.5 0.0 collective-permute-done.8.refs_7_.refs_8_.refs_5_
  29.5 1.1 %shard_map.62.before_ref = f32[16,128,128]{2,1,0:T(8,128)S(1)} custom-call(f32[16,128,128]{2,1,0:T(8,128)S(1)} %shard_map.60.before_ref, s32[2,2,8]{2,1,0:T(2,128)S(1)} %get-tuple-element.23.ids_ref.refs_0_, s32[8,2,8]{2,1,0:T(2,128)S(1)} %pad_add_fusion.refs_1_.asked_ref, ...), custom_call_target="tpu_custom_call", output_to_operand_aliasing={{}: (0, {})} | custom-call | flops 100663296 | bytes 3145728 | tf_op jit(solution)/shard_map/pallas_call | solution.py:251
  30.5 0.0 collective-permute-done.9.refs_4_
  30.5 0.6 %shard_map.63.before_ref = f32[16,128,128]{2,1,0:T(8,128)S(1)} custom-call(f32[16,128,128]{2,1,0:T(8,128)S(1)} %shard_map.62.before_ref, s32[2,2,8]{2,1,0:T(2,128)S(1)} %get-tuple-element.23.ids_ref.refs_0_, s32[8,2,8]{2,1,0:T(2,128)S(1)} %pad_add_fusion.refs_1_.asked_ref, ...), custom_call_target="tpu_custom_call", output_to_operand_aliasing={{}: (0, {})} | custom-call | flops 50331648 | bytes 3145728 | tf_op jit(solution)/shard_map/pallas_call | solution.py:251
  31.2 3.3 %collective-permute-done.10.refs_4_ = f32[2,128,128]{2,1,0:T(8,128)S(1)} collective-permute-done((f32[2,128,128]{2,1,0:T(8,128)S(1)}, f32[2,128,128]{2,1,0:T(8,128)S(1)}, u32[]{:S(2)}, u32[]{:S(2)}) %collective-permute-start.10) | collective-permute-done | bytes 131104 | tf_op jit(solution)/shard_map/ppermute | solution.py:180
  34.5 0.6 %shard_map.64 = (f32[4,128,128]{2,1,0:T(8,128)S(1)}, f32[4,128,128]{2,1,0:T(8,128)S(1)}, f32[4,128,128]{2,1,0:T(8,128)S(1)}, f32[4,128,128]{2,1,0:T(8,128)S(1)}) custom-call(f32[16,128,128]{2,1,0:T(8,128)S(1)} %shard_map.63.before_ref, s32[2,2,8]{2,1,0:T(2,128)S(1)} %get-tuple-element.23.ids_ref.refs_0_, s32[8,2,8]{2,1,0:T(2,128)S(1)} %pad_add_fusion.refs_1_.asked_ref, ...), custom_call_target="tpu_custom_call" | custom-call | flops 50331648 | bytes 3145728 | tf_op jit(solution)/shard_map/pallas_call | solution.py:251
  35.1 0.1 collective-permute-start.12
  35.2 0.5 %collective-permute-start.11 = (f32[4,128,128]{2,1,0:T(8,128)S(1)}, f32[4,128,128]{2,1,0:T(8,128)S(1)}, u32[]{:S(2)}, u32[]{:S(2)}) collective-permute-start(f32[4,128,128]{2,1,0:T(8,128)S(1)} %get-tuple-element.34), channel_id=1, source_target_pairs={{0,1},{1,0},{2,3},{3,2},{4,5},{5,4},{6,7},{7,6},{8,9},{9,8},{10,11... | collective-permute-start | bytes 786440 | tf_op jit(solution)/shard_map/ppermute | solution.py:180
  35.7 1.0 %collective-permute-done.12 = f32[4,128,128]{2,1,0:T(8,128)S(1)} collective-permute-done((f32[4,128,128]{2,1,0:T(8,128)S(1)}, f32[4,128,128]{2,1,0:T(8,128)S(1)}, u32[]{:S(2)}, u32[]{:S(2)}) %collective-permute-start.12) | collective-permute-done | bytes 262176 | tf_op jit(solution)/shard_map/ppermute | solution.py:180
  36.7 1.6 %collective-permute-start.13 = (f32[4,128,128]{2,1,0:T(8,128)S(1)}, f32[4,128,128]{2,1,0:T(8,128)S(1)}, u32[]{:S(2)}, u32[]{:S(2)}) collective-permute-start(f32[4,128,128]{2,1,0:T(8,128)S(1)} %add.10), channel_id=1, source_target_pairs={{0,2},{1,3},{2,0},{3,1},{4,6},{5,7},{6,4},{7,5},{8,10},{9,11},{10,... | collective-permute-start | bytes 786440 | tf_op jit(solution)/shard_map/ppermute | solution.py:180
  38.3 0.0 collective-permute-done.11
  38.3 6.9 %collective-permute-done.13 = f32[4,128,128]{2,1,0:T(8,128)S(1)} collective-permute-done((f32[4,128,128]{2,1,0:T(8,128)S(1)}, f32[4,128,128]{2,1,0:T(8,128)S(1)}, u32[]{:S(2)}, u32[]{:S(2)}) %collective-permute-start.13) | collective-permute-done | bytes 262176 | tf_op jit(solution)/shard_map/ppermute | solution.py:180
  45.2 0.8 %add_add_fusion = f32[4,128,128]{2,1,0:T(8,128)} fusion(f32[4,128,128]{2,1,0:T(8,128)S(1)} %collective-permute-done.13, f32[4,128,128]{2,1,0:T(8,128)S(1)} %get-tuple-element.33, f32[4,128,128]{2,1,0:T(8,128)S(1)} %collective-permute-done.11), kind=kLoop, calls=%fused_computation | loop fusion | flops 131072 | bytes 1048576 | tf_op jit(solution)/shard_map/add | solution.py:268
  (7 shorter events, 0.1 us)
Async XLA Ops:
  0.0 0.7 %copy-start.3 = (s32[1,1,8,2]{2,3,1,0:T(2,128)S(1)}, s32[1,1,8,2]{2,3,1,0:T(2,128)}, u32[]{:S(2)}) copy-start(s32[1,1,8,2]{2,3,1,0:T(2,128)} %param.7) | copy-start | bytes 196
  0.0 0.7 %copy-start.4 = (s32[1,1,8,2]{2,3,1,0:T(2,128)S(1)}, s32[1,1,8,2]{2,3,1,0:T(2,128)}, u32[]{:S(2)}) copy-start(s32[1,1,8,2]{2,3,1,0:T(2,128)} %param.8) | copy-start | bytes 196
  0.0 0.7 %copy-start.2 = (s32[1,1,8,2]{2,3,1,0:T(2,128)S(1)}, s32[1,1,8,2]{2,3,1,0:T(2,128)}, u32[]{:S(2)}) copy-start(s32[1,1,8,2]{2,3,1,0:T(2,128)} %param.6) | copy-start | bytes 196
  0.7 4.1 %copy-start = (f32[2048,128]{1,0:T(8,128)S(1)}, f32[2048,128]{1,0:T(8,128)}, u32[]{:S(2)}) copy-start(f32[2048,128]{1,0:T(8,128)} %param.5) | copy-start | bytes 3145732
  0.7 4.1 %copy-start.1 = (s32[1,1,8,2,8,128]{5,4,3,2,1,0:T(8,128)S(1)}, s32[1,1,8,2,8,128]{5,4,3,2,1,0:T(8,128)}, u32[]{:S(2)}) copy-start(s32[1,1,8,2,8,128]{5,4,3,2,1,0:T(8,128)} %param.9) | copy-start | bytes 196612
  0.7 5.6 %collective-permute-start = (s32[2,8]{1,0:T(2,128)S(1)}, s32[2,8]{1,0:T(2,128)S(1)}, u32[]{:S(2)}, u32[]{:S(2)}) collective-permute-start(s32[2,8]{1,0:T(2,128)S(1)} %get-tuple-element.24), channel_id=1, source_target_pairs={{0,16},{4,20},{8,24},{12,28},{16,0},{20,4},{24,8},{28,12},{1,17},{... | collective-permute-start | bytes 200 | tf_op jit(solution)/shard_map/ppermute | solution.py:180
  5.1 7.6 %collective-permute-start.4 = (f32[4,2,8,128]{3,2,1,0:T(8,128)S(1)}, f32[4,2,8,128]{3,2,1,0:T(8,128)S(1)}, u32[]{:S(2)}, u32[]{:S(2)}) collective-permute-start(f32[4,2,8,128]{3,2,1,0:T(8,128)S(1)} %get-tuple-element.26), channel_id=1, source_target_pairs={{0,16},{4,20},{8,24},{12,28},{16,0},{20,4},{24,8},{28,12},{1,17},{... | collective-permute-start | bytes 98312 | tf_op jit(solution)/shard_map/ppermute | solution.py:180
  6.4 4.7 %collective-permute-start.1 = (s32[2,2,8]{2,1,0:T(2,128)S(1)}, s32[2,2,8]{2,1,0:T(2,128)S(1)}, u32[]{:S(2)}, u32[]{:S(2)}) collective-permute-start(s32[2,2,8]{2,1,0:T(2,128)S(1)} %pad_add_fusion.2.asked_ref), channel_id=1, source_target_pairs={{0,8},{4,12},{8,0},{12,4},{16,24},{20,28},{24,16},{28,20},{1,9},{5... | collective-permute-start | bytes 392 | tf_op jit(solution)/shard_map/ppermute | solution.py:180
  8.4 11.0 %collective-permute-start.3 = (f32[2,128,128]{2,1,0:T(8,128)S(1)}, f32[2,128,128]{2,1,0:T(8,128)S(1)}, u32[]{:S(2)}, u32[]{:S(2)}) collective-permute-start(f32[2,128,128]{2,1,0:T(8,128)S(1)} %shard_map.57.refs_3_), channel_id=1, source_target_pairs={{0,16},{4,20},{8,24},{12,28},{16,0},{20,4},{24,8},{28,12},{1,17},{... | collective-permute-start | bytes 393224 | tf_op jit(solution)/shard_map/ppermute | solution.py:180
  11.1 4.6 %collective-permute-start.2 = (s32[4,2,8]{2,1,0:T(2,128)S(1)}, s32[4,2,8]{2,1,0:T(2,128)S(1)}, u32[]{:S(2)}, u32[]{:S(2)}) collective-permute-start(s32[4,2,8]{2,1,0:T(2,128)S(1)} %pad_add_fusion.1.asked_ref), channel_id=1, source_target_pairs={{0,4},{4,0},{8,12},{12,8},{16,20},{20,16},{24,28},{28,24},{1,5},{5... | collective-permute-start | bytes 776 | tf_op jit(solution)/shard_map/ppermute | solution.py:180
  12.8 10.3 %collective-permute-start.5 = (f32[2,128,128]{2,1,0:T(8,128)S(1)}, f32[2,128,128]{2,1,0:T(8,128)S(1)}, u32[]{:S(2)}, u32[]{:S(2)}) collective-permute-start(f32[2,128,128]{2,1,0:T(8,128)S(1)} %get-tuple-element.27.refs_3_), channel_id=1, source_target_pairs={{0,24},{4,28},{8,16},{12,20},{16,8},{20,12},{24,0},{28,4},{1,25},{... | collective-permute-start | bytes 393224 | tf_op jit(solution)/shard_map/ppermute | solution.py:180
  15.7 11.4 %collective-permute-start.6 = (f32[2,144,128]{2,1,0:T(8,128)S(1)}, f32[2,144,128]{2,1,0:T(8,128)S(1)}, u32[]{:S(2)}, u32[]{:S(2)}) collective-permute-start(f32[2,144,128]{2,1,0:T(8,128)S(1)} %get-tuple-element.28.refs_6_), channel_id=1, source_target_pairs={{0,8},{4,12},{8,0},{12,4},{16,24},{20,28},{24,16},{28,20},{1,9},{5... | collective-permute-start | bytes 442376 | tf_op jit(solution)/shard_map/ppermute | solution.py:180
  15.8 13.6 %collective-permute-start.7 = (f32[2,144,128]{2,1,0:T(8,128)S(1)}, f32[2,144,128]{2,1,0:T(8,128)S(1)}, u32[]{:S(2)}, u32[]{:S(2)}) collective-permute-start(f32[2,144,128]{2,1,0:T(8,128)S(1)} %get-tuple-element.29.refs_3_), channel_id=1, source_target_pairs={{0,12},{4,8},{8,4},{12,0},{16,28},{20,24},{24,20},{28,16},{1,13},{... | collective-permute-start | bytes 442376 | tf_op jit(solution)/shard_map/ppermute | solution.py:180
  17.9 11.6 %collective-permute-start.8 = (f32[2,144,128]{2,1,0:T(8,128)S(1)}, f32[2,144,128]{2,1,0:T(8,128)S(1)}, u32[]{:S(2)}, u32[]{:S(2)}) collective-permute-start(f32[2,144,128]{2,1,0:T(8,128)S(1)} %get-tuple-element.30.refs_6_), channel_id=1, source_target_pairs={{0,4},{4,0},{8,12},{12,8},{16,20},{20,16},{24,28},{28,24},{1,5},{5... | collective-permute-start | bytes 442376 | tf_op jit(solution)/shard_map/ppermute | solution.py:180
  19.4 11.1 %collective-permute-start.9 = (f32[2,128,128]{2,1,0:T(8,128)S(1)}, f32[2,128,128]{2,1,0:T(8,128)S(1)}, u32[]{:S(2)}, u32[]{:S(2)}) collective-permute-start(f32[2,128,128]{2,1,0:T(8,128)S(1)} %get-tuple-element.31.refs_3_), channel_id=1, source_target_pairs={{0,28},{4,24},{8,20},{12,16},{16,12},{20,8},{24,4},{28,0},{1,29},{... | collective-permute-start | bytes 393224 | tf_op jit(solution)/shard_map/ppermute | solution.py:180
  23.1 11.4 %collective-permute-start.10 = (f32[2,128,128]{2,1,0:T(8,128)S(1)}, f32[2,128,128]{2,1,0:T(8,128)S(1)}, u32[]{:S(2)}, u32[]{:S(2)}) collective-permute-start(f32[2,128,128]{2,1,0:T(8,128)S(1)} %get-tuple-element.32.refs_3_), channel_id=1, source_target_pairs={{0,20},{4,16},{8,28},{12,24},{16,4},{20,0},{24,12},{28,8},{1,21},{... | collective-permute-start | bytes 393224 | tf_op jit(solution)/shard_map/ppermute | solution.py:180
  35.1 1.6 %collective-permute-start.12 = (f32[4,128,128]{2,1,0:T(8,128)S(1)}, f32[4,128,128]{2,1,0:T(8,128)S(1)}, u32[]{:S(2)}, u32[]{:S(2)}) collective-permute-start(f32[4,128,128]{2,1,0:T(8,128)S(1)} %get-tuple-element.36), channel_id=1, source_target_pairs={{0,1},{1,0},{2,3},{3,2},{4,5},{5,4},{6,7},{7,6},{8,9},{9,8},{10,11... | collective-permute-start | bytes 786440 | tf_op jit(solution)/shard_map/ppermute | solution.py:180
  35.2 3.1 %collective-permute-start.11 = (f32[4,128,128]{2,1,0:T(8,128)S(1)}, f32[4,128,128]{2,1,0:T(8,128)S(1)}, u32[]{:S(2)}, u32[]{:S(2)}) collective-permute-start(f32[4,128,128]{2,1,0:T(8,128)S(1)} %get-tuple-element.34), channel_id=1, source_target_pairs={{0,1},{1,0},{2,3},{3,2},{4,5},{5,4},{6,7},{7,6},{8,9},{9,8},{10,11... | collective-permute-start | bytes 786440 | tf_op jit(solution)/shard_map/ppermute | solution.py:180
  36.7 8.4 %collective-permute-start.13 = (f32[4,128,128]{2,1,0:T(8,128)S(1)}, f32[4,128,128]{2,1,0:T(8,128)S(1)}, u32[]{:S(2)}, u32[]{:S(2)}) collective-permute-start(f32[4,128,128]{2,1,0:T(8,128)S(1)} %add.10), channel_id=1, source_target_pairs={{0,2},{1,3},{2,0},{3,1},{4,6},{5,7},{6,4},{7,5},{8,10},{9,11},{10,... | collective-permute-start | bytes 786440 | tf_op jit(solution)/shard_map/ppermute | solution.py:180

commit v6 on v5

--- a/solution.py
+++ b/solution.py
@@ -83,37 +83,39 @@
     return jnp.where(low, target.T, target)
 
 
-def add_peer(shift, place, total_ref, ids_ref, asked_ref, coded_ref, sent_ref, message_ref, carrier_ref):
-    quarter = lax.axis_index("pairs") * (total_ref.shape[0] // lax.axis_size("pairs"))
-    tile = coded_ref.shape[-1]
+def peer_tiles(shift, place, ids_ref, asked_ref, coded_ref, sent_ref, message_ref, carrier_ref):
+    width = coded_ref.shape[-1]
+    tiles = []
     for slot, block in enumerate(own_blocks(shift, place, ids_ref, asked_ref)):
-        own = halves(sent_ref[slot, :tile])
-        other = halves(message_ref[slot, :tile])
+        own = halves(sent_ref[slot, :width])
+        other = halves(message_ref[slot, :width])
         target = slot_target(shift, coded_ref, carrier_ref, slot)
         residue = jax.nn.sigmoid(product(own, other, 1, 1)) - target
-        total_ref[block ^ quarter] += product(halves(residue), other, 1, 0)
-
-
-def tables_kernel(left_ref, right_ref, kind_ref, asked_ref, ids_ref, kinds_ref):
-    asked_ref[...] = right_ref[...]
-    ids_ref[0] = left_ref[...]
-    ids_ref[1] = right_ref[...]
-    kinds_ref[...] = kind_ref[...]
-
-
-def setup_kernel(kinds_ref, latent_ref, edges_ref, rows_ref, coded_ref, far_ref, ints_ref, sems):
+        tiles.append((block, product(halves(residue), other, 1, 0)))
+    return tiles
+
+
+def wait_kernel(target_ref):
+    target_ref[...] = jnp.zeros_like(target_ref)
+
+
+def setup_kernel(
+    waited_ref, left_ref, right_ref, kind_ref, latent_ref, edges_ref, rows_ref, ids_ref, coded_ref, far_ref, ints_ref, sems
+):
     copies = [
         pltpu.make_async_copy(source, target, sems.at[at])
         for at, (source, target) in enumerate(((edges_ref, ints_ref), (latent_ref, rows_ref)))
     ]
     for copy in copies:
         copy.start()
+    ids_ref[0] = left_ref[...]
+    ids_ref[1] = right_ref[...]
     copies[0].wait()
     peers, slots = edges_ref.shape[:2]
     for peer in range(peers):
         for slot in range(slots):
             edges = ints_ref[peer, slot].astype(F32)
-            kind = jnp.broadcast_to(kinds_ref[slot : slot + 1, peer : peer + 1], edges.shape)
+            kind = jnp.broadcast_to(kind_ref[slot : slot + 1, peer : peer + 1], edges.shape)
             coded_ref[peer, slot] = jnp.where(kind == 2, edges, -1.0)
     far_ref[...] = coded_ref[far_ref.shape[0] :]
     copies[1].wait()
@@ -133,8 +135,10 @@
 
 def add_peers(shifts, places, total_ref, *refs):
     fixed, refs = refs[:3], refs[3:]
+    quarter = lax.axis_index("pairs") * (total_ref.shape[0] // lax.axis_size("pairs"))
     for at, (shift, place) in enumerate(zip(shifts, places)):
-        add_peer(shift, place, total_ref, *fixed, *refs[3 * at : 3 * at + 3])
+        for block, tile in peer_tiles(shift, place, *fixed, *refs[3 * at : 3 * at + 3]):
+            total_ref[block ^ quarter] += tile
 
 
 def first_kernel(shifts, places, latent_ref, *refs):
@@ -151,25 +155,30 @@
     add_peers(shifts, places, total_ref, *refs)
 
 
-def last_kernel(shifts, places, before_ref, *refs):
-    count = 3 + 3 * len(shifts)
-    refs, part_refs, total_ref = refs[:count], refs[count:-1], refs[-1]
-    total_ref[...] = before_ref[...]
-    add_peers(shifts, places, total_ref, *refs)
+def last_kernel(shifts, places, before_ref, ids_ref, asked_ref, coded_ref, *refs):
+    count = 3 * len(shifts)
+    refs, part_refs = refs[:count], refs[count:]
+    tiles = []
+    for at, (shift, place) in enumerate(zip(shifts, places)):
+        tiles += peer_tiles(shift, place, ids_ref, asked_ref, coded_ref, *refs[3 * at : 3 * at + 3])
+    depth = part_refs[0].shape[0]
+    quarter = lax.axis_index("pairs") * depth
     for place, part_ref in enumerate(part_refs):
-        depth = part_ref.shape[0]
-        part_ref[...] = total_ref[place * depth : (place + 1) * depth]
+        part_ref[...] = before_ref[place * depth : (place + 1) * depth]
+        for block, tile in tiles:
+            at = (block ^ quarter) - place * depth
+
+            @pl.when((at >= 0) & (at < depth))
+            def add():
+                part_ref[at] += tile
 
 
 def shift_groups(peers):
     top = peers // 2
-    sequence, bit = [], top
-    while bit:
-        stage = [at for at in reversed(range(1, peers)) if at & -at == bit]
-        sequence += sorted(stage, key=lambda at: (at < top) != (bit == 1))
-        bit //= 2
-    middle = sequence[1:-2]
-    return [sequence[:1]] + [middle[at : at + 2] for at in range(0, len(middle), 2)] + [[at] for at in sequence[-2:]]
+    near = sorted(range(1, top), key=lambda at: (-(at & -at), -at))
+    groups = [[top]] + [[top + at, at] for at in near]
+    far, last = groups.pop()
+    return groups + [[last], [far]]
 
 
 def estimate(slots, width, moved):
@@ -191,39 +200,38 @@
 
     edges = edge_cols.reshape(peers, slots, lists, tile)
     top = peers // 2
-    small = jax.ShapeDtypeStruct((slots, peers), jnp.int32)
-    own_asked, ids, kinds = pl.pallas_call(
-        tables_kernel,
-        out_shape=(small, jax.ShapeDtypeStruct((2, slots, peers), jnp.int32), small),
-        in_specs=[VMEM] * 3,
-        out_specs=(VMEM,) * 3,
+    waited = pl.pallas_call(
+        wait_kernel,
+        out_shape=jax.ShapeDtypeStruct((8, 128), F32),
+        out_specs=VMEM,
         compiler_params=PARAMS,
         cost_estimate=pl.CostEstimate(flops=WAIT_FLOPS, bytes_accessed=4096, transcendentals=0),
-    )(table(left_block), table(right_block), table(slot_kind))
-    blocks, coded, far_coded = pl.pallas_call(
+    )()
+    blocks, ids, coded, far_coded = pl.pallas_call(
         setup_kernel,
         out_shape=(
             jax.ShapeDtypeStruct(blocks.shape, F32),
+            jax.ShapeDtypeStruct((2, slots, peers), jnp.int32),
             jax.ShapeDtypeStruct(edges.shape, F32),
             jax.ShapeDtypeStruct((top, *edges.shape[1:]), F32),
         ),
-        in_specs=[VMEM] + [HBM] * 2,
-        out_specs=(VMEM,) * 3,
+        in_specs=[VMEM] * 4 + [HBM] * 2,
+        out_specs=(VMEM,) * 4,
         scratch_shapes=[
             pltpu.VMEM(edges.shape, jnp.int32),
             pltpu.SemaphoreType.DMA((2,)),
         ],
         compiler_params=PARAMS,
-    )(kinds, blocks, edges)
+    )(waited, table(left_block), table(right_block), table(slot_kind), blocks, edges)
 
     passed = swap(far_coded, "rows", top)
     near_message = jax.ShapeDtypeStruct((slots, tile + 2 * lists, width), F32)
     far_message = jax.ShapeDtypeStruct((slots, tile, width), F32)
-    asked, where, leaving, arrived = own_asked, [0], {}, {}
+    asked, where, leaving, arrived = right_block, [0], {}, {}
     bit = top
     while bit:
         if len(where) == 1:
-            asked = jnp.concatenate([ids[1:], swap(asked, "rows", bit)[None]])
+            asked = jnp.concatenate([ids[1:], table(swap(asked, "rows", bit))[None]])
         else:
             asked = jnp.concatenate([asked, swap(asked, "rows", bit)])
         where = where + [at ^ bit for at in where]
@@ -257,7 +265,6 @@
             out_shape=[part] * parts if last else [whole],
             in_specs=[VMEM] * (4 + len(messages)),
             out_specs=[VMEM] * (parts if last else 1),
-            scratch_shapes=[pltpu.VMEM(blocks.shape, F32)] if last else [],
             input_output_aliases={} if first or last else {0: 0},
             compiler_params=PARAMS,
             cost_estimate=estimate(slots * len(group), tile, 3 * blocks.size * 4),

time: 46.1 us -> 45.5 us (0.987)
  waiting for transfers between devices: 12.5 us -> 11.5 us
  starting transfers between devices: 26.7 us -> 27.2 us
    ppermute x14, waiting for transfers between devices: 12.5 us -> 11.5 us  [swap(): lax.ppermute(value, axis, [(at, at ^ shift) for at in range(lax.axis_size...]
    ppermute x14, starting transfers between devices: 26.7 us -> 27.2 us  [swap(): lax.ppermute(value, axis, [(at, at ^ shift) for at in range(lax.axis_size...]
where the time goes in v6:
time: 45.5 us; the launch traced here: 45.4 us
  starting transfers between devices  27.2 us (60%)
  waiting for transfers between devices  11.5 us (25%)
  Pallas kernels  5.04 us (11%)
  other arithmetic  0.8 us (2%)
  local copies, waits for them, and re-layouts  0.7 us (2%)
    ppermute x14, starting transfers between devices, swap(): lax.ppermute(value, axis, [(at, at ^ shift) for at in range(lax.axis_size...  27.2 us
    ppermute x14, waiting for transfers between devices, swap(): lax.ppermute(value, axis, [(at, at ^ shift) for at in range(lax.axis_size...  11.5 us
    pallas_call x5, Pallas kernels, body(): pl.pallas_call(functools.partial(first_kernel if first else last_kernel i...  4.32 us
  transfers between devices with their start and end apart: 14, of which 4 were waited for; matrix products, arithmetic and copies ran while one was open for 0% of the time, Pallas kernels for 10%

profile of v6, /device:TPU:0, one launch (start us, length us, event | category | flops | bytes accessed | tf_op | source)
XLA Modules:
  0.0 45.4 jit_solution(5120041784457866524)
XLA Ops:
  0.0 0.0 copy-start
  0.0 0.0 copy-start.1
  0.0 4.0 %collective-permute-start = (s32[1,1,8,2]{2,3,1,0:T(2,128)}, s32[1,1,8,2]{2,3,1,0:T(2,128)S(1)}, u32[]{:S(2)}, u32[]{:S(2)}) collective-permute-start(s32[1,1,8,2]{2,3,1,0:T(2,128)} %param.7), channel_id=1, source_target_pairs={{0,16},{4,20},{8,24},{12,28},{16,0},{20,4},{24,8},{28,12},{1,17},{... | collective-permute-start | bytes 200 | tf_op jit(solution)/shard_map/ppermute | solution.py:189
  4.0 0.0 copy-start.3
  4.0 0.0 copy-start.4
  4.0 0.0 copy-start.2
  4.1 0.0 copy-done
  4.1 0.0 copy-done.1
  4.1 0.6 %copy-done.3 = s32[1,1,8,2]{2,3,1,0:T(2,128)S(1)} copy-done((s32[1,1,8,2]{2,3,1,0:T(2,128)S(1)}, s32[1,1,8,2]{2,3,1,0:T(2,128)}, u32[]{:S(2)}) %copy-start.3) | copy-done | bytes 88
  4.7 0.0 copy-done.4
  4.8 0.0 copy-done.2
  4.8 0.3 shard_map.56
  5.0 0.6 %collective-permute-start.4 = (f32[4,2,8,128]{3,2,1,0:T(8,128)S(1)}, f32[4,2,8,128]{3,2,1,0:T(8,128)S(1)}, u32[]{:S(2)}, u32[]{:S(2)}) collective-permute-start(f32[4,2,8,128]{3,2,1,0:T(8,128)S(1)} %get-tuple-element.22), channel_id=1, source_target_pairs={{0,16},{4,20},{8,24},{12,28},{16,0},{20,4},{24,8},{28,12},{1,17},{... | collective-permute-start | bytes 98312 | tf_op jit(solution)/shard_map/ppermute | solution.py:189
  5.7 0.1 collective-permute-done
  5.8 1.9 %collective-permute-start.1 = (s32[2,2,8]{2,1,0:T(2,128)S(1)}, s32[2,2,8]{2,1,0:T(2,128)S(1)}, u32[]{:S(2)}, u32[]{:S(2)}) collective-permute-start(s32[2,2,8]{2,1,0:T(2,128)S(1)} %pad_add_fusion.2.asked_ref), channel_id=1, source_target_pairs={{0,8},{4,12},{8,0},{12,4},{16,24},{20,28},{24,16},{28,20},{1,9},{5... | collective-permute-start | bytes 392 | tf_op jit(solution)/shard_map/ppermute | solution.py:189
  7.7 0.1 shard_map.57.refs_3_
  7.9 2.7 %collective-permute-start.3 = (f32[2,128,128]{2,1,0:T(8,128)S(1)}, f32[2,128,128]{2,1,0:T(8,128)S(1)}, u32[]{:S(2)}, u32[]{:S(2)}) collective-permute-start(f32[2,128,128]{2,1,0:T(8,128)S(1)} %shard_map.57.refs_3_), channel_id=1, source_target_pairs={{0,16},{4,20},{8,24},{12,28},{16,0},{20,4},{24,8},{28,12},{1,17},{... | collective-permute-start | bytes 393224 | tf_op jit(solution)/shard_map/ppermute | solution.py:189
  10.5 0.0 collective-permute-done.1
  10.5 1.6 %collective-permute-start.2 = (s32[4,2,8]{2,1,0:T(2,128)S(1)}, s32[4,2,8]{2,1,0:T(2,128)S(1)}, u32[]{:S(2)}, u32[]{:S(2)}) collective-permute-start(s32[4,2,8]{2,1,0:T(2,128)S(1)} %pad_add_fusion.1.asked_ref), channel_id=1, source_target_pairs={{0,4},{4,0},{8,12},{12,8},{16,20},{20,16},{24,28},{28,24},{1,5},{5... | collective-permute-start | bytes 776 | tf_op jit(solution)/shard_map/ppermute | solution.py:189
  12.1 0.0 collective-permute-done.4.refs_5_.passed_ref
  12.1 0.1 shard_map.59
  12.3 0.8 %collective-permute-start.6 = (f32[2,144,128]{2,1,0:T(8,128)S(1)}, f32[2,144,128]{2,1,0:T(8,128)S(1)}, u32[]{:S(2)}, u32[]{:S(2)}) collective-permute-start(f32[2,144,128]{2,1,0:T(8,128)S(1)} %get-tuple-element.24.refs_6_), channel_id=1, source_target_pairs={{0,8},{4,12},{8,0},{12,4},{16,24},{20,28},{24,16},{28,20},{1,9},{5... | collective-permute-start | bytes 442376 | tf_op jit(solution)/shard_map/ppermute | solution.py:189
  13.0 2.6 %collective-permute-start.5 = (f32[2,128,128]{2,1,0:T(8,128)S(1)}, f32[2,128,128]{2,1,0:T(8,128)S(1)}, u32[]{:S(2)}, u32[]{:S(2)}) collective-permute-start(f32[2,128,128]{2,1,0:T(8,128)S(1)} %get-tuple-element.23.refs_3_), channel_id=1, source_target_pairs={{0,24},{4,28},{8,16},{12,20},{16,8},{20,12},{24,0},{28,4},{1,25},{... | collective-permute-start | bytes 393224 | tf_op jit(solution)/shard_map/ppermute | solution.py:189
  15.6 0.0 collective-permute-done.2
  15.6 0.2 shard_map.61
  15.8 0.6 %collective-permute-start.8 = (f32[2,144,128]{2,1,0:T(8,128)S(1)}, f32[2,144,128]{2,1,0:T(8,128)S(1)}, u32[]{:S(2)}, u32[]{:S(2)}) collective-permute-start(f32[2,144,128]{2,1,0:T(8,128)S(1)} %get-tuple-element.26.refs_6_), channel_id=1, source_target_pairs={{0,12},{4,8},{8,4},{12,0},{16,28},{20,24},{24,20},{28,16},{1,13},{... | collective-permute-start | bytes 442376 | tf_op jit(solution)/shard_map/ppermute | solution.py:189
  16.4 1.5 %collective-permute-start.9 = (f32[2,144,128]{2,1,0:T(8,128)S(1)}, f32[2,144,128]{2,1,0:T(8,128)S(1)}, u32[]{:S(2)}, u32[]{:S(2)}) collective-permute-start(f32[2,144,128]{2,1,0:T(8,128)S(1)} %get-tuple-element.27.refs_3_), channel_id=1, source_target_pairs={{0,4},{4,0},{8,12},{12,8},{16,20},{20,16},{24,28},{28,24},{1,5},{5... | collective-permute-start | bytes 442376 | tf_op jit(solution)/shard_map/ppermute | solution.py:189
  17.9 0.0 collective-permute-done.3.refs_4_
  17.9 3.6 %collective-permute-start.7 = (f32[2,128,128]{2,1,0:T(8,128)S(1)}, f32[2,128,128]{2,1,0:T(8,128)S(1)}, u32[]{:S(2)}, u32[]{:S(2)}) collective-permute-start(f32[2,128,128]{2,1,0:T(8,128)S(1)} %get-tuple-element.25.refs_3_), channel_id=1, source_target_pairs={{0,28},{4,24},{8,20},{12,16},{16,12},{20,8},{24,4},{28,0},{1,29},{... | collective-permute-start | bytes 393224 | tf_op jit(solution)/shard_map/ppermute | solution.py:189
  21.5 0.0 collective-permute-done.5.refs_4_
  21.5 5.3 %collective-permute-start.10 = (f32[2,128,128]{2,1,0:T(8,128)S(1)}, f32[2,128,128]{2,1,0:T(8,128)S(1)}, u32[]{:S(2)}, u32[]{:S(2)}) collective-permute-start(f32[2,128,128]{2,1,0:T(8,128)S(1)} %get-tuple-element.28.refs_0_), channel_id=1, source_target_pairs={{0,20},{4,16},{8,28},{12,24},{16,4},{20,0},{24,12},{28,8},{1,21},{... | collective-permute-start | bytes 393224 | tf_op jit(solution)/shard_map/ppermute | solution.py:189
  26.8 0.9 %shard_map.58.before_ref = f32[16,128,128]{2,1,0:T(8,128)S(1)} custom-call(f32[16,128,128]{2,1,0:T(8,128)S(1)} %get-tuple-element.19.latent_ref, s32[2,2,8]{2,1,0:T(2,128)S(1)} %get-tuple-element.20.ids_ref.refs_0_, s32[8,2,8]{2,1,0:T(2,128)S(1)} %pad_add_fusion.refs_1_.asked_ref, f32[8,2,8,128]{3,2,1,0:T(8,128)S(1)} %get-tuple-element.21.coded_ref.refs_2_, ...), custom_call_target="tpu_custom_call" | custom-call | flops 50331648 | bytes 3145728 | tf_op jit(solution)/shard_map/pallas_call | solution.py:259
  27.7 0.0 collective-permute-done.6.refs_5_.refs_7_.refs_8_
  27.7 1.1 %shard_map.60.before_ref = f32[16,128,128]{2,1,0:T(8,128)S(1)} custom-call(f32[16,128,128]{2,1,0:T(8,128)S(1)} %shard_map.58.before_ref, s32[2,2,8]{2,1,0:T(2,128)S(1)} %get-tuple-element.20.ids_ref.refs_0_, s32[8,2,8]{2,1,0:T(2,128)S(1)} %pad_add_fusion.refs_1_.asked_ref, ...), custom_call_target="tpu_custom_call", output_to_operand_aliasing={{}: (0, {})} | custom-call | flops 100663296 | bytes 3145728 | tf_op jit(solution)/shard_map/pallas_call | solution.py:259
  28.8 0.0 collective-permute-done.7.refs_4_
  28.8 0.0 collective-permute-done.8.refs_5_.refs_7_.refs_8_
  28.8 1.1 %shard_map.62.before_ref = f32[16,128,128]{2,1,0:T(8,128)S(1)} custom-call(f32[16,128,128]{2,1,0:T(8,128)S(1)} %shard_map.60.before_ref, s32[2,2,8]{2,1,0:T(2,128)S(1)} %get-tuple-element.20.ids_ref.refs_0_, s32[8,2,8]{2,1,0:T(2,128)S(1)} %pad_add_fusion.refs_1_.asked_ref, ...), custom_call_target="tpu_custom_call", output_to_operand_aliasing={{}: (0, {})} | custom-call | flops 100663296 | bytes 3145728 | tf_op jit(solution)/shard_map/pallas_call | solution.py:259
  29.9 0.0 collective-permute-done.9.refs_4_.refs_5_.refs_2_
  29.9 0.6 %shard_map.63.before_ref = f32[16,128,128]{2,1,0:T(8,128)S(1)} custom-call(f32[16,128,128]{2,1,0:T(8,128)S(1)} %shard_map.62.before_ref, s32[2,2,8]{2,1,0:T(2,128)S(1)} %get-tuple-element.20.ids_ref.refs_0_, s32[8,2,8]{2,1,0:T(2,128)S(1)} %pad_add_fusion.refs_1_.asked_ref, ...), custom_call_target="tpu_custom_call", output_to_operand_aliasing={{}: (0, {})} | custom-call | flops 50331648 | bytes 3145728 | tf_op jit(solution)/shard_map/pallas_call | solution.py:259
  30.5 3.4 %collective-permute-done.10.refs_1_ = f32[2,128,128]{2,1,0:T(8,128)S(1)} collective-permute-done((f32[2,128,128]{2,1,0:T(8,128)S(1)}, f32[2,128,128]{2,1,0:T(8,128)S(1)}, u32[]{:S(2)}, u32[]{:S(2)}) %collective-permute-start.10) | collective-permute-done | bytes 131104 | tf_op jit(solution)/shard_map/ppermute | solution.py:189
  33.9 0.6 %shard_map.64 = (f32[4,128,128]{2,1,0:T(8,128)S(1)}, f32[4,128,128]{2,1,0:T(8,128)S(1)}, f32[4,128,128]{2,1,0:T(8,128)S(1)}, f32[4,128,128]{2,1,0:T(8,128)S(1)}) custom-call(f32[16,128,128]{2,1,0:T(8,128)S(1)} %shard_map.63.before_ref, s32[2,2,8]{2,1,0:T(2,128)S(1)} %get-tuple-element.20.ids_ref.refs_0_, s32[8,2,8]{2,1,0:T(2,128)S(1)} %pad_add_fusion.refs_1_.asked_ref, ...), custom_call_target="tpu_custom_call" | custom-call | flops 50331648 | bytes 3145728 | tf_op jit(solution)/shard_map/pallas_call | solution.py:259
  34.6 0.1 collective-permute-start.12
  34.7 0.5 %collective-permute-start.11 = (f32[4,128,128]{2,1,0:T(8,128)S(1)}, f32[4,128,128]{2,1,0:T(8,128)S(1)}, u32[]{:S(2)}, u32[]{:S(2)}) collective-permute-start(f32[4,128,128]{2,1,0:T(8,128)S(1)} %get-tuple-element.30), channel_id=1, source_target_pairs={{0,1},{1,0},{2,3},{3,2},{4,5},{5,4},{6,7},{7,6},{8,9},{9,8},{10,11... | collective-permute-start | bytes 786440 | tf_op jit(solution)/shard_map/ppermute | solution.py:189
  35.2 1.0 %collective-permute-done.12 = f32[4,128,128]{2,1,0:T(8,128)S(1)} collective-permute-done((f32[4,128,128]{2,1,0:T(8,128)S(1)}, f32[4,128,128]{2,1,0:T(8,128)S(1)}, u32[]{:S(2)}, u32[]{:S(2)}) %collective-permute-start.12) | collective-permute-done | bytes 262176 | tf_op jit(solution)/shard_map/ppermute | solution.py:189
  36.2 1.6 %collective-permute-start.13 = (f32[4,128,128]{2,1,0:T(8,128)S(1)}, f32[4,128,128]{2,1,0:T(8,128)S(1)}, u32[]{:S(2)}, u32[]{:S(2)}) collective-permute-start(f32[4,128,128]{2,1,0:T(8,128)S(1)} %add.10), channel_id=1, source_target_pairs={{0,2},{1,3},{2,0},{3,1},{4,6},{5,7},{6,4},{7,5},{8,10},{9,11},{10,... | collective-permute-start | bytes 786440 | tf_op jit(solution)/shard_map/ppermute | solution.py:189
  37.8 0.0 collective-permute-done.11
  37.8 6.9 %collective-permute-done.13 = f32[4,128,128]{2,1,0:T(8,128)S(1)} collective-permute-done((f32[4,128,128]{2,1,0:T(8,128)S(1)}, f32[4,128,128]{2,1,0:T(8,128)S(1)}, u32[]{:S(2)}, u32[]{:S(2)}) %collective-permute-start.13) | collective-permute-done | bytes 262176 | tf_op jit(solution)/shard_map/ppermute | solution.py:189
  44.6 0.8 %add_add_fusion = f32[4,128,128]{2,1,0:T(8,128)} fusion(f32[4,128,128]{2,1,0:T(8,128)S(1)} %collective-permute-done.13, f32[4,128,128]{2,1,0:T(8,128)S(1)} %get-tuple-element.29, f32[4,128,128]{2,1,0:T(8,128)S(1)} %collective-permute-done.11), kind=kLoop, calls=%fused_computation | loop fusion | flops 131072 | bytes 1048576 | tf_op jit(solution)/shard_map/add | solution.py:275
  (7 shorter events, 0.1 us)
Async XLA Ops:
  0.0 4.1 %copy-start = (f32[2048,128]{1,0:T(8,128)S(1)}, f32[2048,128]{1,0:T(8,128)}, u32[]{:S(2)}) copy-start(f32[2048,128]{1,0:T(8,128)} %param.5) | copy-start | bytes 3145732
  0.0 4.1 %copy-start.1 = (s32[1,1,8,2,8,128]{5,4,3,2,1,0:T(8,128)S(1)}, s32[1,1,8,2,8,128]{5,4,3,2,1,0:T(8,128)}, u32[]{:S(2)}) copy-start(s32[1,1,8,2,8,128]{5,4,3,2,1,0:T(8,128)} %param.9) | copy-start | bytes 196612
  0.0 5.8 %collective-permute-start = (s32[1,1,8,2]{2,3,1,0:T(2,128)}, s32[1,1,8,2]{2,3,1,0:T(2,128)S(1)}, u32[]{:S(2)}, u32[]{:S(2)}) collective-permute-start(s32[1,1,8,2]{2,3,1,0:T(2,128)} %param.7), channel_id=1, source_target_pairs={{0,16},{4,20},{8,24},{12,28},{16,0},{20,4},{24,8},{28,12},{1,17},{... | collective-permute-start | bytes 200 | tf_op jit(solution)/shard_map/ppermute | solution.py:189
  4.0 0.7 %copy-start.3 = (s32[1,1,8,2]{2,3,1,0:T(2,128)S(1)}, s32[1,1,8,2]{2,3,1,0:T(2,128)}, u32[]{:S(2)}) copy-start(s32[1,1,8,2]{2,3,1,0:T(2,128)} %param.8) | copy-start | bytes 196
  4.0 0.7 %copy-start.4 = (s32[1,1,8,2]{2,3,1,0:T(2,128)S(1)}, s32[1,1,8,2]{2,3,1,0:T(2,128)}, u32[]{:S(2)}) copy-start(s32[1,1,8,2]{2,3,1,0:T(2,128)} %param.7) | copy-start | bytes 196
  4.0 0.7 %copy-start.2 = (s32[1,1,8,2]{2,3,1,0:T(2,128)S(1)}, s32[1,1,8,2]{2,3,1,0:T(2,128)}, u32[]{:S(2)}) copy-start(s32[1,1,8,2]{2,3,1,0:T(2,128)} %param.6) | copy-start | bytes 196
  5.0 7.1 %collective-permute-start.4 = (f32[4,2,8,128]{3,2,1,0:T(8,128)S(1)}, f32[4,2,8,128]{3,2,1,0:T(8,128)S(1)}, u32[]{:S(2)}, u32[]{:S(2)}) collective-permute-start(f32[4,2,8,128]{3,2,1,0:T(8,128)S(1)} %get-tuple-element.22), channel_id=1, source_target_pairs={{0,16},{4,20},{8,24},{12,28},{16,0},{20,4},{24,8},{28,12},{1,17},{... | collective-permute-start | bytes 98312 | tf_op jit(solution)/shard_map/ppermute | solution.py:189
  5.8 4.7 %collective-permute-start.1 = (s32[2,2,8]{2,1,0:T(2,128)S(1)}, s32[2,2,8]{2,1,0:T(2,128)S(1)}, u32[]{:S(2)}, u32[]{:S(2)}) collective-permute-start(s32[2,2,8]{2,1,0:T(2,128)S(1)} %pad_add_fusion.2.asked_ref), channel_id=1, source_target_pairs={{0,8},{4,12},{8,0},{12,4},{16,24},{20,28},{24,16},{28,20},{1,9},{5... | collective-permute-start | bytes 392 | tf_op jit(solution)/shard_map/ppermute | solution.py:189
  7.9 10.1 %collective-permute-start.3 = (f32[2,128,128]{2,1,0:T(8,128)S(1)}, f32[2,128,128]{2,1,0:T(8,128)S(1)}, u32[]{:S(2)}, u32[]{:S(2)}) collective-permute-start(f32[2,128,128]{2,1,0:T(8,128)S(1)} %shard_map.57.refs_3_), channel_id=1, source_target_pairs={{0,16},{4,20},{8,24},{12,28},{16,0},{20,4},{24,8},{28,12},{1,17},{... | collective-permute-start | bytes 393224 | tf_op jit(solution)/shard_map/ppermute | solution.py:189
  10.5 5.1 %collective-permute-start.2 = (s32[4,2,8]{2,1,0:T(2,128)S(1)}, s32[4,2,8]{2,1,0:T(2,128)S(1)}, u32[]{:S(2)}, u32[]{:S(2)}) collective-permute-start(s32[4,2,8]{2,1,0:T(2,128)S(1)} %pad_add_fusion.1.asked_ref), channel_id=1, source_target_pairs={{0,4},{4,0},{8,12},{12,8},{16,20},{20,16},{24,28},{28,24},{1,5},{5... | collective-permute-start | bytes 776 | tf_op jit(solution)/shard_map/ppermute | solution.py:189
  12.3 15.4 %collective-permute-start.6 = (f32[2,144,128]{2,1,0:T(8,128)S(1)}, f32[2,144,128]{2,1,0:T(8,128)S(1)}, u32[]{:S(2)}, u32[]{:S(2)}) collective-permute-start(f32[2,144,128]{2,1,0:T(8,128)S(1)} %get-tuple-element.24.refs_6_), channel_id=1, source_target_pairs={{0,8},{4,12},{8,0},{12,4},{16,24},{20,28},{24,16},{28,20},{1,9},{5... | collective-permute-start | bytes 442376 | tf_op jit(solution)/shard_map/ppermute | solution.py:189
  13.0 8.4 %collective-permute-start.5 = (f32[2,128,128]{2,1,0:T(8,128)S(1)}, f32[2,128,128]{2,1,0:T(8,128)S(1)}, u32[]{:S(2)}, u32[]{:S(2)}) collective-permute-start(f32[2,128,128]{2,1,0:T(8,128)S(1)} %get-tuple-element.23.refs_3_), channel_id=1, source_target_pairs={{0,24},{4,28},{8,16},{12,20},{16,8},{20,12},{24,0},{28,4},{1,25},{... | collective-permute-start | bytes 393224 | tf_op jit(solution)/shard_map/ppermute | solution.py:189
  15.8 13.0 %collective-permute-start.8 = (f32[2,144,128]{2,1,0:T(8,128)S(1)}, f32[2,144,128]{2,1,0:T(8,128)S(1)}, u32[]{:S(2)}, u32[]{:S(2)}) collective-permute-start(f32[2,144,128]{2,1,0:T(8,128)S(1)} %get-tuple-element.26.refs_6_), channel_id=1, source_target_pairs={{0,12},{4,8},{8,4},{12,0},{16,28},{20,24},{24,20},{28,16},{1,13},{... | collective-permute-start | bytes 442376 | tf_op jit(solution)/shard_map/ppermute | solution.py:189
  16.4 13.5 %collective-permute-start.9 = (f32[2,144,128]{2,1,0:T(8,128)S(1)}, f32[2,144,128]{2,1,0:T(8,128)S(1)}, u32[]{:S(2)}, u32[]{:S(2)}) collective-permute-start(f32[2,144,128]{2,1,0:T(8,128)S(1)} %get-tuple-element.27.refs_3_), channel_id=1, source_target_pairs={{0,4},{4,0},{8,12},{12,8},{16,20},{20,16},{24,28},{28,24},{1,5},{5... | collective-permute-start | bytes 442376 | tf_op jit(solution)/shard_map/ppermute | solution.py:189
  17.9 10.8 %collective-permute-start.7 = (f32[2,128,128]{2,1,0:T(8,128)S(1)}, f32[2,128,128]{2,1,0:T(8,128)S(1)}, u32[]{:S(2)}, u32[]{:S(2)}) collective-permute-start(f32[2,128,128]{2,1,0:T(8,128)S(1)} %get-tuple-element.25.refs_3_), channel_id=1, source_target_pairs={{0,28},{4,24},{8,20},{12,16},{16,12},{20,8},{24,4},{28,0},{1,29},{... | collective-permute-start | bytes 393224 | tf_op jit(solution)/shard_map/ppermute | solution.py:189
  21.5 12.5 %collective-permute-start.10 = (f32[2,128,128]{2,1,0:T(8,128)S(1)}, f32[2,128,128]{2,1,0:T(8,128)S(1)}, u32[]{:S(2)}, u32[]{:S(2)}) collective-permute-start(f32[2,128,128]{2,1,0:T(8,128)S(1)} %get-tuple-element.28.refs_0_), channel_id=1, source_target_pairs={{0,20},{4,16},{8,28},{12,24},{16,4},{20,0},{24,12},{28,8},{1,21},{... | collective-permute-start | bytes 393224 | tf_op jit(solution)/shard_map/ppermute | solution.py:189
  34.6 1.6 %collective-permute-start.12 = (f32[4,128,128]{2,1,0:T(8,128)S(1)}, f32[4,128,128]{2,1,0:T(8,128)S(1)}, u32[]{:S(2)}, u32[]{:S(2)}) collective-permute-start(f32[4,128,128]{2,1,0:T(8,128)S(1)} %get-tuple-element.32), channel_id=1, source_target_pairs={{0,1},{1,0},{2,3},{3,2},{4,5},{5,4},{6,7},{7,6},{8,9},{9,8},{10,11... | collective-permute-start | bytes 786440 | tf_op jit(solution)/shard_map/ppermute | solution.py:189
  34.7 3.1 %collective-permute-start.11 = (f32[4,128,128]{2,1,0:T(8,128)S(1)}, f32[4,128,128]{2,1,0:T(8,128)S(1)}, u32[]{:S(2)}, u32[]{:S(2)}) collective-permute-start(f32[4,128,128]{2,1,0:T(8,128)S(1)} %get-tuple-element.30), channel_id=1, source_target_pairs={{0,1},{1,0},{2,3},{3,2},{4,5},{5,4},{6,7},{7,6},{8,9},{9,8},{10,11... | collective-permute-start | bytes 786440 | tf_op jit(solution)/shard_map/ppermute | solution.py:189
  36.2 8.4 %collective-permute-start.13 = (f32[4,128,128]{2,1,0:T(8,128)S(1)}, f32[4,128,128]{2,1,0:T(8,128)S(1)}, u32[]{:S(2)}, u32[]{:S(2)}) collective-permute-start(f32[4,128,128]{2,1,0:T(8,128)S(1)} %add.10), channel_id=1, source_target_pairs={{0,2},{1,3},{2,0},{3,1},{4,6},{5,7},{6,4},{7,5},{8,10},{9,11},{10,... | collective-permute-start | bytes 786440 | tf_op jit(solution)/shard_map/ppermute | solution.py:189

commit v7 on v6

--- a/solution.py
+++ b/solution.py
@@ -175,7 +175,7 @@
 
 def shift_groups(peers):
     top = peers // 2
-    near = sorted(range(1, top), key=lambda at: (-(at & -at), -at))
+    near = sorted(range(1, top), key=lambda at: (at.bit_length(), -at))
     groups = [[top]] + [[top + at, at] for at in near]
     far, last = groups.pop()
     return groups + [[last], [far]]
@@ -228,14 +228,13 @@
     near_message = jax.ShapeDtypeStruct((slots, tile + 2 * lists, width), F32)
     far_message = jax.ShapeDtypeStruct((slots, tile, width), F32)
     asked, where, leaving, arrived = right_block, [0], {}, {}
-    bit = top
-    while bit:
+    for bit in [top] + [1 << at for at in range(top.bit_length() - 1)]:
         if len(where) == 1:
             asked = jnp.concatenate([ids[1:], table(swap(asked, "rows", bit))[None]])
         else:
             asked = jnp.concatenate([asked, swap(asked, "rows", bit)])
         where = where + [at ^ bit for at in where]
-        shifts = [at for at in reversed(range(1, peers)) if at & -at == bit]
+        shifts = sorted(where[len(where) // 2 :], reverse=True)
         sent = pl.pallas_call(
             functools.partial(pack_kernel, shifts, [where.index(at) for at in shifts]),
             out_shape=[far_message if at >= top else near_message for at in shifts],
@@ -245,7 +244,6 @@
         )(ids, asked, blocks, coded, passed if bit < top else coded[:top])
         for shift, value in zip(shifts, sent):
             leaving[shift], arrived[shift] = value, swap(value, "rows", shift)
-        bit //= 2
 
     whole = jax.ShapeDtypeStruct(blocks.shape, F32)
     parts = lax.axis_size("pairs")

time: 45.5 us -> 44.4 us (0.976)
  starting transfers between devices: 27.2 us -> 25.9 us
    ppermute x14, starting transfers between devices: 27.2 us -> 25.9 us  [swap(): lax.ppermute(value, axis, [(at, at ^ shift) for at in range(lax.axis_size...]
  transfers between devices with their start and end apart: 14 -> 14, of which waited for: 4 -> 6; matrix products, arithmetic and copies ran while one was open for 0% -> 0% of each run, Pallas kernels for 10% -> 10%
where the time goes in v7:
time: 44.4 us; the launch traced here: 44.3 us
  starting transfers between devices  25.9 us (58%)
  waiting for transfers between devices  11.7 us (26%)
  Pallas kernels  5.04 us (11%)
  other arithmetic  0.8 us (2%)
  local copies, waits for them, and re-layouts  0.7 us (2%)
    ppermute x14, starting transfers between devices, swap(): lax.ppermute(value, axis, [(at, at ^ shift) for at in range(lax.axis_size...  25.9 us
    ppermute x14, waiting for transfers between devices, swap(): lax.ppermute(value, axis, [(at, at ^ shift) for at in range(lax.axis_size...  11.7 us
    pallas_call x5, Pallas kernels, body(): pl.pallas_call(functools.partial(first_kernel if first else last_kernel i...  4.32 us
  transfers between devices with their start and end apart: 14, of which 6 were waited for; matrix products, arithmetic and copies ran while one was open for 0% of the time, Pallas kernels for 10%

profile of v7, /device:TPU:0, one launch (start us, length us, event | category | flops | bytes accessed | tf_op | source)
XLA Modules:
  0.0 44.3 jit_solution(8600943283032989160)
XLA Ops:
  0.0 0.0 copy-start
  0.0 0.0 copy-start.1
  0.0 4.0 %collective-permute-start = (s32[1,1,8,2]{2,3,1,0:T(2,128)}, s32[1,1,8,2]{2,3,1,0:T(2,128)S(1)}, u32[]{:S(2)}, u32[]{:S(2)}) collective-permute-start(s32[1,1,8,2]{2,3,1,0:T(2,128)} %param.7), channel_id=1, source_target_pairs={{0,16},{4,20},{8,24},{12,28},{16,0},{20,4},{24,8},{28,12},{1,17},{... | collective-permute-start | bytes 200 | tf_op jit(solution)/shard_map/ppermute | solution.py:189
  4.0 0.0 copy-start.3
  4.0 0.0 copy-start.4
  4.0 0.0 copy-start.2
  4.1 0.0 copy-done
  4.1 0.0 copy-done.1
  4.1 0.6 %copy-done.3 = s32[1,1,8,2]{2,3,1,0:T(2,128)S(1)} copy-done((s32[1,1,8,2]{2,3,1,0:T(2,128)S(1)}, s32[1,1,8,2]{2,3,1,0:T(2,128)}, u32[]{:S(2)}) %copy-start.3) | copy-done | bytes 88
  4.7 0.0 copy-done.4
  4.8 0.0 copy-done.2
  4.8 0.3 shard_map.56
  5.0 0.6 %collective-permute-start.4 = (f32[4,2,8,128]{3,2,1,0:T(8,128)S(1)}, f32[4,2,8,128]{3,2,1,0:T(8,128)S(1)}, u32[]{:S(2)}, u32[]{:S(2)}) collective-permute-start(f32[4,2,8,128]{3,2,1,0:T(8,128)S(1)} %get-tuple-element.22), channel_id=1, source_target_pairs={{0,16},{4,20},{8,24},{12,28},{16,0},{20,4},{24,8},{28,12},{1,17},{... | collective-permute-start | bytes 98312 | tf_op jit(solution)/shard_map/ppermute | solution.py:189
  5.7 0.1 collective-permute-done
  5.8 1.9 %collective-permute-start.1 = (s32[2,2,8]{2,1,0:T(2,128)S(1)}, s32[2,2,8]{2,1,0:T(2,128)S(1)}, u32[]{:S(2)}, u32[]{:S(2)}) collective-permute-start(s32[2,2,8]{2,1,0:T(2,128)S(1)} %pad_add_fusion.2.asked_ref), channel_id=1, source_target_pairs={{0,4},{4,0},{8,12},{12,8},{16,20},{20,16},{24,28},{28,24},{1,5},{5... | collective-permute-start | bytes 392 | tf_op jit(solution)/shard_map/ppermute | solution.py:189
  7.7 0.1 shard_map.57.refs_3_
  7.8 2.7 %collective-permute-start.3 = (f32[2,128,128]{2,1,0:T(8,128)S(1)}, f32[2,128,128]{2,1,0:T(8,128)S(1)}, u32[]{:S(2)}, u32[]{:S(2)}) collective-permute-start(f32[2,128,128]{2,1,0:T(8,128)S(1)} %shard_map.57.refs_3_), channel_id=1, source_target_pairs={{0,16},{4,20},{8,24},{12,28},{16,0},{20,4},{24,8},{28,12},{1,17},{... | collective-permute-start | bytes 393224 | tf_op jit(solution)/shard_map/ppermute | solution.py:189
  10.5 0.0 collective-permute-done.1
  10.5 1.6 %collective-permute-start.2 = (s32[4,2,8]{2,1,0:T(2,128)S(1)}, s32[4,2,8]{2,1,0:T(2,128)S(1)}, u32[]{:S(2)}, u32[]{:S(2)}) collective-permute-start(s32[4,2,8]{2,1,0:T(2,128)S(1)} %pad_add_fusion.1.asked_ref), channel_id=1, source_target_pairs={{0,8},{4,12},{8,0},{12,4},{16,24},{20,28},{24,16},{28,20},{1,9},{5... | collective-permute-start | bytes 776 | tf_op jit(solution)/shard_map/ppermute | solution.py:189
  12.1 0.0 collective-permute-done.4.refs_5_.passed_ref
  12.1 0.1 shard_map.59
  12.3 0.8 %collective-permute-start.6 = (f32[2,144,128]{2,1,0:T(8,128)S(1)}, f32[2,144,128]{2,1,0:T(8,128)S(1)}, u32[]{:S(2)}, u32[]{:S(2)}) collective-permute-start(f32[2,144,128]{2,1,0:T(8,128)S(1)} %get-tuple-element.24.refs_6_), channel_id=1, source_target_pairs={{0,4},{4,0},{8,12},{12,8},{16,20},{20,16},{24,28},{28,24},{1,5},{5... | collective-permute-start | bytes 442376 | tf_op jit(solution)/shard_map/ppermute | solution.py:189
  13.0 2.5 %collective-permute-start.5 = (f32[2,128,128]{2,1,0:T(8,128)S(1)}, f32[2,128,128]{2,1,0:T(8,128)S(1)}, u32[]{:S(2)}, u32[]{:S(2)}) collective-permute-start(f32[2,128,128]{2,1,0:T(8,128)S(1)} %get-tuple-element.23.refs_3_), channel_id=1, source_target_pairs={{0,20},{4,16},{8,28},{12,24},{16,4},{20,0},{24,12},{28,8},{1,21},{... | collective-permute-start | bytes 393224 | tf_op jit(solution)/shard_map/ppermute | solution.py:189
  15.6 0.0 collective-permute-done.2
  15.6 0.2 shard_map.61
  15.8 1.5 %collective-permute-start.8 = (f32[2,144,128]{2,1,0:T(8,128)S(1)}, f32[2,144,128]{2,1,0:T(8,128)S(1)}, u32[]{:S(2)}, u32[]{:S(2)}) collective-permute-start(f32[2,144,128]{2,1,0:T(8,128)S(1)} %get-tuple-element.26.refs_6_), channel_id=1, source_target_pairs={{0,12},{4,8},{8,4},{12,0},{16,28},{20,24},{24,20},{28,16},{1,13},{... | collective-permute-start | bytes 442376 | tf_op jit(solution)/shard_map/ppermute | solution.py:189
  17.2 1.6 %collective-permute-start.9 = (f32[2,144,128]{2,1,0:T(8,128)S(1)}, f32[2,144,128]{2,1,0:T(8,128)S(1)}, u32[]{:S(2)}, u32[]{:S(2)}) collective-permute-start(f32[2,144,128]{2,1,0:T(8,128)S(1)} %get-tuple-element.27.refs_3_), channel_id=1, source_target_pairs={{0,8},{4,12},{8,0},{12,4},{16,24},{20,28},{24,16},{28,20},{1,9},{5... | collective-permute-start | bytes 442376 | tf_op jit(solution)/shard_map/ppermute | solution.py:189
  18.8 0.0 collective-permute-done.3.refs_4_
  18.8 2.8 %collective-permute-start.7 = (f32[2,128,128]{2,1,0:T(8,128)S(1)}, f32[2,128,128]{2,1,0:T(8,128)S(1)}, u32[]{:S(2)}, u32[]{:S(2)}) collective-permute-start(f32[2,128,128]{2,1,0:T(8,128)S(1)} %get-tuple-element.25.refs_3_), channel_id=1, source_target_pairs={{0,28},{4,24},{8,20},{12,16},{16,12},{20,8},{24,4},{28,0},{1,29},{... | collective-permute-start | bytes 393224 | tf_op jit(solution)/shard_map/ppermute | solution.py:189
  21.6 1.7 %collective-permute-done.5.refs_4_ = f32[2,128,128]{2,1,0:T(8,128)S(1)} collective-permute-done((f32[2,128,128]{2,1,0:T(8,128)S(1)}, f32[2,128,128]{2,1,0:T(8,128)S(1)}, u32[]{:S(2)}, u32[]{:S(2)}) %collective-permute-start.5) | collective-permute-done | bytes 131104 | tf_op jit(solution)/shard_map/ppermute | solution.py:189
  23.3 3.8 %collective-permute-start.10 = (f32[2,128,128]{2,1,0:T(8,128)S(1)}, f32[2,128,128]{2,1,0:T(8,128)S(1)}, u32[]{:S(2)}, u32[]{:S(2)}) collective-permute-start(f32[2,128,128]{2,1,0:T(8,128)S(1)} %get-tuple-element.28.refs_0_), channel_id=1, source_target_pairs={{0,24},{4,28},{8,16},{12,20},{16,8},{20,12},{24,0},{28,4},{1,25},{... | collective-permute-start | bytes 393224 | tf_op jit(solution)/shard_map/ppermute | solution.py:189
  27.2 0.9 %shard_map.58.before_ref = f32[16,128,128]{2,1,0:T(8,128)S(1)} custom-call(f32[16,128,128]{2,1,0:T(8,128)S(1)} %get-tuple-element.19.latent_ref, s32[2,2,8]{2,1,0:T(2,128)S(1)} %get-tuple-element.20.ids_ref.refs_0_, s32[8,2,8]{2,1,0:T(2,128)S(1)} %pad_add_fusion.refs_1_.asked_ref, f32[8,2,8,128]{3,2,1,0:T(8,128)S(1)} %get-tuple-element.21.coded_ref.refs_2_, ...), custom_call_target="tpu_custom_call" | custom-call | flops 50331648 | bytes 3145728 | tf_op jit(solution)/shard_map/pallas_call | solution.py:257
  28.1 0.0 collective-permute-done.6.refs_5_.refs_7_.refs_8_
  28.1 1.1 %shard_map.60.before_ref = f32[16,128,128]{2,1,0:T(8,128)S(1)} custom-call(f32[16,128,128]{2,1,0:T(8,128)S(1)} %shard_map.58.before_ref, s32[2,2,8]{2,1,0:T(2,128)S(1)} %get-tuple-element.20.ids_ref.refs_0_, s32[8,2,8]{2,1,0:T(2,128)S(1)} %pad_add_fusion.refs_1_.asked_ref, ...), custom_call_target="tpu_custom_call", output_to_operand_aliasing={{}: (0, {})} | custom-call | flops 100663296 | bytes 3145728 | tf_op jit(solution)/shard_map/pallas_call | solution.py:257
  29.2 0.2 collective-permute-done.7.refs_4_
  29.4 0.0 collective-permute-done.8.refs_5_.refs_7_.refs_8_
  29.4 1.1 %shard_map.62.before_ref = f32[16,128,128]{2,1,0:T(8,128)S(1)} custom-call(f32[16,128,128]{2,1,0:T(8,128)S(1)} %shard_map.60.before_ref, s32[2,2,8]{2,1,0:T(2,128)S(1)} %get-tuple-element.20.ids_ref.refs_0_, s32[8,2,8]{2,1,0:T(2,128)S(1)} %pad_add_fusion.refs_1_.asked_ref, ...), custom_call_target="tpu_custom_call", output_to_operand_aliasing={{}: (0, {})} | custom-call | flops 100663296 | bytes 3145728 | tf_op jit(solution)/shard_map/pallas_call | solution.py:257
  30.5 1.7 %collective-permute-done.9.refs_4_.refs_5_.refs_2_ = f32[2,144,128]{2,1,0:T(8,128)S(1)} collective-permute-done((f32[2,144,128]{2,1,0:T(8,128)S(1)}, f32[2,144,128]{2,1,0:T(8,128)S(1)}, u32[]{:S(2)}, u32[]{:S(2)}) %collective-permute-start.9) | collective-permute-done | bytes 147488 | tf_op jit(solution)/shard_map/ppermute | solution.py:189
  32.2 0.6 %shard_map.63.before_ref = f32[16,128,128]{2,1,0:T(8,128)S(1)} custom-call(f32[16,128,128]{2,1,0:T(8,128)S(1)} %shard_map.62.before_ref, s32[2,2,8]{2,1,0:T(2,128)S(1)} %get-tuple-element.20.ids_ref.refs_0_, s32[8,2,8]{2,1,0:T(2,128)S(1)} %pad_add_fusion.refs_1_.asked_ref, ...), custom_call_target="tpu_custom_call", output_to_operand_aliasing={{}: (0, {})} | custom-call | flops 50331648 | bytes 3145728 | tf_op jit(solution)/shard_map/pallas_call | solution.py:257
  32.8 0.0 collective-permute-done.10.refs_1_
  32.8 0.6 %shard_map.64 = (f32[4,128,128]{2,1,0:T(8,128)S(1)}, f32[4,128,128]{2,1,0:T(8,128)S(1)}, f32[4,128,128]{2,1,0:T(8,128)S(1)}, f32[4,128,128]{2,1,0:T(8,128)S(1)}) custom-call(f32[16,128,128]{2,1,0:T(8,128)S(1)} %shard_map.63.before_ref, s32[2,2,8]{2,1,0:T(2,128)S(1)} %get-tuple-element.20.ids_ref.refs_0_, s32[8,2,8]{2,1,0:T(2,128)S(1)} %pad_add_fusion.refs_1_.asked_ref, ...), custom_call_target="tpu_custom_call" | custom-call | flops 50331648 | bytes 3145728 | tf_op jit(solution)/shard_map/pallas_call | solution.py:257
  33.5 0.1 collective-permute-start.12
  33.6 0.5 %collective-permute-start.11 = (f32[4,128,128]{2,1,0:T(8,128)S(1)}, f32[4,128,128]{2,1,0:T(8,128)S(1)}, u32[]{:S(2)}, u32[]{:S(2)}) collective-permute-start(f32[4,128,128]{2,1,0:T(8,128)S(1)} %get-tuple-element.30), channel_id=1, source_target_pairs={{0,1},{1,0},{2,3},{3,2},{4,5},{5,4},{6,7},{7,6},{8,9},{9,8},{10,11... | collective-permute-start | bytes 786440 | tf_op jit(solution)/shard_map/ppermute | solution.py:189
  34.0 1.0 %collective-permute-done.12 = f32[4,128,128]{2,1,0:T(8,128)S(1)} collective-permute-done((f32[4,128,128]{2,1,0:T(8,128)S(1)}, f32[4,128,128]{2,1,0:T(8,128)S(1)}, u32[]{:S(2)}, u32[]{:S(2)}) %collective-permute-start.12) | collective-permute-done | bytes 262176 | tf_op jit(solution)/shard_map/ppermute | solution.py:189
  35.1 1.6 %collective-permute-start.13 = (f32[4,128,128]{2,1,0:T(8,128)S(1)}, f32[4,128,128]{2,1,0:T(8,128)S(1)}, u32[]{:S(2)}, u32[]{:S(2)}) collective-permute-start(f32[4,128,128]{2,1,0:T(8,128)S(1)} %add.10), channel_id=1, source_target_pairs={{0,2},{1,3},{2,0},{3,1},{4,6},{5,7},{6,4},{7,5},{8,10},{9,11},{10,... | collective-permute-start | bytes 786440 | tf_op jit(solution)/shard_map/ppermute | solution.py:189
  36.7 0.0 collective-permute-done.11
  36.7 6.9 %collective-permute-done.13 = f32[4,128,128]{2,1,0:T(8,128)S(1)} collective-permute-done((f32[4,128,128]{2,1,0:T(8,128)S(1)}, f32[4,128,128]{2,1,0:T(8,128)S(1)}, u32[]{:S(2)}, u32[]{:S(2)}) %collective-permute-start.13) | collective-permute-done | bytes 262176 | tf_op jit(solution)/shard_map/ppermute | solution.py:189
  43.5 0.8 %add_add_fusion = f32[4,128,128]{2,1,0:T(8,128)} fusion(f32[4,128,128]{2,1,0:T(8,128)S(1)} %collective-permute-done.13, f32[4,128,128]{2,1,0:T(8,128)S(1)} %get-tuple-element.29, f32[4,128,128]{2,1,0:T(8,128)S(1)} %collective-permute-done.11), kind=kLoop, calls=%fused_computation | loop fusion | flops 131072 | bytes 1048576 | tf_op jit(solution)/shard_map/add | solution.py:273
  (7 shorter events, 0.1 us)
Async XLA Ops:
  0.0 4.1 %copy-start = (f32[2048,128]{1,0:T(8,128)S(1)}, f32[2048,128]{1,0:T(8,128)}, u32[]{:S(2)}) copy-start(f32[2048,128]{1,0:T(8,128)} %param.5) | copy-start | bytes 3145732
  0.0 4.1 %copy-start.1 = (s32[1,1,8,2,8,128]{5,4,3,2,1,0:T(8,128)S(1)}, s32[1,1,8,2,8,128]{5,4,3,2,1,0:T(8,128)}, u32[]{:S(2)}) copy-start(s32[1,1,8,2,8,128]{5,4,3,2,1,0:T(8,128)} %param.9) | copy-start | bytes 196612
  0.0 5.8 %collective-permute-start = (s32[1,1,8,2]{2,3,1,0:T(2,128)}, s32[1,1,8,2]{2,3,1,0:T(2,128)S(1)}, u32[]{:S(2)}, u32[]{:S(2)}) collective-permute-start(s32[1,1,8,2]{2,3,1,0:T(2,128)} %param.7), channel_id=1, source_target_pairs={{0,16},{4,20},{8,24},{12,28},{16,0},{20,4},{24,8},{28,12},{1,17},{... | collective-permute-start | bytes 200 | tf_op jit(solution)/shard_map/ppermute | solution.py:189
  4.0 0.7 %copy-start.3 = (s32[1,1,8,2]{2,3,1,0:T(2,128)S(1)}, s32[1,1,8,2]{2,3,1,0:T(2,128)}, u32[]{:S(2)}) copy-start(s32[1,1,8,2]{2,3,1,0:T(2,128)} %param.8) | copy-start | bytes 196
  4.0 0.7 %copy-start.4 = (s32[1,1,8,2]{2,3,1,0:T(2,128)S(1)}, s32[1,1,8,2]{2,3,1,0:T(2,128)}, u32[]{:S(2)}) copy-start(s32[1,1,8,2]{2,3,1,0:T(2,128)} %param.7) | copy-start | bytes 196
  4.0 0.7 %copy-start.2 = (s32[1,1,8,2]{2,3,1,0:T(2,128)S(1)}, s32[1,1,8,2]{2,3,1,0:T(2,128)}, u32[]{:S(2)}) copy-start(s32[1,1,8,2]{2,3,1,0:T(2,128)} %param.6) | copy-start | bytes 196
  5.0 7.1 %collective-permute-start.4 = (f32[4,2,8,128]{3,2,1,0:T(8,128)S(1)}, f32[4,2,8,128]{3,2,1,0:T(8,128)S(1)}, u32[]{:S(2)}, u32[]{:S(2)}) collective-permute-start(f32[4,2,8,128]{3,2,1,0:T(8,128)S(1)} %get-tuple-element.22), channel_id=1, source_target_pairs={{0,16},{4,20},{8,24},{12,28},{16,0},{20,4},{24,8},{28,12},{1,17},{... | collective-permute-start | bytes 98312 | tf_op jit(solution)/shard_map/ppermute | solution.py:189
  5.8 4.7 %collective-permute-start.1 = (s32[2,2,8]{2,1,0:T(2,128)S(1)}, s32[2,2,8]{2,1,0:T(2,128)S(1)}, u32[]{:S(2)}, u32[]{:S(2)}) collective-permute-start(s32[2,2,8]{2,1,0:T(2,128)S(1)} %pad_add_fusion.2.asked_ref), channel_id=1, source_target_pairs={{0,4},{4,0},{8,12},{12,8},{16,20},{20,16},{24,28},{28,24},{1,5},{5... | collective-permute-start | bytes 392 | tf_op jit(solution)/shard_map/ppermute | solution.py:189
  7.8 11.0 %collective-permute-start.3 = (f32[2,128,128]{2,1,0:T(8,128)S(1)}, f32[2,128,128]{2,1,0:T(8,128)S(1)}, u32[]{:S(2)}, u32[]{:S(2)}) collective-permute-start(f32[2,128,128]{2,1,0:T(8,128)S(1)} %shard_map.57.refs_3_), channel_id=1, source_target_pairs={{0,16},{4,20},{8,24},{12,28},{16,0},{20,4},{24,8},{28,12},{1,17},{... | collective-permute-start | bytes 393224 | tf_op jit(solution)/shard_map/ppermute | solution.py:189
  10.5 5.1 %collective-permute-start.2 = (s32[4,2,8]{2,1,0:T(2,128)S(1)}, s32[4,2,8]{2,1,0:T(2,128)S(1)}, u32[]{:S(2)}, u32[]{:S(2)}) collective-permute-start(s32[4,2,8]{2,1,0:T(2,128)S(1)} %pad_add_fusion.1.asked_ref), channel_id=1, source_target_pairs={{0,8},{4,12},{8,0},{12,4},{16,24},{20,28},{24,16},{28,20},{1,9},{5... | collective-permute-start | bytes 776 | tf_op jit(solution)/shard_map/ppermute | solution.py:189
  12.3 15.8 %collective-permute-start.6 = (f32[2,144,128]{2,1,0:T(8,128)S(1)}, f32[2,144,128]{2,1,0:T(8,128)S(1)}, u32[]{:S(2)}, u32[]{:S(2)}) collective-permute-start(f32[2,144,128]{2,1,0:T(8,128)S(1)} %get-tuple-element.24.refs_6_), channel_id=1, source_target_pairs={{0,4},{4,0},{8,12},{12,8},{16,20},{20,16},{24,28},{28,24},{1,5},{5... | collective-permute-start | bytes 442376 | tf_op jit(solution)/shard_map/ppermute | solution.py:189
  13.0 10.3 %collective-permute-start.5 = (f32[2,128,128]{2,1,0:T(8,128)S(1)}, f32[2,128,128]{2,1,0:T(8,128)S(1)}, u32[]{:S(2)}, u32[]{:S(2)}) collective-permute-start(f32[2,128,128]{2,1,0:T(8,128)S(1)} %get-tuple-element.23.refs_3_), channel_id=1, source_target_pairs={{0,20},{4,16},{8,28},{12,24},{16,4},{20,0},{24,12},{28,8},{1,21},{... | collective-permute-start | bytes 393224 | tf_op jit(solution)/shard_map/ppermute | solution.py:189
  15.8 13.6 %collective-permute-start.8 = (f32[2,144,128]{2,1,0:T(8,128)S(1)}, f32[2,144,128]{2,1,0:T(8,128)S(1)}, u32[]{:S(2)}, u32[]{:S(2)}) collective-permute-start(f32[2,144,128]{2,1,0:T(8,128)S(1)} %get-tuple-element.26.refs_6_), channel_id=1, source_target_pairs={{0,12},{4,8},{8,4},{12,0},{16,28},{20,24},{24,20},{28,16},{1,13},{... | collective-permute-start | bytes 442376 | tf_op jit(solution)/shard_map/ppermute | solution.py:189
  17.2 14.9 %collective-permute-start.9 = (f32[2,144,128]{2,1,0:T(8,128)S(1)}, f32[2,144,128]{2,1,0:T(8,128)S(1)}, u32[]{:S(2)}, u32[]{:S(2)}) collective-permute-start(f32[2,144,128]{2,1,0:T(8,128)S(1)} %get-tuple-element.27.refs_3_), channel_id=1, source_target_pairs={{0,8},{4,12},{8,0},{12,4},{16,24},{20,28},{24,16},{28,20},{1,9},{5... | collective-permute-start | bytes 442376 | tf_op jit(solution)/shard_map/ppermute | solution.py:189
  18.8 10.6 %collective-permute-start.7 = (f32[2,128,128]{2,1,0:T(8,128)S(1)}, f32[2,128,128]{2,1,0:T(8,128)S(1)}, u32[]{:S(2)}, u32[]{:S(2)}) collective-permute-start(f32[2,128,128]{2,1,0:T(8,128)S(1)} %get-tuple-element.25.refs_3_), channel_id=1, source_target_pairs={{0,28},{4,24},{8,20},{12,16},{16,12},{20,8},{24,4},{28,0},{1,29},{... | collective-permute-start | bytes 393224 | tf_op jit(solution)/shard_map/ppermute | solution.py:189
  23.3 9.5 %collective-permute-start.10 = (f32[2,128,128]{2,1,0:T(8,128)S(1)}, f32[2,128,128]{2,1,0:T(8,128)S(1)}, u32[]{:S(2)}, u32[]{:S(2)}) collective-permute-start(f32[2,128,128]{2,1,0:T(8,128)S(1)} %get-tuple-element.28.refs_0_), channel_id=1, source_target_pairs={{0,24},{4,28},{8,16},{12,20},{16,8},{20,12},{24,0},{28,4},{1,25},{... | collective-permute-start | bytes 393224 | tf_op jit(solution)/shard_map/ppermute | solution.py:189
  33.5 1.6 %collective-permute-start.12 = (f32[4,128,128]{2,1,0:T(8,128)S(1)}, f32[4,128,128]{2,1,0:T(8,128)S(1)}, u32[]{:S(2)}, u32[]{:S(2)}) collective-permute-start(f32[4,128,128]{2,1,0:T(8,128)S(1)} %get-tuple-element.32), channel_id=1, source_target_pairs={{0,1},{1,0},{2,3},{3,2},{4,5},{5,4},{6,7},{7,6},{8,9},{9,8},{10,11... | collective-permute-start | bytes 786440 | tf_op jit(solution)/shard_map/ppermute | solution.py:189
  33.6 3.1 %collective-permute-start.11 = (f32[4,128,128]{2,1,0:T(8,128)S(1)}, f32[4,128,128]{2,1,0:T(8,128)S(1)}, u32[]{:S(2)}, u32[]{:S(2)}) collective-permute-start(f32[4,128,128]{2,1,0:T(8,128)S(1)} %get-tuple-element.30), channel_id=1, source_target_pairs={{0,1},{1,0},{2,3},{3,2},{4,5},{5,4},{6,7},{7,6},{8,9},{9,8},{10,11... | collective-permute-start | bytes 786440 | tf_op jit(solution)/shard_map/ppermute | solution.py:189
  35.1 8.4 %collective-permute-start.13 = (f32[4,128,128]{2,1,0:T(8,128)S(1)}, f32[4,128,128]{2,1,0:T(8,128)S(1)}, u32[]{:S(2)}, u32[]{:S(2)}) collective-permute-start(f32[4,128,128]{2,1,0:T(8,128)S(1)} %add.10), channel_id=1, source_target_pairs={{0,2},{1,3},{2,0},{3,1},{4,6},{5,7},{6,4},{7,5},{8,10},{9,11},{10,... | collective-permute-start | bytes 786440 | tf_op jit(solution)/shard_map/ppermute | solution.py:189

commit v8 on v7

--- a/solution.py
+++ b/solution.py
@@ -175,10 +175,8 @@
 
 def shift_groups(peers):
     top = peers // 2
-    near = sorted(range(1, top), key=lambda at: (at.bit_length(), -at))
-    groups = [[top]] + [[top + at, at] for at in near]
-    far, last = groups.pop()
-    return groups + [[last], [far]]
+    near = sorted(range(1, top), key=lambda at: (at.bit_length(), at))
+    return [[top]] + [[top + at, at] for at in near]
 
 
 def estimate(slots, width, moved):
@@ -234,7 +232,7 @@
         else:
             asked = jnp.concatenate([asked, swap(asked, "rows", bit)])
         where = where + [at ^ bit for at in where]
-        shifts = sorted(where[len(where) // 2 :], reverse=True)
+        shifts = sorted(where[len(where) // 2 :])
         sent = pl.pallas_call(
             functools.partial(pack_kernel, shifts, [where.index(at) for at in shifts]),
             out_shape=[far_message if at >= top else near_message for at in shifts],

time: 44.4 us -> 44.3 us (level)
  starting transfers between devices: 25.9 us -> 27.2 us
  waiting for transfers between devices: 11.7 us -> 10.5 us
    ppermute x14, starting transfers between devices: 25.9 us -> 27.2 us  [swap(): lax.ppermute(value, axis, [(at, at ^ shift) for at in range(lax.axis_size...]
    ppermute x14, waiting for transfers between devices: 11.7 us -> 10.5 us  [swap(): lax.ppermute(value, axis, [(at, at ^ shift) for at in range(lax.axis_size...]
    pallas_call x5 -> x4, Pallas kernels: 4.32 us -> 4.14 us  [body(): pl.pallas_call(functools.partial(first_kernel if first else last_kernel i...]
  transfers between devices with their start and end apart: 14 -> 14, of which waited for: 6 -> 6; matrix products, arithmetic and copies ran while one was open for 0% -> 0% of each run, Pallas kernels for 10% -> 9%
where the time goes in v8:
time: 44.3 us; the launch traced here: 44.2 us
  starting transfers between devices  27.2 us (61%)
  waiting for transfers between devices  10.5 us (24%)
  Pallas kernels  4.87 us (11%)
  other arithmetic  0.8 us (2%)
  local copies, waits for them, and re-layouts  0.7 us (2%)
    ppermute x14, starting transfers between devices, swap(): lax.ppermute(value, axis, [(at, at ^ shift) for at in range(lax.axis_size...  27.2 us
    ppermute x14, waiting for transfers between devices, swap(): lax.ppermute(value, axis, [(at, at ^ shift) for at in range(lax.axis_size...  10.5 us
    pallas_call x4, Pallas kernels, body(): pl.pallas_call(functools.partial(first_kernel if first else last_kernel i...  4.14 us
  transfers between devices with their start and end apart: 14, of which 6 were waited for; matrix products, arithmetic and copies ran while one was open for 0% of the time, Pallas kernels for 9%

profile of v8, /device:TPU:0, one launch (start us, length us, event | category | flops | bytes accessed | tf_op | source)
XLA Modules:
  0.0 44.2 jit_solution(5627357861872262355)
XLA Ops:
  0.0 0.0 copy-start
  0.0 0.0 copy-start.1
  0.0 4.0 %collective-permute-start = (s32[1,1,8,2]{2,3,1,0:T(2,128)}, s32[1,1,8,2]{2,3,1,0:T(2,128)S(1)}, u32[]{:S(2)}, u32[]{:S(2)}) collective-permute-start(s32[1,1,8,2]{2,3,1,0:T(2,128)} %param.7), channel_id=1, source_target_pairs={{0,16},{4,20},{8,24},{12,28},{16,0},{20,4},{24,8},{28,12},{1,17},{... | collective-permute-start | bytes 200 | tf_op jit(solution)/shard_map/ppermute | solution.py:187
  4.0 0.0 copy-start.3
  4.0 0.0 copy-start.4
  4.0 0.0 copy-start.2
  4.1 0.0 copy-done
  4.1 0.0 copy-done.1
  4.1 0.6 %copy-done.3 = s32[1,1,8,2]{2,3,1,0:T(2,128)S(1)} copy-done((s32[1,1,8,2]{2,3,1,0:T(2,128)S(1)}, s32[1,1,8,2]{2,3,1,0:T(2,128)}, u32[]{:S(2)}) %copy-start.3) | copy-done | bytes 88
  4.7 0.0 copy-done.4
  4.8 0.0 copy-done.2
  4.8 0.3 shard_map.56
  5.0 0.6 %collective-permute-start.4 = (f32[4,2,8,128]{3,2,1,0:T(8,128)S(1)}, f32[4,2,8,128]{3,2,1,0:T(8,128)S(1)}, u32[]{:S(2)}, u32[]{:S(2)}) collective-permute-start(f32[4,2,8,128]{3,2,1,0:T(8,128)S(1)} %get-tuple-element.22), channel_id=1, source_target_pairs={{0,16},{4,20},{8,24},{12,28},{16,0},{20,4},{24,8},{28,12},{1,17},{... | collective-permute-start | bytes 98312 | tf_op jit(solution)/shard_map/ppermute | solution.py:187
  5.7 0.1 collective-permute-done
  5.8 1.9 %collective-permute-start.1 = (s32[2,2,8]{2,1,0:T(2,128)S(1)}, s32[2,2,8]{2,1,0:T(2,128)S(1)}, u32[]{:S(2)}, u32[]{:S(2)}) collective-permute-start(s32[2,2,8]{2,1,0:T(2,128)S(1)} %pad_add_fusion.2.asked_ref), channel_id=1, source_target_pairs={{0,4},{4,0},{8,12},{12,8},{16,20},{20,16},{24,28},{28,24},{1,5},{5... | collective-permute-start | bytes 392 | tf_op jit(solution)/shard_map/ppermute | solution.py:187
  7.7 0.1 shard_map.57.refs_3_
  7.8 2.7 %collective-permute-start.3 = (f32[2,128,128]{2,1,0:T(8,128)S(1)}, f32[2,128,128]{2,1,0:T(8,128)S(1)}, u32[]{:S(2)}, u32[]{:S(2)}) collective-permute-start(f32[2,128,128]{2,1,0:T(8,128)S(1)} %shard_map.57.refs_3_), channel_id=1, source_target_pairs={{0,16},{4,20},{8,24},{12,28},{16,0},{20,4},{24,8},{28,12},{1,17},{... | collective-permute-start | bytes 393224 | tf_op jit(solution)/shard_map/ppermute | solution.py:187
  10.5 0.0 collective-permute-done.1
  10.5 1.6 %collective-permute-start.2 = (s32[4,2,8]{2,1,0:T(2,128)S(1)}, s32[4,2,8]{2,1,0:T(2,128)S(1)}, u32[]{:S(2)}, u32[]{:S(2)}) collective-permute-start(s32[4,2,8]{2,1,0:T(2,128)S(1)} %pad_add_fusion.1.asked_ref), channel_id=1, source_target_pairs={{0,8},{4,12},{8,0},{12,4},{16,24},{20,28},{24,16},{28,20},{1,9},{5... | collective-permute-start | bytes 776 | tf_op jit(solution)/shard_map/ppermute | solution.py:187
  12.1 0.0 collective-permute-done.4.refs_5_.passed_ref
  12.1 0.1 shard_map.59
  12.3 0.8 %collective-permute-start.6 = (f32[2,144,128]{2,1,0:T(8,128)S(1)}, f32[2,144,128]{2,1,0:T(8,128)S(1)}, u32[]{:S(2)}, u32[]{:S(2)}) collective-permute-start(f32[2,144,128]{2,1,0:T(8,128)S(1)} %get-tuple-element.24.refs_6_), channel_id=1, source_target_pairs={{0,4},{4,0},{8,12},{12,8},{16,20},{20,16},{24,28},{28,24},{1,5},{5... | collective-permute-start | bytes 442376 | tf_op jit(solution)/shard_map/ppermute | solution.py:187
  13.0 2.5 %collective-permute-start.5 = (f32[2,128,128]{2,1,0:T(8,128)S(1)}, f32[2,128,128]{2,1,0:T(8,128)S(1)}, u32[]{:S(2)}, u32[]{:S(2)}) collective-permute-start(f32[2,128,128]{2,1,0:T(8,128)S(1)} %get-tuple-element.23.refs_3_), channel_id=1, source_target_pairs={{0,20},{4,16},{8,28},{12,24},{16,4},{20,0},{24,12},{28,8},{1,21},{... | collective-permute-start | bytes 393224 | tf_op jit(solution)/shard_map/ppermute | solution.py:187
  15.6 0.0 collective-permute-done.2
  15.6 0.2 shard_map.61
  15.8 0.5 %collective-permute-start.8 = (f32[2,144,128]{2,1,0:T(8,128)S(1)}, f32[2,144,128]{2,1,0:T(8,128)S(1)}, u32[]{:S(2)}, u32[]{:S(2)}) collective-permute-start(f32[2,144,128]{2,1,0:T(8,128)S(1)} %get-tuple-element.26.refs_6_), channel_id=1, source_target_pairs={{0,8},{4,12},{8,0},{12,4},{16,24},{20,28},{24,16},{28,20},{1,9},{5... | collective-permute-start | bytes 442376 | tf_op jit(solution)/shard_map/ppermute | solution.py:187
  16.3 2.5 %collective-permute-start.10 = (f32[2,144,128]{2,1,0:T(8,128)S(1)}, f32[2,144,128]{2,1,0:T(8,128)S(1)}, u32[]{:S(2)}, u32[]{:S(2)}) collective-permute-start(f32[2,144,128]{2,1,0:T(8,128)S(1)} %get-tuple-element.28.refs_3_), channel_id=1, source_target_pairs={{0,12},{4,8},{8,4},{12,0},{16,28},{20,24},{24,20},{28,16},{1,13},{... | collective-permute-start | bytes 442376 | tf_op jit(solution)/shard_map/ppermute | solution.py:187
  18.8 0.0 collective-permute-done.3.refs_4_
  18.8 3.4 %collective-permute-start.7 = (f32[2,128,128]{2,1,0:T(8,128)S(1)}, f32[2,128,128]{2,1,0:T(8,128)S(1)}, u32[]{:S(2)}, u32[]{:S(2)}) collective-permute-start(f32[2,128,128]{2,1,0:T(8,128)S(1)} %get-tuple-element.25.refs_3_), channel_id=1, source_target_pairs={{0,24},{4,28},{8,16},{12,20},{16,8},{20,12},{24,0},{28,4},{1,25},{... | collective-permute-start | bytes 393224 | tf_op jit(solution)/shard_map/ppermute | solution.py:187
  22.3 1.5 %collective-permute-done.5.refs_4_ = f32[2,128,128]{2,1,0:T(8,128)S(1)} collective-permute-done((f32[2,128,128]{2,1,0:T(8,128)S(1)}, f32[2,128,128]{2,1,0:T(8,128)S(1)}, u32[]{:S(2)}, u32[]{:S(2)}) %collective-permute-start.5) | collective-permute-done | bytes 131104 | tf_op jit(solution)/shard_map/ppermute | solution.py:187
  23.7 4.4 %collective-permute-start.9 = (f32[2,128,128]{2,1,0:T(8,128)S(1)}, f32[2,128,128]{2,1,0:T(8,128)S(1)}, u32[]{:S(2)}, u32[]{:S(2)}) collective-permute-start(f32[2,128,128]{2,1,0:T(8,128)S(1)} %get-tuple-element.27.refs_0_), channel_id=1, source_target_pairs={{0,28},{4,24},{8,20},{12,16},{16,12},{20,8},{24,4},{28,0},{1,29},{... | collective-permute-start | bytes 393224 | tf_op jit(solution)/shard_map/ppermute | solution.py:187
  28.2 0.9 %shard_map.58.before_ref = f32[16,128,128]{2,1,0:T(8,128)S(1)} custom-call(f32[16,128,128]{2,1,0:T(8,128)S(1)} %get-tuple-element.19.latent_ref, s32[2,2,8]{2,1,0:T(2,128)S(1)} %get-tuple-element.20.ids_ref.refs_0_, s32[8,2,8]{2,1,0:T(2,128)S(1)} %pad_add_fusion.refs_1_.asked_ref, f32[8,2,8,128]{3,2,1,0:T(8,128)S(1)} %get-tuple-element.21.coded_ref.refs_2_, ...), custom_call_target="tpu_custom_call" | custom-call | flops 50331648 | bytes 3145728 | tf_op jit(solution)/shard_map/pallas_call | solution.py:255
  29.1 0.0 collective-permute-done.6.refs_5_.refs_7_.refs_8_
  29.1 1.1 %shard_map.60.before_ref = f32[16,128,128]{2,1,0:T(8,128)S(1)} custom-call(f32[16,128,128]{2,1,0:T(8,128)S(1)} %shard_map.58.before_ref, s32[2,2,8]{2,1,0:T(2,128)S(1)} %get-tuple-element.20.ids_ref.refs_0_, s32[8,2,8]{2,1,0:T(2,128)S(1)} %pad_add_fusion.refs_1_.asked_ref, ...), custom_call_target="tpu_custom_call", output_to_operand_aliasing={{}: (0, {})} | custom-call | flops 100663296 | bytes 3145728 | tf_op jit(solution)/shard_map/pallas_call | solution.py:255
  30.2 0.0 collective-permute-done.7.refs_4_
  30.2 0.0 collective-permute-done.8.refs_5_.refs_7_.refs_8_
  30.2 1.1 %shard_map.62.before_ref = f32[16,128,128]{2,1,0:T(8,128)S(1)} custom-call(f32[16,128,128]{2,1,0:T(8,128)S(1)} %shard_map.60.before_ref, s32[2,2,8]{2,1,0:T(2,128)S(1)} %get-tuple-element.20.ids_ref.refs_0_, s32[8,2,8]{2,1,0:T(2,128)S(1)} %pad_add_fusion.refs_1_.asked_ref, ...), custom_call_target="tpu_custom_call", output_to_operand_aliasing={{}: (0, {})} | custom-call | flops 100663296 | bytes 3145728 | tf_op jit(solution)/shard_map/pallas_call | solution.py:255
  31.3 0.2 collective-permute-done.9.refs_1_
  31.5 0.8 %collective-permute-done.10.refs_2_.refs_4_.refs_5_ = f32[2,144,128]{2,1,0:T(8,128)S(1)} collective-permute-done((f32[2,144,128]{2,1,0:T(8,128)S(1)}, f32[2,144,128]{2,1,0:T(8,128)S(1)}, u32[]{:S(2)}, u32[]{:S(2)}) %collective-permute-start.10) | collective-permute-done | bytes 147488 | tf_op jit(solution)/shard_map/ppermute | solution.py:187
  32.3 1.1 %shard_map.63 = (f32[4,128,128]{2,1,0:T(8,128)S(1)}, f32[4,128,128]{2,1,0:T(8,128)S(1)}, f32[4,128,128]{2,1,0:T(8,128)S(1)}, f32[4,128,128]{2,1,0:T(8,128)S(1)}) custom-call(f32[16,128,128]{2,1,0:T(8,128)S(1)} %shard_map.62.before_ref, s32[2,2,8]{2,1,0:T(2,128)S(1)} %get-tuple-element.20.ids_ref.refs_0_, s32[8,2,8]{2,1,0:T(2,128)S(1)} %pad_add_fusion.refs_1_.asked_ref, ...), custom_call_target="tpu_custom_call" | custom-call | flops 100663296 | bytes 3145728 | tf_op jit(solution)/shard_map/pallas_call | solution.py:255
  33.4 0.1 collective-permute-start.12
  33.5 0.5 %collective-permute-start.11 = (f32[4,128,128]{2,1,0:T(8,128)S(1)}, f32[4,128,128]{2,1,0:T(8,128)S(1)}, u32[]{:S(2)}, u32[]{:S(2)}) collective-permute-start(f32[4,128,128]{2,1,0:T(8,128)S(1)} %get-tuple-element.30), channel_id=1, source_target_pairs={{0,1},{1,0},{2,3},{3,2},{4,5},{5,4},{6,7},{7,6},{8,9},{9,8},{10,11... | collective-permute-start | bytes 786440 | tf_op jit(solution)/shard_map/ppermute | solution.py:187
  34.0 1.0 %collective-permute-done.12 = f32[4,128,128]{2,1,0:T(8,128)S(1)} collective-permute-done((f32[4,128,128]{2,1,0:T(8,128)S(1)}, f32[4,128,128]{2,1,0:T(8,128)S(1)}, u32[]{:S(2)}, u32[]{:S(2)}) %collective-permute-start.12) | collective-permute-done | bytes 262176 | tf_op jit(solution)/shard_map/ppermute | solution.py:187
  35.0 1.6 %collective-permute-start.13 = (f32[4,128,128]{2,1,0:T(8,128)S(1)}, f32[4,128,128]{2,1,0:T(8,128)S(1)}, u32[]{:S(2)}, u32[]{:S(2)}) collective-permute-start(f32[4,128,128]{2,1,0:T(8,128)S(1)} %add.10), channel_id=1, source_target_pairs={{0,2},{1,3},{2,0},{3,1},{4,6},{5,7},{6,4},{7,5},{8,10},{9,11},{10,... | collective-permute-start | bytes 786440 | tf_op jit(solution)/shard_map/ppermute | solution.py:187
  36.6 0.0 collective-permute-done.11
  36.6 6.9 %collective-permute-done.13 = f32[4,128,128]{2,1,0:T(8,128)S(1)} collective-permute-done((f32[4,128,128]{2,1,0:T(8,128)S(1)}, f32[4,128,128]{2,1,0:T(8,128)S(1)}, u32[]{:S(2)}, u32[]{:S(2)}) %collective-permute-start.13) | collective-permute-done | bytes 262176 | tf_op jit(solution)/shard_map/ppermute | solution.py:187
  43.4 0.8 %add_add_fusion = f32[4,128,128]{2,1,0:T(8,128)} fusion(f32[4,128,128]{2,1,0:T(8,128)S(1)} %collective-permute-done.13, f32[4,128,128]{2,1,0:T(8,128)S(1)} %get-tuple-element.29, f32[4,128,128]{2,1,0:T(8,128)S(1)} %collective-permute-done.11), kind=kLoop, calls=%fused_computation | loop fusion | flops 131072 | bytes 1048576 | tf_op jit(solution)/shard_map/add | solution.py:271
  (7 shorter events, 0.1 us)
Async XLA Ops:
  0.0 4.1 %copy-start = (f32[2048,128]{1,0:T(8,128)S(1)}, f32[2048,128]{1,0:T(8,128)}, u32[]{:S(2)}) copy-start(f32[2048,128]{1,0:T(8,128)} %param.5) | copy-start | bytes 3145732
  0.0 4.1 %copy-start.1 = (s32[1,1,8,2,8,128]{5,4,3,2,1,0:T(8,128)S(1)}, s32[1,1,8,2,8,128]{5,4,3,2,1,0:T(8,128)}, u32[]{:S(2)}) copy-start(s32[1,1,8,2,8,128]{5,4,3,2,1,0:T(8,128)} %param.9) | copy-start | bytes 196612
  0.0 5.8 %collective-permute-start = (s32[1,1,8,2]{2,3,1,0:T(2,128)}, s32[1,1,8,2]{2,3,1,0:T(2,128)S(1)}, u32[]{:S(2)}, u32[]{:S(2)}) collective-permute-start(s32[1,1,8,2]{2,3,1,0:T(2,128)} %param.7), channel_id=1, source_target_pairs={{0,16},{4,20},{8,24},{12,28},{16,0},{20,4},{24,8},{28,12},{1,17},{... | collective-permute-start | bytes 200 | tf_op jit(solution)/shard_map/ppermute | solution.py:187
  4.0 0.7 %copy-start.3 = (s32[1,1,8,2]{2,3,1,0:T(2,128)S(1)}, s32[1,1,8,2]{2,3,1,0:T(2,128)}, u32[]{:S(2)}) copy-start(s32[1,1,8,2]{2,3,1,0:T(2,128)} %param.8) | copy-start | bytes 196
  4.0 0.7 %copy-start.4 = (s32[1,1,8,2]{2,3,1,0:T(2,128)S(1)}, s32[1,1,8,2]{2,3,1,0:T(2,128)}, u32[]{:S(2)}) copy-start(s32[1,1,8,2]{2,3,1,0:T(2,128)} %param.7) | copy-start | bytes 196
  4.0 0.7 %copy-start.2 = (s32[1,1,8,2]{2,3,1,0:T(2,128)S(1)}, s32[1,1,8,2]{2,3,1,0:T(2,128)}, u32[]{:S(2)}) copy-start(s32[1,1,8,2]{2,3,1,0:T(2,128)} %param.6) | copy-start | bytes 196
  5.0 7.1 %collective-permute-start.4 = (f32[4,2,8,128]{3,2,1,0:T(8,128)S(1)}, f32[4,2,8,128]{3,2,1,0:T(8,128)S(1)}, u32[]{:S(2)}, u32[]{:S(2)}) collective-permute-start(f32[4,2,8,128]{3,2,1,0:T(8,128)S(1)} %get-tuple-element.22), channel_id=1, source_target_pairs={{0,16},{4,20},{8,24},{12,28},{16,0},{20,4},{24,8},{28,12},{1,17},{... | collective-permute-start | bytes 98312 | tf_op jit(solution)/shard_map/ppermute | solution.py:187
  5.8 4.7 %collective-permute-start.1 = (s32[2,2,8]{2,1,0:T(2,128)S(1)}, s32[2,2,8]{2,1,0:T(2,128)S(1)}, u32[]{:S(2)}, u32[]{:S(2)}) collective-permute-start(s32[2,2,8]{2,1,0:T(2,128)S(1)} %pad_add_fusion.2.asked_ref), channel_id=1, source_target_pairs={{0,4},{4,0},{8,12},{12,8},{16,20},{20,16},{24,28},{28,24},{1,5},{5... | collective-permute-start | bytes 392 | tf_op jit(solution)/shard_map/ppermute | solution.py:187
  7.8 11.0 %collective-permute-start.3 = (f32[2,128,128]{2,1,0:T(8,128)S(1)}, f32[2,128,128]{2,1,0:T(8,128)S(1)}, u32[]{:S(2)}, u32[]{:S(2)}) collective-permute-start(f32[2,128,128]{2,1,0:T(8,128)S(1)} %shard_map.57.refs_3_), channel_id=1, source_target_pairs={{0,16},{4,20},{8,24},{12,28},{16,0},{20,4},{24,8},{28,12},{1,17},{... | collective-permute-start | bytes 393224 | tf_op jit(solution)/shard_map/ppermute | solution.py:187
  10.5 5.1 %collective-permute-start.2 = (s32[4,2,8]{2,1,0:T(2,128)S(1)}, s32[4,2,8]{2,1,0:T(2,128)S(1)}, u32[]{:S(2)}, u32[]{:S(2)}) collective-permute-start(s32[4,2,8]{2,1,0:T(2,128)S(1)} %pad_add_fusion.1.asked_ref), channel_id=1, source_target_pairs={{0,8},{4,12},{8,0},{12,4},{16,24},{20,28},{24,16},{28,20},{1,9},{5... | collective-permute-start | bytes 776 | tf_op jit(solution)/shard_map/ppermute | solution.py:187
  12.3 16.8 %collective-permute-start.6 = (f32[2,144,128]{2,1,0:T(8,128)S(1)}, f32[2,144,128]{2,1,0:T(8,128)S(1)}, u32[]{:S(2)}, u32[]{:S(2)}) collective-permute-start(f32[2,144,128]{2,1,0:T(8,128)S(1)} %get-tuple-element.24.refs_6_), channel_id=1, source_target_pairs={{0,4},{4,0},{8,12},{12,8},{16,20},{20,16},{24,28},{28,24},{1,5},{5... | collective-permute-start | bytes 442376 | tf_op jit(solution)/shard_map/ppermute | solution.py:187
  13.0 10.7 %collective-permute-start.5 = (f32[2,128,128]{2,1,0:T(8,128)S(1)}, f32[2,128,128]{2,1,0:T(8,128)S(1)}, u32[]{:S(2)}, u32[]{:S(2)}) collective-permute-start(f32[2,128,128]{2,1,0:T(8,128)S(1)} %get-tuple-element.23.refs_3_), channel_id=1, source_target_pairs={{0,20},{4,16},{8,28},{12,24},{16,4},{20,0},{24,12},{28,8},{1,21},{... | collective-permute-start | bytes 393224 | tf_op jit(solution)/shard_map/ppermute | solution.py:187
  15.8 14.4 %collective-permute-start.8 = (f32[2,144,128]{2,1,0:T(8,128)S(1)}, f32[2,144,128]{2,1,0:T(8,128)S(1)}, u32[]{:S(2)}, u32[]{:S(2)}) collective-permute-start(f32[2,144,128]{2,1,0:T(8,128)S(1)} %get-tuple-element.26.refs_6_), channel_id=1, source_target_pairs={{0,8},{4,12},{8,0},{12,4},{16,24},{20,28},{24,16},{28,20},{1,9},{5... | collective-permute-start | bytes 442376 | tf_op jit(solution)/shard_map/ppermute | solution.py:187
  16.3 16.0 %collective-permute-start.10 = (f32[2,144,128]{2,1,0:T(8,128)S(1)}, f32[2,144,128]{2,1,0:T(8,128)S(1)}, u32[]{:S(2)}, u32[]{:S(2)}) collective-permute-start(f32[2,144,128]{2,1,0:T(8,128)S(1)} %get-tuple-element.28.refs_3_), channel_id=1, source_target_pairs={{0,12},{4,8},{8,4},{12,0},{16,28},{20,24},{24,20},{28,16},{1,13},{... | collective-permute-start | bytes 442376 | tf_op jit(solution)/shard_map/ppermute | solution.py:187
  18.8 11.3 %collective-permute-start.7 = (f32[2,128,128]{2,1,0:T(8,128)S(1)}, f32[2,128,128]{2,1,0:T(8,128)S(1)}, u32[]{:S(2)}, u32[]{:S(2)}) collective-permute-start(f32[2,128,128]{2,1,0:T(8,128)S(1)} %get-tuple-element.25.refs_3_), channel_id=1, source_target_pairs={{0,24},{4,28},{8,16},{12,20},{16,8},{20,12},{24,0},{28,4},{1,25},{... | collective-permute-start | bytes 393224 | tf_op jit(solution)/shard_map/ppermute | solution.py:187
  23.7 7.8 %collective-permute-start.9 = (f32[2,128,128]{2,1,0:T(8,128)S(1)}, f32[2,128,128]{2,1,0:T(8,128)S(1)}, u32[]{:S(2)}, u32[]{:S(2)}) collective-permute-start(f32[2,128,128]{2,1,0:T(8,128)S(1)} %get-tuple-element.27.refs_0_), channel_id=1, source_target_pairs={{0,28},{4,24},{8,20},{12,16},{16,12},{20,8},{24,4},{28,0},{1,29},{... | collective-permute-start | bytes 393224 | tf_op jit(solution)/shard_map/ppermute | solution.py:187
  33.4 1.6 %collective-permute-start.12 = (f32[4,128,128]{2,1,0:T(8,128)S(1)}, f32[4,128,128]{2,1,0:T(8,128)S(1)}, u32[]{:S(2)}, u32[]{:S(2)}) collective-permute-start(f32[4,128,128]{2,1,0:T(8,128)S(1)} %get-tuple-element.32), channel_id=1, source_target_pairs={{0,1},{1,0},{2,3},{3,2},{4,5},{5,4},{6,7},{7,6},{8,9},{9,8},{10,11... | collective-permute-start | bytes 786440 | tf_op jit(solution)/shard_map/ppermute | solution.py:187
  33.5 3.1 %collective-permute-start.11 = (f32[4,128,128]{2,1,0:T(8,128)S(1)}, f32[4,128,128]{2,1,0:T(8,128)S(1)}, u32[]{:S(2)}, u32[]{:S(2)}) collective-permute-start(f32[4,128,128]{2,1,0:T(8,128)S(1)} %get-tuple-element.30), channel_id=1, source_target_pairs={{0,1},{1,0},{2,3},{3,2},{4,5},{5,4},{6,7},{7,6},{8,9},{9,8},{10,11... | collective-permute-start | bytes 786440 | tf_op jit(solution)/shard_map/ppermute | solution.py:187
  35.0 8.4 %collective-permute-start.13 = (f32[4,128,128]{2,1,0:T(8,128)S(1)}, f32[4,128,128]{2,1,0:T(8,128)S(1)}, u32[]{:S(2)}, u32[]{:S(2)}) collective-permute-start(f32[4,128,128]{2,1,0:T(8,128)S(1)} %add.10), channel_id=1, source_target_pairs={{0,2},{1,3},{2,0},{3,1},{4,6},{5,7},{6,4},{7,5},{8,10},{9,11},{10,... | collective-permute-start | bytes 786440 | tf_op jit(solution)/shard_map/ppermute | solution.py:187

commit v9 on v8

--- a/solution.py
+++ b/solution.py
@@ -175,7 +175,7 @@
 
 def shift_groups(peers):
     top = peers // 2
-    near = sorted(range(1, top), key=lambda at: (at.bit_length(), at))
+    near = sorted(range(1, top), key=lambda at: (at.bit_length(), -at))
     return [[top]] + [[top + at, at] for at in near]
 
 
@@ -232,7 +232,7 @@
         else:
             asked = jnp.concatenate([asked, swap(asked, "rows", bit)])
         where = where + [at ^ bit for at in where]
-        shifts = sorted(where[len(where) // 2 :])
+        shifts = sorted(where[len(where) // 2 :], reverse=True)
         sent = pl.pallas_call(
             functools.partial(pack_kernel, shifts, [where.index(at) for at in shifts]),
             out_shape=[far_message if at >= top else near_message for at in shifts],

time: 44.3 us -> 44.2 us (level)
  starting transfers between devices: 27.2 us -> 25.9 us
  waiting for transfers between devices: 10.5 us -> 11.7 us
    ppermute x14, starting transfers between devices: 27.2 us -> 25.9 us  [swap(): lax.ppermute(value, axis, [(at, at ^ shift) for at in range(lax.axis_size...]
    ppermute x14, waiting for transfers between devices: 10.5 us -> 11.7 us  [swap(): lax.ppermute(value, axis, [(at, at ^ shift) for at in range(lax.axis_size...]
where the time goes in v9:
time: 44.2 us; the launch traced here: 44.1 us
  starting transfers between devices  25.9 us (59%)
  waiting for transfers between devices  11.7 us (26%)
  Pallas kernels  4.86 us (11%)
  other arithmetic  0.8 us (2%)
  local copies, waits for them, and re-layouts  0.7 us (2%)
    ppermute x14, starting transfers between devices, swap(): lax.ppermute(value, axis, [(at, at ^ shift) for at in range(lax.axis_size...  25.9 us
    ppermute x14, waiting for transfers between devices, swap(): lax.ppermute(value, axis, [(at, at ^ shift) for at in range(lax.axis_size...  11.7 us
    pallas_call x4, Pallas kernels, body(): pl.pallas_call(functools.partial(first_kernel if first else last_kernel i...  4.14 us
  transfers between devices with their start and end apart: 14, of which 6 were waited for; matrix products, arithmetic and copies ran while one was open for 0% of the time, Pallas kernels for 9%

profile of v9, /device:TPU:0, one launch (start us, length us, event | category | flops | bytes accessed | tf_op | source)
XLA Modules:
  0.0 44.1 jit_solution(6186521471305963065)
XLA Ops:
  0.0 0.0 copy-start
  0.0 0.0 copy-start.1
  0.0 4.0 %collective-permute-start = (s32[1,1,8,2]{2,3,1,0:T(2,128)}, s32[1,1,8,2]{2,3,1,0:T(2,128)S(1)}, u32[]{:S(2)}, u32[]{:S(2)}) collective-permute-start(s32[1,1,8,2]{2,3,1,0:T(2,128)} %param.7), channel_id=1, source_target_pairs={{0,16},{4,20},{8,24},{12,28},{16,0},{20,4},{24,8},{28,12},{1,17},{... | collective-permute-start | bytes 200 | tf_op jit(solution)/shard_map/ppermute | solution.py:187
  4.0 0.0 copy-start.3
  4.0 0.0 copy-start.4
  4.0 0.0 copy-start.2
  4.1 0.0 copy-done
  4.1 0.0 copy-done.1
  4.1 0.6 %copy-done.3 = s32[1,1,8,2]{2,3,1,0:T(2,128)S(1)} copy-done((s32[1,1,8,2]{2,3,1,0:T(2,128)S(1)}, s32[1,1,8,2]{2,3,1,0:T(2,128)}, u32[]{:S(2)}) %copy-start.3) | copy-done | bytes 88
  4.7 0.0 copy-done.4
  4.8 0.0 copy-done.2
  4.8 0.3 shard_map.56
  5.0 0.6 %collective-permute-start.4 = (f32[4,2,8,128]{3,2,1,0:T(8,128)S(1)}, f32[4,2,8,128]{3,2,1,0:T(8,128)S(1)}, u32[]{:S(2)}, u32[]{:S(2)}) collective-permute-start(f32[4,2,8,128]{3,2,1,0:T(8,128)S(1)} %get-tuple-element.22), channel_id=1, source_target_pairs={{0,16},{4,20},{8,24},{12,28},{16,0},{20,4},{24,8},{28,12},{1,17},{... | collective-permute-start | bytes 98312 | tf_op jit(solution)/shard_map/ppermute | solution.py:187
  5.7 0.1 collective-permute-done
  5.8 1.9 %collective-permute-start.1 = (s32[2,2,8]{2,1,0:T(2,128)S(1)}, s32[2,2,8]{2,1,0:T(2,128)S(1)}, u32[]{:S(2)}, u32[]{:S(2)}) collective-permute-start(s32[2,2,8]{2,1,0:T(2,128)S(1)} %pad_add_fusion.2.asked_ref), channel_id=1, source_target_pairs={{0,4},{4,0},{8,12},{12,8},{16,20},{20,16},{24,28},{28,24},{1,5},{5... | collective-permute-start | bytes 392 | tf_op jit(solution)/shard_map/ppermute | solution.py:187
  7.7 0.1 shard_map.57.refs_3_
  7.8 2.7 %collective-permute-start.3 = (f32[2,128,128]{2,1,0:T(8,128)S(1)}, f32[2,128,128]{2,1,0:T(8,128)S(1)}, u32[]{:S(2)}, u32[]{:S(2)}) collective-permute-start(f32[2,128,128]{2,1,0:T(8,128)S(1)} %shard_map.57.refs_3_), channel_id=1, source_target_pairs={{0,16},{4,20},{8,24},{12,28},{16,0},{20,4},{24,8},{28,12},{1,17},{... | collective-permute-start | bytes 393224 | tf_op jit(solution)/shard_map/ppermute | solution.py:187
  10.5 0.0 collective-permute-done.1
  10.5 1.6 %collective-permute-start.2 = (s32[4,2,8]{2,1,0:T(2,128)S(1)}, s32[4,2,8]{2,1,0:T(2,128)S(1)}, u32[]{:S(2)}, u32[]{:S(2)}) collective-permute-start(s32[4,2,8]{2,1,0:T(2,128)S(1)} %pad_add_fusion.1.asked_ref), channel_id=1, source_target_pairs={{0,8},{4,12},{8,0},{12,4},{16,24},{20,28},{24,16},{28,20},{1,9},{5... | collective-permute-start | bytes 776 | tf_op jit(solution)/shard_map/ppermute | solution.py:187
  12.1 0.0 collective-permute-done.4.refs_5_.passed_ref
  12.1 0.1 shard_map.59
  12.3 0.8 %collective-permute-start.6 = (f32[2,144,128]{2,1,0:T(8,128)S(1)}, f32[2,144,128]{2,1,0:T(8,128)S(1)}, u32[]{:S(2)}, u32[]{:S(2)}) collective-permute-start(f32[2,144,128]{2,1,0:T(8,128)S(1)} %get-tuple-element.24.refs_6_), channel_id=1, source_target_pairs={{0,4},{4,0},{8,12},{12,8},{16,20},{20,16},{24,28},{28,24},{1,5},{5... | collective-permute-start | bytes 442376 | tf_op jit(solution)/shard_map/ppermute | solution.py:187
  13.0 2.5 %collective-permute-start.5 = (f32[2,128,128]{2,1,0:T(8,128)S(1)}, f32[2,128,128]{2,1,0:T(8,128)S(1)}, u32[]{:S(2)}, u32[]{:S(2)}) collective-permute-start(f32[2,128,128]{2,1,0:T(8,128)S(1)} %get-tuple-element.23.refs_3_), channel_id=1, source_target_pairs={{0,20},{4,16},{8,28},{12,24},{16,4},{20,0},{24,12},{28,8},{1,21},{... | collective-permute-start | bytes 393224 | tf_op jit(solution)/shard_map/ppermute | solution.py:187
  15.6 0.0 collective-permute-done.2
  15.6 0.2 shard_map.61
  15.8 1.5 %collective-permute-start.8 = (f32[2,144,128]{2,1,0:T(8,128)S(1)}, f32[2,144,128]{2,1,0:T(8,128)S(1)}, u32[]{:S(2)}, u32[]{:S(2)}) collective-permute-start(f32[2,144,128]{2,1,0:T(8,128)S(1)} %get-tuple-element.26.refs_6_), channel_id=1, source_target_pairs={{0,12},{4,8},{8,4},{12,0},{16,28},{20,24},{24,20},{28,16},{1,13},{... | collective-permute-start | bytes 442376 | tf_op jit(solution)/shard_map/ppermute | solution.py:187
  17.2 1.6 %collective-permute-start.10 = (f32[2,144,128]{2,1,0:T(8,128)S(1)}, f32[2,144,128]{2,1,0:T(8,128)S(1)}, u32[]{:S(2)}, u32[]{:S(2)}) collective-permute-start(f32[2,144,128]{2,1,0:T(8,128)S(1)} %get-tuple-element.28.refs_3_), channel_id=1, source_target_pairs={{0,8},{4,12},{8,0},{12,4},{16,24},{20,28},{24,16},{28,20},{1,9},{5... | collective-permute-start | bytes 442376 | tf_op jit(solution)/shard_map/ppermute | solution.py:187
  18.8 0.0 collective-permute-done.3.refs_4_
  18.8 2.8 %collective-permute-start.7 = (f32[2,128,128]{2,1,0:T(8,128)S(1)}, f32[2,128,128]{2,1,0:T(8,128)S(1)}, u32[]{:S(2)}, u32[]{:S(2)}) collective-permute-start(f32[2,128,128]{2,1,0:T(8,128)S(1)} %get-tuple-element.25.refs_3_), channel_id=1, source_target_pairs={{0,28},{4,24},{8,20},{12,16},{16,12},{20,8},{24,4},{28,0},{1,29},{... | collective-permute-start | bytes 393224 | tf_op jit(solution)/shard_map/ppermute | solution.py:187
  21.6 1.7 %collective-permute-done.5.refs_4_ = f32[2,128,128]{2,1,0:T(8,128)S(1)} collective-permute-done((f32[2,128,128]{2,1,0:T(8,128)S(1)}, f32[2,128,128]{2,1,0:T(8,128)S(1)}, u32[]{:S(2)}, u32[]{:S(2)}) %collective-permute-start.5) | collective-permute-done | bytes 131104 | tf_op jit(solution)/shard_map/ppermute | solution.py:187
  23.3 3.8 %collective-permute-start.9 = (f32[2,128,128]{2,1,0:T(8,128)S(1)}, f32[2,128,128]{2,1,0:T(8,128)S(1)}, u32[]{:S(2)}, u32[]{:S(2)}) collective-permute-start(f32[2,128,128]{2,1,0:T(8,128)S(1)} %get-tuple-element.27.refs_0_), channel_id=1, source_target_pairs={{0,24},{4,28},{8,16},{12,20},{16,8},{20,12},{24,0},{28,4},{1,25},{... | collective-permute-start | bytes 393224 | tf_op jit(solution)/shard_map/ppermute | solution.py:187
  27.2 0.9 %shard_map.58.before_ref = f32[16,128,128]{2,1,0:T(8,128)S(1)} custom-call(f32[16,128,128]{2,1,0:T(8,128)S(1)} %get-tuple-element.19.latent_ref, s32[2,2,8]{2,1,0:T(2,128)S(1)} %get-tuple-element.20.ids_ref.refs_0_, s32[8,2,8]{2,1,0:T(2,128)S(1)} %pad_add_fusion.refs_1_.asked_ref, f32[8,2,8,128]{3,2,1,0:T(8,128)S(1)} %get-tuple-element.21.coded_ref.refs_2_, ...), custom_call_target="tpu_custom_call" | custom-call | flops 50331648 | bytes 3145728 | tf_op jit(solution)/shard_map/pallas_call | solution.py:255
  28.1 0.0 collective-permute-done.6.refs_5_.refs_7_.refs_8_
  28.1 1.1 %shard_map.60.before_ref = f32[16,128,128]{2,1,0:T(8,128)S(1)} custom-call(f32[16,128,128]{2,1,0:T(8,128)S(1)} %shard_map.58.before_ref, s32[2,2,8]{2,1,0:T(2,128)S(1)} %get-tuple-element.20.ids_ref.refs_0_, s32[8,2,8]{2,1,0:T(2,128)S(1)} %pad_add_fusion.refs_1_.asked_ref, ...), custom_call_target="tpu_custom_call", output_to_operand_aliasing={{}: (0, {})} | custom-call | flops 100663296 | bytes 3145728 | tf_op jit(solution)/shard_map/pallas_call | solution.py:255
  29.2 0.2 collective-permute-done.7.refs_4_
  29.4 0.0 collective-permute-done.8.refs_5_.refs_7_.refs_8_
  29.4 1.1 %shard_map.62.before_ref = f32[16,128,128]{2,1,0:T(8,128)S(1)} custom-call(f32[16,128,128]{2,1,0:T(8,128)S(1)} %shard_map.60.before_ref, s32[2,2,8]{2,1,0:T(2,128)S(1)} %get-tuple-element.20.ids_ref.refs_0_, s32[8,2,8]{2,1,0:T(2,128)S(1)} %pad_add_fusion.refs_1_.asked_ref, ...), custom_call_target="tpu_custom_call", output_to_operand_aliasing={{}: (0, {})} | custom-call | flops 100663296 | bytes 3145728 | tf_op jit(solution)/shard_map/pallas_call | solution.py:255
  30.5 0.0 collective-permute-done.9.refs_1_
  30.5 1.7 %collective-permute-done.10.refs_2_.refs_4_.refs_5_ = f32[2,144,128]{2,1,0:T(8,128)S(1)} collective-permute-done((f32[2,144,128]{2,1,0:T(8,128)S(1)}, f32[2,144,128]{2,1,0:T(8,128)S(1)}, u32[]{:S(2)}, u32[]{:S(2)}) %collective-permute-start.10) | collective-permute-done | bytes 147488 | tf_op jit(solution)/shard_map/ppermute | solution.py:187
  32.2 1.1 %shard_map.63 = (f32[4,128,128]{2,1,0:T(8,128)S(1)}, f32[4,128,128]{2,1,0:T(8,128)S(1)}, f32[4,128,128]{2,1,0:T(8,128)S(1)}, f32[4,128,128]{2,1,0:T(8,128)S(1)}) custom-call(f32[16,128,128]{2,1,0:T(8,128)S(1)} %shard_map.62.before_ref, s32[2,2,8]{2,1,0:T(2,128)S(1)} %get-tuple-element.20.ids_ref.refs_0_, s32[8,2,8]{2,1,0:T(2,128)S(1)} %pad_add_fusion.refs_1_.asked_ref, ...), custom_call_target="tpu_custom_call" | custom-call | flops 100663296 | bytes 3145728 | tf_op jit(solution)/shard_map/pallas_call | solution.py:255
  33.3 0.1 collective-permute-start.12
  33.4 0.5 %collective-permute-start.11 = (f32[4,128,128]{2,1,0:T(8,128)S(1)}, f32[4,128,128]{2,1,0:T(8,128)S(1)}, u32[]{:S(2)}, u32[]{:S(2)}) collective-permute-start(f32[4,128,128]{2,1,0:T(8,128)S(1)} %get-tuple-element.30), channel_id=1, source_target_pairs={{0,1},{1,0},{2,3},{3,2},{4,5},{5,4},{6,7},{7,6},{8,9},{9,8},{10,11... | collective-permute-start | bytes 786440 | tf_op jit(solution)/shard_map/ppermute | solution.py:187
  33.9 1.0 %collective-permute-done.12 = f32[4,128,128]{2,1,0:T(8,128)S(1)} collective-permute-done((f32[4,128,128]{2,1,0:T(8,128)S(1)}, f32[4,128,128]{2,1,0:T(8,128)S(1)}, u32[]{:S(2)}, u32[]{:S(2)}) %collective-permute-start.12) | collective-permute-done | bytes 262176 | tf_op jit(solution)/shard_map/ppermute | solution.py:187
  34.9 1.6 %collective-permute-start.13 = (f32[4,128,128]{2,1,0:T(8,128)S(1)}, f32[4,128,128]{2,1,0:T(8,128)S(1)}, u32[]{:S(2)}, u32[]{:S(2)}) collective-permute-start(f32[4,128,128]{2,1,0:T(8,128)S(1)} %add.10), channel_id=1, source_target_pairs={{0,2},{1,3},{2,0},{3,1},{4,6},{5,7},{6,4},{7,5},{8,10},{9,11},{10,... | collective-permute-start | bytes 786440 | tf_op jit(solution)/shard_map/ppermute | solution.py:187
  36.5 0.0 collective-permute-done.11
  36.5 6.8 %collective-permute-done.13 = f32[4,128,128]{2,1,0:T(8,128)S(1)} collective-permute-done((f32[4,128,128]{2,1,0:T(8,128)S(1)}, f32[4,128,128]{2,1,0:T(8,128)S(1)}, u32[]{:S(2)}, u32[]{:S(2)}) %collective-permute-start.13) | collective-permute-done | bytes 262176 | tf_op jit(solution)/shard_map/ppermute | solution.py:187
  43.3 0.8 %add_add_fusion = f32[4,128,128]{2,1,0:T(8,128)} fusion(f32[4,128,128]{2,1,0:T(8,128)S(1)} %collective-permute-done.13, f32[4,128,128]{2,1,0:T(8,128)S(1)} %get-tuple-element.29, f32[4,128,128]{2,1,0:T(8,128)S(1)} %collective-permute-done.11), kind=kLoop, calls=%fused_computation | loop fusion | flops 131072 | bytes 1048576 | tf_op jit(solution)/shard_map/add | solution.py:271
  (7 shorter events, 0.1 us)
Async XLA Ops:
  0.0 4.1 %copy-start = (f32[2048,128]{1,0:T(8,128)S(1)}, f32[2048,128]{1,0:T(8,128)}, u32[]{:S(2)}) copy-start(f32[2048,128]{1,0:T(8,128)} %param.5) | copy-start | bytes 3145732
  0.0 4.1 %copy-start.1 = (s32[1,1,8,2,8,128]{5,4,3,2,1,0:T(8,128)S(1)}, s32[1,1,8,2,8,128]{5,4,3,2,1,0:T(8,128)}, u32[]{:S(2)}) copy-start(s32[1,1,8,2,8,128]{5,4,3,2,1,0:T(8,128)} %param.9) | copy-start | bytes 196612
  0.0 5.8 %collective-permute-start = (s32[1,1,8,2]{2,3,1,0:T(2,128)}, s32[1,1,8,2]{2,3,1,0:T(2,128)S(1)}, u32[]{:S(2)}, u32[]{:S(2)}) collective-permute-start(s32[1,1,8,2]{2,3,1,0:T(2,128)} %param.7), channel_id=1, source_target_pairs={{0,16},{4,20},{8,24},{12,28},{16,0},{20,4},{24,8},{28,12},{1,17},{... | collective-permute-start | bytes 200 | tf_op jit(solution)/shard_map/ppermute | solution.py:187
  4.0 0.7 %copy-start.3 = (s32[1,1,8,2]{2,3,1,0:T(2,128)S(1)}, s32[1,1,8,2]{2,3,1,0:T(2,128)}, u32[]{:S(2)}) copy-start(s32[1,1,8,2]{2,3,1,0:T(2,128)} %param.8) | copy-start | bytes 196
  4.0 0.7 %copy-start.4 = (s32[1,1,8,2]{2,3,1,0:T(2,128)S(1)}, s32[1,1,8,2]{2,3,1,0:T(2,128)}, u32[]{:S(2)}) copy-start(s32[1,1,8,2]{2,3,1,0:T(2,128)} %param.7) | copy-start | bytes 196
  4.0 0.7 %copy-start.2 = (s32[1,1,8,2]{2,3,1,0:T(2,128)S(1)}, s32[1,1,8,2]{2,3,1,0:T(2,128)}, u32[]{:S(2)}) copy-start(s32[1,1,8,2]{2,3,1,0:T(2,128)} %param.6) | copy-start | bytes 196
  5.0 7.1 %collective-permute-start.4 = (f32[4,2,8,128]{3,2,1,0:T(8,128)S(1)}, f32[4,2,8,128]{3,2,1,0:T(8,128)S(1)}, u32[]{:S(2)}, u32[]{:S(2)}) collective-permute-start(f32[4,2,8,128]{3,2,1,0:T(8,128)S(1)} %get-tuple-element.22), channel_id=1, source_target_pairs={{0,16},{4,20},{8,24},{12,28},{16,0},{20,4},{24,8},{28,12},{1,17},{... | collective-permute-start | bytes 98312 | tf_op jit(solution)/shard_map/ppermute | solution.py:187
  5.8 4.7 %collective-permute-start.1 = (s32[2,2,8]{2,1,0:T(2,128)S(1)}, s32[2,2,8]{2,1,0:T(2,128)S(1)}, u32[]{:S(2)}, u32[]{:S(2)}) collective-permute-start(s32[2,2,8]{2,1,0:T(2,128)S(1)} %pad_add_fusion.2.asked_ref), channel_id=1, source_target_pairs={{0,4},{4,0},{8,12},{12,8},{16,20},{20,16},{24,28},{28,24},{1,5},{5... | collective-permute-start | bytes 392 | tf_op jit(solution)/shard_map/ppermute | solution.py:187
  7.8 11.0 %collective-permute-start.3 = (f32[2,128,128]{2,1,0:T(8,128)S(1)}, f32[2,128,128]{2,1,0:T(8,128)S(1)}, u32[]{:S(2)}, u32[]{:S(2)}) collective-permute-start(f32[2,128,128]{2,1,0:T(8,128)S(1)} %shard_map.57.refs_3_), channel_id=1, source_target_pairs={{0,16},{4,20},{8,24},{12,28},{16,0},{20,4},{24,8},{28,12},{1,17},{... | collective-permute-start | bytes 393224 | tf_op jit(solution)/shard_map/ppermute | solution.py:187
  10.5 5.1 %collective-permute-start.2 = (s32[4,2,8]{2,1,0:T(2,128)S(1)}, s32[4,2,8]{2,1,0:T(2,128)S(1)}, u32[]{:S(2)}, u32[]{:S(2)}) collective-permute-start(s32[4,2,8]{2,1,0:T(2,128)S(1)} %pad_add_fusion.1.asked_ref), channel_id=1, source_target_pairs={{0,8},{4,12},{8,0},{12,4},{16,24},{20,28},{24,16},{28,20},{1,9},{5... | collective-permute-start | bytes 776 | tf_op jit(solution)/shard_map/ppermute | solution.py:187
  12.3 15.8 %collective-permute-start.6 = (f32[2,144,128]{2,1,0:T(8,128)S(1)}, f32[2,144,128]{2,1,0:T(8,128)S(1)}, u32[]{:S(2)}, u32[]{:S(2)}) collective-permute-start(f32[2,144,128]{2,1,0:T(8,128)S(1)} %get-tuple-element.24.refs_6_), channel_id=1, source_target_pairs={{0,4},{4,0},{8,12},{12,8},{16,20},{20,16},{24,28},{28,24},{1,5},{5... | collective-permute-start | bytes 442376 | tf_op jit(solution)/shard_map/ppermute | solution.py:187
  13.0 10.3 %collective-permute-start.5 = (f32[2,128,128]{2,1,0:T(8,128)S(1)}, f32[2,128,128]{2,1,0:T(8,128)S(1)}, u32[]{:S(2)}, u32[]{:S(2)}) collective-permute-start(f32[2,128,128]{2,1,0:T(8,128)S(1)} %get-tuple-element.23.refs_3_), channel_id=1, source_target_pairs={{0,20},{4,16},{8,28},{12,24},{16,4},{20,0},{24,12},{28,8},{1,21},{... | collective-permute-start | bytes 393224 | tf_op jit(solution)/shard_map/ppermute | solution.py:187
  15.8 13.6 %collective-permute-start.8 = (f32[2,144,128]{2,1,0:T(8,128)S(1)}, f32[2,144,128]{2,1,0:T(8,128)S(1)}, u32[]{:S(2)}, u32[]{:S(2)}) collective-permute-start(f32[2,144,128]{2,1,0:T(8,128)S(1)} %get-tuple-element.26.refs_6_), channel_id=1, source_target_pairs={{0,12},{4,8},{8,4},{12,0},{16,28},{20,24},{24,20},{28,16},{1,13},{... | collective-permute-start | bytes 442376 | tf_op jit(solution)/shard_map/ppermute | solution.py:187
  17.2 14.9 %collective-permute-start.10 = (f32[2,144,128]{2,1,0:T(8,128)S(1)}, f32[2,144,128]{2,1,0:T(8,128)S(1)}, u32[]{:S(2)}, u32[]{:S(2)}) collective-permute-start(f32[2,144,128]{2,1,0:T(8,128)S(1)} %get-tuple-element.28.refs_3_), channel_id=1, source_target_pairs={{0,8},{4,12},{8,0},{12,4},{16,24},{20,28},{24,16},{28,20},{1,9},{5... | collective-permute-start | bytes 442376 | tf_op jit(solution)/shard_map/ppermute | solution.py:187
  18.8 10.6 %collective-permute-start.7 = (f32[2,128,128]{2,1,0:T(8,128)S(1)}, f32[2,128,128]{2,1,0:T(8,128)S(1)}, u32[]{:S(2)}, u32[]{:S(2)}) collective-permute-start(f32[2,128,128]{2,1,0:T(8,128)S(1)} %get-tuple-element.25.refs_3_), channel_id=1, source_target_pairs={{0,28},{4,24},{8,20},{12,16},{16,12},{20,8},{24,4},{28,0},{1,29},{... | collective-permute-start | bytes 393224 | tf_op jit(solution)/shard_map/ppermute | solution.py:187
  23.3 7.1 %collective-permute-start.9 = (f32[2,128,128]{2,1,0:T(8,128)S(1)}, f32[2,128,128]{2,1,0:T(8,128)S(1)}, u32[]{:S(2)}, u32[]{:S(2)}) collective-permute-start(f32[2,128,128]{2,1,0:T(8,128)S(1)} %get-tuple-element.27.refs_0_), channel_id=1, source_target_pairs={{0,24},{4,28},{8,16},{12,20},{16,8},{20,12},{24,0},{28,4},{1,25},{... | collective-permute-start | bytes 393224 | tf_op jit(solution)/shard_map/ppermute | solution.py:187
  33.3 1.6 %collective-permute-start.12 = (f32[4,128,128]{2,1,0:T(8,128)S(1)}, f32[4,128,128]{2,1,0:T(8,128)S(1)}, u32[]{:S(2)}, u32[]{:S(2)}) collective-permute-start(f32[4,128,128]{2,1,0:T(8,128)S(1)} %get-tuple-element.32), channel_id=1, source_target_pairs={{0,1},{1,0},{2,3},{3,2},{4,5},{5,4},{6,7},{7,6},{8,9},{9,8},{10,11... | collective-permute-start | bytes 786440 | tf_op jit(solution)/shard_map/ppermute | solution.py:187
  33.4 3.1 %collective-permute-start.11 = (f32[4,128,128]{2,1,0:T(8,128)S(1)}, f32[4,128,128]{2,1,0:T(8,128)S(1)}, u32[]{:S(2)}, u32[]{:S(2)}) collective-permute-start(f32[4,128,128]{2,1,0:T(8,128)S(1)} %get-tuple-element.30), channel_id=1, source_target_pairs={{0,1},{1,0},{2,3},{3,2},{4,5},{5,4},{6,7},{7,6},{8,9},{9,8},{10,11... | collective-permute-start | bytes 786440 | tf_op jit(solution)/shard_map/ppermute | solution.py:187
  34.9 8.4 %collective-permute-start.13 = (f32[4,128,128]{2,1,0:T(8,128)S(1)}, f32[4,128,128]{2,1,0:T(8,128)S(1)}, u32[]{:S(2)}, u32[]{:S(2)}) collective-permute-start(f32[4,128,128]{2,1,0:T(8,128)S(1)} %add.10), channel_id=1, source_target_pairs={{0,2},{1,3},{2,0},{3,1},{4,6},{5,7},{6,4},{7,5},{8,10},{9,11},{10,... | collective-permute-start | bytes 786440 | tf_op jit(solution)/shard_map/ppermute | solution.py:187
